TPU v7x, 32 devices: a whole 2x2x4 slice. The times are simulated.
32 devices in a mesh: rep: 4 (over y, x), fsdp: 8 (over z, core).
Axes of the slice: x: 2, y: 2, z: 4, core: 2. Of those that a mesh axis runs over, the one named last changes fastest.
Arguments:
- grad_blocks: bfloat16 [4, 8, 512, 512], P('rep', None, 'fsdp'), may hold values from -6 to 6
- graft_accum: float32 [8, 512, 512], P(None, 'fsdp'), may hold values from 0.1 to 1000000
- left_stats: float32 [16, 512, 512], P('fsdp'), may hold values from -300000 to 300000, as said below
- right_stats: float32 [16, 512, 512], P('fsdp'), may hold values from -300000 to 300000, as said below
- block_slot: int32 [8], replicated, may hold values from 0 to 15, as said below
- vocab_grads: bfloat16 [4, 2, 64, 8192], P('rep', None, 'fsdp'), may hold values from -6 to 6
- vocab_accum: float32 [2, 64, 8192], P(None, 'fsdp'), may hold values from 0.01 to 10
Outputs:
- direction: bfloat16 [8, 512, 512], P(None, 'fsdp')
- graft_accum_new: float32 [8, 512, 512], P(None, 'fsdp')
- left_new: float32 [16, 512, 512], P('fsdp')
- right_new: float32 [16, 512, 512], P('fsdp')
- vocab_accum_new: float32 [2, 64, 8192], P(None, 'fsdp')
- vocab_step: bfloat16 [2, 64, 8192], P(None, 'fsdp')
Inputs may be any that keep to these rules, and one draw needn't show every extreme that they name: Block b's statistics sit in slot block_slot[b]; slot s belongs to fsdp index s // 2; no two blocks name the same slot; every fsdp index owns at most 2 blocks and some index owns exactly 2. `left_stats`: every slot holds a symmetric positive definite matrix. `right_stats`: every slot holds a symmetric positive definite matrix.
All inputs are finite; a program needn't handle non-finite values.
Results may differ from a plain program's by a relative error of at most 0.017.
Values may be sent and summed in bfloat16 or wider, within the bound.
No kernel may reach another device: no remote copies, remote signals or barrier semaphores. Data moves between devices by JAX's collectives and lax.ppermute only.
A program may use at most 64 MiB of HBM per device.

v0:
```python
import jax
import jax.numpy as jnp
from jax import lax
from jax.experimental import pallas as pl
from jax.experimental.pallas import tpu as pltpu
from jax.sharding import PartitionSpec as P

ITERS = 6
TAIL = 16
F32 = jnp.float32
BF16 = jnp.bfloat16
VMEM = pl.BlockSpec(memory_space=pltpu.VMEM)
SMEM = pl.BlockSpec(memory_space=pltpu.SMEM)
ANY = pl.BlockSpec(memory_space=pl.ANY)
HBM = pl.BlockSpec(memory_space=pltpu.HBM)
MIB = 1 << 20
LONG = 4 * 10**9


def shape(dims, dtype):
    return jax.ShapeDtypeStruct(dims, dtype)


def call(body, outs, in_specs, out_specs=None, scratch=(), flops=1, vmem=8):
    return pl.pallas_call(
        body,
        out_shape=outs,
        in_specs=in_specs,
        out_specs=jax.tree.map(lambda _: VMEM, outs) if out_specs is None else out_specs,
        scratch_shapes=list(scratch),
        compiler_params=pltpu.CompilerParams(vmem_limit_bytes=vmem * MIB),
        cost_estimate=pl.CostEstimate(flops=flops, bytes_accessed=1, transcendentals=0),
    )


def dot(left, right):
    return jnp.dot(left, right, preferred_element_type=F32)


def gram(value, axis):
    return lax.dot_general(
        value, value, (((axis,), (axis,)), ((), ())), preferred_element_type=F32
    )


def three_terms(value):
    high = value.astype(BF16).astype(F32)
    middle = (value - high).astype(BF16).astype(F32)
    return high, middle, value - high - middle


def exchange(values, axis, mask, size):
    return lax.ppermute(values, axis, [(i, i ^ mask) for i in range(size)])


def fence(arrays, *done, flops=1):
    def body(*refs):
        pass

    return pl.pallas_call(
        body,
        out_shape=[shape(array.shape, array.dtype) for array in arrays],
        in_specs=[ANY] * (len(arrays) + len(done)),
        out_specs=[ANY] * len(arrays),
        input_output_aliases={i: i for i in range(len(arrays))},
        compiler_params=pltpu.CompilerParams(vmem_limit_bytes=MIB),
        cost_estimate=pl.CostEstimate(flops=flops, bytes_accessed=1, transcendentals=0),
    )(*arrays, *done)


def late(arrays, *done):
    return fence(fence(arrays, flops=LONG), *done)


def in_hbm(array):
    return pltpu.with_memory_space_constraint(array, pltpu.HBM)


def place():
    index = lax.axis_index("fsdp")
    return lax.axis_index("rep"), index // 2, index % 2


def on_device(
    grad_blocks, graft_accum, left_stats, right_stats, block_slot, vocab_grads, vocab_accum
):
    reps, indices = lax.axis_size("rep"), lax.axis_size("fsdp")
    blocks, rows, order = grad_blocks.shape[1:]
    most = left_stats.shape[0]
    planes, per, cols = indices // 2, 2 * most, order // reps
    assert per <= reps and blocks % reps == 0
    share, slots = blocks // reps, per * planes
    rep_partners, plane_partners = range(1, reps), range(1, planes)
    entries = float(order * order)
    square = (order, order)
    scratch_type = BF16 if rows % 16 == 0 else F32
    vocab_own = vocab_grads[0]
    vocab_cols = vocab_own.shape[2] // reps
    grad_rows, pair_rows = blocks * rows, vocab_own.shape[0] * vocab_own.shape[1]
    chunks = vocab_cols // cols
    vocab_rows = chunks * pair_rows
    share_rows = (grad_rows + vocab_rows) // 2
    assert share_rows % rows == 0 and share_rows % pair_rows == 0
    assert reps == 4 and most == 2
    ways = ((1, 2), (2, 1))
    right_other = exchange(right_stats, "fsdp", 1, indices)

    def ranked(slot_ref, who, visit):
        for s in range(slots):
            who[s] = -1
        for b in range(blocks):
            who[slot_ref[0, b]] = b
        count = jnp.int32(0)
        for s in range(slots):
            block = who[s]
            visit(s, block, count)
            count = count + jnp.where(block >= 0, 1, 0)

    def local_slots(slot_ref, who, local_of):
        plane_here = place()[1]
        for j in range(reps):
            local_of[j] = 0

        def visit(s, block, count):
            @pl.when((block >= 0) & (plane_here == s // per))
            def _():
                local_of[count % reps] = s % per

        ranked(slot_ref, who, visit)

    def cut_body(slot_ref, grad_ref, vocab_ref, *refs):
        out_refs, table_ref = refs[:reps], refs[reps]
        line = lax.broadcasted_iota(jnp.int32, table_ref.shape, 1)
        table = jnp.zeros(table_ref.shape, jnp.int32)
        for b in range(blocks):
            table = jnp.where(line == b, slot_ref[b], table)
        table_ref[...] = table
        for k in range(reps):
            part = place()[0] ^ k
            at = pl.ds(pl.multiple_of(part * cols, cols), cols)
            for b in range(blocks):
                out_refs[k][b * rows : (b + 1) * rows, :] = grad_ref[b, :, at]
            at = pl.ds(pl.multiple_of(part * vocab_cols, vocab_cols), vocab_cols)
            value = vocab_ref[:, :, at].astype(F32).reshape(pair_rows, vocab_cols).astype(BF16)
            for i in range(chunks):
                first = grad_rows + i * pair_rows
                out_refs[k][first : first + pair_rows, :] = value[:, i * cols : (i + 1) * cols]

    cut = call(
        cut_body,
        [shape((grad_rows + vocab_rows, cols), BF16)] * reps
        + [shape((1, 128), jnp.int32)],
        [SMEM, VMEM, VMEM],
        vmem=8,
    )(in_hbm(block_slot), in_hbm(grad_blocks[0]), in_hbm(vocab_own))
    pieces, table = cut[:reps], cut[reps]
    accum_share = lax.dynamic_slice_in_dim(
        graft_accum, lax.axis_index("rep") * cols, cols, 2
    )

    terms = [pieces[0]] + [exchange(pieces[k], "rep", k, reps) for k in rep_partners]
    payload_rows = per * rows + TAIL

    book = [pltpu.SMEM((slots,), jnp.int32), pltpu.SMEM((reps,), jnp.int32)]

    def sum_body(slot_ref, *refs):
        term_refs, accum_ref, share_refs = refs[:reps], refs[reps], refs[reps + 1 : reps + 3]
        out_refs = refs[reps + 3 : reps + 3 + planes]
        held, parts, tail = refs[reps + 3 + planes :]
        plane_here = place()[1]

        def total_of(first, count):
            total = term_refs[0][first : first + count, :].astype(F32)
            for term in term_refs[1:]:
                total = total + term[first : first + count, :].astype(F32)
            return total.astype(BF16)

        def keep(first, value):
            half, at = first // share_rows, first % share_rows
            share_refs[half][at : at + value.shape[0], :] = value

        for i in range(chunks):
            first = grad_rows + i * pair_rows
            keep(first, total_of(first, pair_rows))
        held[...] = jnp.zeros_like(held)
        parts[...] = jnp.zeros_like(parts)
        for b in range(blocks):
            summed = total_of(b * rows, rows)
            keep(b * rows, summed)
            value = summed.astype(F32)
            grafted = value / (jnp.sqrt(accum_ref[b] + value * value) + 1e-10)
            slot = slot_ref[0, b]
            away = (slot // per) ^ plane_here
            local = slot % per
            held[away, local] = summed
            parts[away, pl.ds(local, 1), :] = jnp.sum(grafted * grafted, axis=0, keepdims=True)
        tail[...] = jnp.zeros_like(tail)
        for k in range(planes):
            for s in range(per):
                out_refs[k][s * rows : (s + 1) * rows, :] = held[k, s]
            for t, term in enumerate(three_terms(parts[k, :per, :])):
                tail[t * per : (t + 1) * per, :] = term
            out_refs[k][per * rows :, :] = tail[...].astype(BF16)

    summed = call(
        sum_body,
        [shape((share_rows, cols), BF16)] * 2
        + [shape((payload_rows, cols), BF16)] * planes,
        [SMEM] + [VMEM] * (reps + 1),
        scratch=[
            pltpu.VMEM((planes, per, rows, cols), BF16),
            pltpu.VMEM((planes, 8, cols), F32),
            pltpu.VMEM((TAIL, cols), F32),
        ],
    )(table, *terms, accum_share)
    shares, payloads = summed[:2], summed[2:]

    arrived = [payloads[0]] + [
        exchange(payloads[k], "fsdp", 2 * k, indices) for k in plane_partners
    ]

    share_firsts = [exchange(shares[m], "rep", ways[m][0], reps) for m in range(2)]
    part_rows = planes * rows + TAIL

    def route_body(slot_ref, *refs):
        in_refs = refs[:planes]
        out_refs = refs[planes : planes + reps]
        half_refs = refs[planes + reps : planes + reps + most]
        parts, tail, who, local_of = refs[planes + reps + most :]
        rep_here = place()[0]
        local_slots(slot_ref, who, local_of)
        total = jnp.zeros((per, cols), F32)
        for ref in in_refs:
            bits = ref[per * rows :, :].astype(F32)
            for t in range(3):
                total = total + bits[t * per : (t + 1) * per]
        parts[:per, :] = total
        tail[...] = jnp.zeros_like(tail)
        for j in range(reps):
            local = local_of[rep_here ^ j]
            for s in range(per):

                @pl.when(local == s)
                def _():
                    for k in range(planes):
                        out_refs[j][k * rows : (k + 1) * rows, :] = in_refs[k][
                            s * rows : (s + 1) * rows, :
                        ]

            for t, term in enumerate(three_terms(parts[pl.ds(local, 1), :])):
                tail[t : t + 1, :] = term
            out_refs[j][planes * rows :, :] = tail[...].astype(BF16)
        for k in range(planes):
            for m in range(most):
                for side in range(2):
                    s = side * most + m
                    at = (side * planes + k) * rows
                    half_refs[m][at : at + rows, :] = in_refs[k][s * rows : (s + 1) * rows, :]

    half = shape((2 * planes * rows, cols), BF16)
    routed = call(
        route_body,
        [shape((part_rows, cols), BF16)] * reps + [half] * most,
        [SMEM] + [VMEM] * planes,
        scratch=[pltpu.VMEM((8, cols), F32), pltpu.VMEM((TAIL, cols), F32)] + book,
    )(table, *arrived)
    routed = late(routed, *share_firsts, right_other)
    parts, halves = routed[:reps], routed[reps:]

    met = [parts[0]] + [exchange(parts[j], "rep", j, reps) for j in rep_partners]
    firsts = [exchange(halves[m], "rep", ways[m][0], reps) for m in range(2)]
    mine = late([jnp.stack(met)], *firsts)[0]
    other = exchange(mine, "fsdp", 1, indices)
    half_rows = 2 * planes * rows
    lasts = []
    for m in range(2):
        arrays = (halves[m], firsts[m], shares[m], share_firsts[m])
        joined = jnp.concatenate([array.reshape(-1, cols) for array in arrays])
        lasts.append(exchange(fence([joined], mine)[0], "rep", ways[m][1], reps))

    def assemble(grad, rep_here, plane_here, core_here, piece, k, j):
        row = pl.multiple_of((2 * (plane_here ^ k) + core_here) * rows, rows)
        col = pl.multiple_of((rep_here ^ j) * cols, cols)
        grad[pl.ds(row, rows), pl.ds(col, cols)] = piece.astype(scratch_type)

    def root_body(slot_ref, mine_ref, other_ref, left_ref, right_ref,
                  out_ref, graft_ref, grad, matrix, start, who, local_of, sem):
        rep_here, plane_here, core_here = place()
        local_slots(slot_ref, who, local_of)
        owner, at = local_of[rep_here] // most, local_of[rep_here] % most

        @pl.when(owner == core_here)
        def _():
            pltpu.make_async_copy(left_ref.at[at], matrix, sem).start()

        @pl.when(owner != core_here)
        def _():
            pltpu.make_async_copy(right_ref.at[at], matrix, sem).start()

        graft = jnp.zeros((1, cols), F32)
        for j in range(reps):
            for ref, side in ((mine_ref, core_here), (other_ref, 1 - core_here)):
                for k in range(planes):
                    assemble(grad, rep_here, plane_here, side,
                             ref[j, k * rows : (k + 1) * rows, :], k, j)
                bits = ref[j, planes * rows :, :].astype(F32)
                graft = graft + jnp.sum(bits[:8], axis=0, keepdims=True)
        line = lax.broadcasted_iota(jnp.int32, graft_ref.shape, 0)
        first = jnp.where(owner == core_here, 1.0, 0.0)
        graft_ref[...] = jnp.where(line == 0, jnp.broadcast_to(graft, graft_ref.shape), first)
        pltpu.make_async_copy(left_ref.at[at], matrix, sem).wait()

        @pl.when(owner == core_here)
        def _():
            value = grad[...].astype(BF16)
            matrix[...] += gram(value, 1)
            start[...] = value.astype(F32)

        @pl.when(owner != core_here)
        def _():
            matrix[...] += gram(grad[...].astype(BF16), 0)
            line = lax.broadcasted_iota(jnp.int32, square, 0)
            start[...] = (line == lax.broadcasted_iota(jnp.int32, square, 1)).astype(F32)

        scaled = matrix[...]
        scaled = scaled / jnp.sqrt(jnp.sum(scaled * scaled))
        result = start[...]
        for iteration in range(ITERS):
            low = scaled.astype(BF16)
            result = 1.25 * result - 0.25 * dot(low, result.astype(BF16))
            if iteration + 1 < ITERS:
                step = (dot(low, low) * 0.0625 - 0.625 * scaled).astype(BF16)
                twice = 1.5625 * scaled + dot(low, step)
                scaled = 1.5625 * twice + dot(twice.astype(BF16), step)
        out_ref[...] = result.astype(BF16)

    root, graft_sum = call(
        root_body,
        [shape(square, BF16), shape((8, cols), F32)],
        [SMEM, VMEM, VMEM, ANY, ANY],
        scratch=[
            pltpu.VMEM(square, scratch_type),
            pltpu.VMEM(square, F32),
            pltpu.VMEM(square, F32),
        ]
        + book
        + [pltpu.SemaphoreType.DMA],
        flops=1,
        vmem=20,
    )(table, mine, other, left_stats, right_other)
    root = fence([root], *lasts)[0]
    root_other = exchange(root, "fsdp", 1, indices)

    def finish_body(mine_ref, other_ref, graft_ref, *refs):
        out_refs, result = refs[:planes], refs[planes]
        _, plane_here, core_here = place()
        left_here = jnp.sum(graft_ref[1:2, :]) > 0.5

        @pl.when(left_here)
        def _():
            result[...] = dot(mine_ref[...], other_ref[...])

        @pl.when(jnp.logical_not(left_here))
        def _():
            result[...] = dot(other_ref[...], mine_ref[...])

        value = result[...]
        mean = jnp.sum(value * value) / entries
        graft_mean = jnp.sum(graft_ref[0:1, :]) / entries
        scale = jnp.sqrt(graft_mean) / jnp.sqrt(mean + 1e-06)
        for k in range(planes):
            row = pl.multiple_of((2 * (plane_here ^ k) + core_here) * rows, rows)
            out_refs[k][...] = (result[pl.ds(row, rows), :] * scale).astype(BF16)

    slabs = call(
        finish_body,
        [shape((rows, order), BF16)] * planes,
        [VMEM, VMEM, VMEM],
        scratch=[pltpu.VMEM(square, F32)],
        flops=2 * order**3,
    )(root, root_other, graft_sum)

    def side_body(*refs):
        keep_ref, give_ref = refs[6:]
        core_here = place()[2]
        side_rows = planes * rows
        for m in range(2):
            own_ref, first_ref, last_ref = refs[m], refs[2 + m], refs[4 + m]
            near, far = ways[m]
            places = (
                (0, own_ref, 0),
                (near, first_ref, 0),
                (far, last_ref, 0),
                (near ^ far, last_ref, half_rows),
            )
            for j, ref, at in places:
                for target, side in ((keep_ref, core_here), (give_ref, 1 - core_here)):
                    first = pl.multiple_of(at + side * side_rows, side_rows)
                    target[j, m] = ref[pl.ds(first, side_rows), :]

    side = shape((reps, most, planes * rows, cols), BF16)
    keep, give = call(side_body, [side, side], [VMEM] * 6)(*halves, *firsts, *lasts)
    other_side = exchange(give, "fsdp", 1, indices)
    slabs = fence(slabs, other_side)

    returned = [slabs[0]] + [
        exchange(slabs[k], "fsdp", 2 * k, indices) for k in plane_partners
    ]

    def stats_body(left_ref, right_ref, after_ref, keep_ref, other_ref,
                   left_out, right_out, token_ref, grad):
        m = pl.program_id(0)
        token_ref[...] = jnp.zeros_like(token_ref)
        rep_here, plane_here, core_here = place()
        for j in range(reps):
            for ref, side in ((keep_ref, core_here), (other_ref, 1 - core_here)):
                for k in range(planes):
                    assemble(grad, rep_here, plane_here, side,
                             ref[j, m, k * rows : (k + 1) * rows, :], k, j)
        value = grad[...].astype(BF16)
        left_out[0] = left_ref[0] + gram(value, 1)
        right_out[0] = right_ref[0] + gram(value, 0)

    token = shape((8, 128), F32)
    slot_block = pl.BlockSpec((1, order, order), lambda m: (m, 0, 0))
    left_new, right_new, stats_token = pl.pallas_call(
        stats_body,
        grid=(most,),
        out_shape=[shape(left_stats.shape, F32), shape(right_stats.shape, F32), token],
        in_specs=[slot_block, slot_block, ANY, VMEM, VMEM],
        out_specs=[slot_block, slot_block, pl.BlockSpec((8, 128), lambda m: (0, 0))],
        scratch_shapes=[pltpu.VMEM(square, scratch_type)],
        compiler_params=pltpu.CompilerParams(vmem_limit_bytes=20 * MIB),
        cost_estimate=pl.CostEstimate(
            flops=1, bytes_accessed=1, transcendentals=0
        ),
    )(left_stats, right_stats, slabs[0], keep, other_side)

    def pick_body(slot_ref, *refs):
        out_ref, who = refs[-2:]
        rep_here, plane_here, _ = place()

        def visit(s, block, count):
            @pl.when((block >= 0) & (count % reps == rep_here))
            def _():
                for k in range(planes):

                    @pl.when(plane_here == (s // per) ^ k)
                    def _():
                        out_ref[count // reps] = refs[k][...]

        ranked(slot_ref, who, visit)

    picked = call(
        pick_body,
        shape((share, rows, order), BF16),
        [SMEM] + [VMEM] * planes + [ANY],
        scratch=book[:1],
    )(table, *returned, stats_token)
    gathered = [picked] + [exchange(picked, "rep", j, reps) for j in rep_partners]

    def accum_body(accum_ref, vocab_ref, after_ref, *refs):

        def piece(j, first, count):
            m, at = first // share_rows, first % share_rows
            near, far = ways[m]
            ref, base = {
                0: (refs[m], 0),
                near: (refs[2 + m], 0),
                far: (refs[4 + m], 2 * half_rows),
                near ^ far: (refs[4 + m], 2 * half_rows + share_rows),
            }[j]
            return ref[base + at : base + at + count, :].astype(F32)

        accum_out, vocab_out, step_out, token_ref = refs[6:]
        token_ref[...] = jnp.zeros_like(token_ref)
        rep_here = place()[0]
        for j in range(reps):
            at = pl.ds(pl.multiple_of((rep_here ^ j) * cols, cols), cols)
            for b in range(blocks):
                value = piece(j, b * rows, rows)
                accum_out[b, :, at] = accum_ref[b, :, at] + value * value
            for i in range(chunks):
                value = piece(j, grad_rows + i * pair_rows, pair_rows)
                value = value.reshape(vocab_own.shape[:2] + (cols,))
                start = pl.multiple_of((rep_here ^ j) * vocab_cols + i * cols, cols)
                at_vocab = pl.ds(start, cols)
                accum = vocab_ref[:, :, at_vocab] + value * value
                vocab_out[:, :, at_vocab] = accum
                step_out[:, :, at_vocab] = (value / (jnp.sqrt(accum) + 1e-10)).astype(BF16)

    graft_accum_new, vocab_accum_new, vocab_step, accum_token = call(
        accum_body,
        [
            shape(graft_accum.shape, F32),
            shape(vocab_accum.shape, F32),
            shape(vocab_accum.shape, BF16),
            token,
        ],
        [VMEM, VMEM, ANY] + [VMEM] * 6,
        vmem=12,
    )(graft_accum, vocab_accum, picked, *shares, *share_firsts, *lasts)

    def place_body(slot_ref, *refs):
        out_ref, who, block_of, sem = refs[reps + 1 :]
        rep_here = place()[0]

        def visit(s, block, count):
            @pl.when(block >= 0)
            def _():
                block_of[count] = block

        ranked(slot_ref, who, visit)
        copies = []
        for j in range(reps):
            for m in range(share):
                block = block_of[m * reps + (rep_here ^ j)]
                copies.append(
                    pltpu.make_async_copy(
                        refs[j].at[m], out_ref.at[block], sem.at[j * share + m]
                    )
                )
                copies[-1].start()
        for copy in copies:
            copy.wait()

    direction = call(
        place_body,
        shape((blocks, rows, order), BF16),
        [SMEM] + [VMEM] * reps + [ANY],
        out_specs=HBM,
        scratch=[
            book[0],
            pltpu.SMEM((blocks,), jnp.int32),
            pltpu.SemaphoreType.DMA((blocks,)),
        ],
    )(table, *gathered, accum_token)
    return (direction, graft_accum_new, left_new, right_new, vocab_accum_new, vocab_step)


def solution(mesh):
    in_specs = (
        P("rep", None, "fsdp", None),
        P(None, "fsdp", None),
        P("fsdp", None, None),
        P("fsdp", None, None),
        P(),
        P("rep", None, "fsdp", None),
        P(None, "fsdp", None),
    )
    out_specs = (
        P(None, "fsdp", None),
        P(None, "fsdp", None),
        P("fsdp", None, None),
        P("fsdp", None, None),
        P(None, "fsdp", None),
        P(None, "fsdp", None),
    )
    return jax.shard_map(
        on_device, mesh=mesh, in_specs=in_specs, out_specs=out_specs, check_vma=False
    )
```

profile of v0, /device:TPU:0, one launch (start us, length us, event | category | flops | bytes accessed | tf_op | source)
XLA Modules:
  0.0 73.4 jit_solution(15506228334729162152)
XLA Ops:
  1.1 1.3 %shard_map.118 = (bf16[768,128]{1,0:T(8,128)(2,1)S(1)}, bf16[768,128]{1,0:T(8,128)(2,1)S(1)}, bf16[768,128]{1,0:T(8,128)(2,1)S(1)}, bf16[768,128]{1,0:T(8,128)(2,1)S(1)}, s32[1,128]{1,0:T(1,128)S(1)}) custom-call(s32[8]{0:T(128)} %slot_ref.1, bf16[8,64,512]{2,1,0:T(8,128)(2,1)} %bitcast.7, bf16[2,8,8192]{2,1,0:T(8,128)(2,1)} %bitcast.8), custom_call_target="tpu_custom_call" | custom-call | flops 1 | bytes 1 | tf_op jit(solution)/shard_map/pallas_call | solution.py:149
  2.4 2.6 %collective-permute-start = (bf16[768,128]{1,0:T(8,128)(2,1)S(1)}, bf16[768,128]{1,0:T(8,128)(2,1)S(1)}, u32[]{:S(2)}, u32[]{:S(2)}) collective-permute-start(bf16[768,128]{1,0:T(8,128)(2,1)S(1)} %get-tuple-element.56), channel_id=1, source_target_pairs={{0,8},{8,0},{16,24},{24,16},{1,9},{9,1},{17,25},{25,17},{2,10},{10... | collective-permute-start | bytes 589832 | tf_op jit(solution)/shard_map/ppermute | solution.py:53
  5.0 1.5 %collective-permute-start.1 = (bf16[768,128]{1,0:T(8,128)(2,1)S(1)}, bf16[768,128]{1,0:T(8,128)(2,1)S(1)}, u32[]{:S(2)}, u32[]{:S(2)}) collective-permute-start(bf16[768,128]{1,0:T(8,128)(2,1)S(1)} %get-tuple-element.57), channel_id=1, source_target_pairs={{0,16},{8,24},{16,0},{24,8},{1,17},{9,25},{17,1},{25,9},{2,18},{10... | collective-permute-start | bytes 589832 | tf_op jit(solution)/shard_map/ppermute | solution.py:53
  7.5 3.2 %collective-permute-done.refs_1_ = bf16[768,128]{1,0:T(8,128)(2,1)S(1)} collective-permute-done((bf16[768,128]{1,0:T(8,128)(2,1)S(1)}, bf16[768,128]{1,0:T(8,128)(2,1)S(1)}, u32[]{:S(2)}, u32[]{:S(2)}) %collective-permute-start) | collective-permute-done | bytes 196640 | tf_op jit(solution)/shard_map/ppermute | solution.py:53
  10.7 5.5 %collective-permute-done.1.refs_2_ = bf16[768,128]{1,0:T(8,128)(2,1)S(1)} collective-permute-done((bf16[768,128]{1,0:T(8,128)(2,1)S(1)}, bf16[768,128]{1,0:T(8,128)(2,1)S(1)}, u32[]{:S(2)}, u32[]{:S(2)}) %collective-permute-start.1) | collective-permute-done | bytes 196640 | tf_op jit(solution)/shard_map/ppermute | solution.py:53
  17.1 1.6 %collective-permute-start.3 = (bf16[272,128]{1,0:T(8,128)(2,1)S(1)}, bf16[272,128]{1,0:T(8,128)(2,1)S(1)}, u32[]{:S(2)}, u32[]{:S(2)}) collective-permute-start(bf16[272,128]{1,0:T(8,128)(2,1)S(1)} %get-tuple-element.60), channel_id=1, source_target_pairs={{0,2},{1,3},{2,0},{3,1},{4,6},{5,7},{6,4},{7,5},{8,10},{9,11},{10,... | collective-permute-start | bytes 208904 | tf_op jit(solution)/shard_map/ppermute | solution.py:53
  18.7 2.6 %collective-permute-start.4 = (bf16[272,128]{1,0:T(8,128)(2,1)S(1)}, bf16[272,128]{1,0:T(8,128)(2,1)S(1)}, u32[]{:S(2)}, u32[]{:S(2)}) collective-permute-start(bf16[272,128]{1,0:T(8,128)(2,1)S(1)} %get-tuple-element.61), channel_id=1, source_target_pairs={{0,4},{1,5},{2,6},{3,7},{4,0},{5,1},{6,2},{7,3},{8,12},{9,13},{10,... | collective-permute-start | bytes 208904 | tf_op jit(solution)/shard_map/ppermute | solution.py:53
  21.5 1.2 %collective-permute-start.6 = (bf16[384,128]{1,0:T(8,128)(2,1)S(1)}, bf16[384,128]{1,0:T(8,128)(2,1)S(1)}, u32[]{:S(2)}, u32[]{:S(2)}) collective-permute-start(bf16[384,128]{1,0:T(8,128)(2,1)S(1)} %get-tuple-element.75.refs_0_), channel_id=1, source_target_pairs={{0,8},{8,0},{16,24},{24,16},{1,9},{9,1},{17,25},{25,17},{2,10},{10... | collective-permute-start | bytes 294920 | tf_op jit(solution)/shard_map/ppermute | solution.py:53
  23.6 2.3 %collective-permute-done.4.refs_2_ = bf16[272,128]{1,0:T(8,128)(2,1)S(1)} collective-permute-done((bf16[272,128]{1,0:T(8,128)(2,1)S(1)}, bf16[272,128]{1,0:T(8,128)(2,1)S(1)}, u32[]{:S(2)}, u32[]{:S(2)}) %collective-permute-start.4) | collective-permute-done | bytes 69664 | tf_op jit(solution)/shard_map/ppermute | solution.py:53
  25.9 1.5 %collective-permute-done.5.refs_3_ = bf16[272,128]{1,0:T(8,128)(2,1)S(1)} collective-permute-done((bf16[272,128]{1,0:T(8,128)(2,1)S(1)}, bf16[272,128]{1,0:T(8,128)(2,1)S(1)}, u32[]{:S(2)}, u32[]{:S(2)}) %collective-permute-start.5) | collective-permute-done | bytes 69664 | tf_op jit(solution)/shard_map/ppermute | solution.py:53
  28.2 1.4 %collective-permute-start.9 = (bf16[272,128]{1,0:T(8,128)(2,1)S(1)}, bf16[272,128]{1,0:T(8,128)(2,1)S(1)}, u32[]{:S(2)}, u32[]{:S(2)}) collective-permute-start(bf16[272,128]{1,0:T(8,128)(2,1)S(1)} %get-tuple-element.78), channel_id=1, source_target_pairs={{0,8},{8,0},{16,24},{24,16},{1,9},{9,1},{17,25},{25,17},{2,10},{10... | collective-permute-start | bytes 208904 | tf_op jit(solution)/shard_map/ppermute | solution.py:53
  30.3 1.4 %collective-permute-start.11 = (bf16[272,128]{1,0:T(8,128)(2,1)S(1)}, bf16[272,128]{1,0:T(8,128)(2,1)S(1)}, u32[]{:S(2)}, u32[]{:S(2)}) collective-permute-start(bf16[272,128]{1,0:T(8,128)(2,1)S(1)} %get-tuple-element.80), channel_id=1, source_target_pairs={{0,24},{8,16},{16,8},{24,0},{1,25},{9,17},{17,9},{25,1},{2,26},{10... | collective-permute-start | bytes 208904 | tf_op jit(solution)/shard_map/ppermute | solution.py:53
  31.8 1.5 %collective-permute-start.13 = (bf16[512,128]{1,0:T(8,128)(2,1)S(1)}, bf16[512,128]{1,0:T(8,128)(2,1)S(1)}, u32[]{:S(2)}, u32[]{:S(2)}) collective-permute-start(bf16[512,128]{1,0:T(8,128)(2,1)S(1)} %get-tuple-element.82.refs_1_), channel_id=1, source_target_pairs={{0,16},{8,24},{16,0},{24,8},{1,17},{9,25},{17,1},{25,9},{2,18},{10... | collective-permute-start | bytes 393224 | tf_op jit(solution)/shard_map/ppermute | solution.py:53
  33.9 1.6 %collective-permute-done.11 = bf16[272,128]{1,0:T(8,128)(2,1)S(1)} collective-permute-done((bf16[272,128]{1,0:T(8,128)(2,1)S(1)}, bf16[272,128]{1,0:T(8,128)(2,1)S(1)}, u32[]{:S(2)}, u32[]{:S(2)}) %collective-permute-start.11) | collective-permute-done | bytes 69664 | tf_op jit(solution)/shard_map/ppermute | solution.py:53
  35.6 1.3 %collective-permute-done.13.refs_2_.refs_3_ = bf16[512,128]{1,0:T(8,128)(2,1)S(1)} collective-permute-done((bf16[512,128]{1,0:T(8,128)(2,1)S(1)}, bf16[512,128]{1,0:T(8,128)(2,1)S(1)}, u32[]{:S(2)}, u32[]{:S(2)}) %collective-permute-start.13) | collective-permute-done | bytes 131104 | tf_op jit(solution)/shard_map/ppermute | solution.py:53
  37.0 2.7 %collective-permute-done.12.refs_1_.refs_2_ = bf16[512,128]{1,0:T(8,128)(2,1)S(1)} collective-permute-done((bf16[512,128]{1,0:T(8,128)(2,1)S(1)}, bf16[512,128]{1,0:T(8,128)(2,1)S(1)}, u32[]{:S(2)}, u32[]{:S(2)}) %collective-permute-start.12) | collective-permute-done | bytes 131104 | tf_op jit(solution)/shard_map/ppermute | solution.py:53
  39.8 1.7 %collective-permute-start.15 = (bf16[1792,128]{1,0:T(8,128)(2,1)S(1)}, bf16[1792,128]{1,0:T(8,128)(2,1)S(1)}, u32[]{:S(2)}, u32[]{:S(2)}) collective-permute-start(bf16[1792,128]{1,0:T(8,128)(2,1)S(1)} %shard_map.126), channel_id=1, source_target_pairs={{0,16},{8,24},{16,0},{24,8},{1,17},{9,25},{17,1},{25,9},{2,18},{10... | collective-permute-start | bytes 1376264 | tf_op jit(solution)/shard_map/ppermute | solution.py:53
  41.4 1.6 %collective-permute-done.14.other_ref = bf16[4,272,128]{2,1,0:T(8,128)(2,1)S(1)} collective-permute-done((bf16[4,272,128]{2,1,0:T(8,128)(2,1)S(1)}, bf16[4,272,128]{2,1,0:T(8,128)(2,1)S(1)}, u32[]{:S(2)}, u32[]{:S(2)}) %collective-permute-start.14) | collective-permute-done | bytes 278560 | tf_op jit(solution)/shard_map/ppermute | solution.py:53
  43.0 8.0 %shard_map.125 = (bf16[512,512]{1,0:T(8,128)(2,1)S(1)}, f32[8,128]{1,0:T(8,128)S(1)}) custom-call(s32[1,128]{1,0:T(1,128)S(1)} %get-tuple-element.54.slot_ref, bf16[4,272,128]{2,1,0:T(8,128)(2,1)S(1)} %shard_map.124.mine_ref.refs_1_, bf16[4,272,128]{2,1,0:T(8,128)(2,1)S(1)} %collective-permute-done.14.other_ref, f32[2,512,512]{2,1,0:T(8,128)S(1)} %copy-done, ...), custom_call_target="tpu_custom_call" | custom-call | flops 1 | bytes 1 | tf_op jit(solution)/shard_map/pallas_call | solution.py:337
  51.8 1.3 %collective-permute-done.17.other_ref = bf16[512,512]{1,0:T(8,128)(2,1)S(1)} collective-permute-done((bf16[512,512]{1,0:T(8,128)(2,1)S(1)}, bf16[512,512]{1,0:T(8,128)(2,1)S(1)}, u32[]{:S(2)}, u32[]{:S(2)}) %collective-permute-start.17) | collective-permute-done | bytes 524320 | tf_op jit(solution)/shard_map/ppermute | solution.py:53
  53.1 1.1 %shard_map.129 = (bf16[64,512]{1,0:T(8,128)(2,1)S(1)}, bf16[64,512]{1,0:T(8,128)(2,1)S(1)}, bf16[64,512]{1,0:T(8,128)(2,1)S(1)}, bf16[64,512]{1,0:T(8,128)(2,1)S(1)}) custom-call(bf16[512,512]{1,0:T(8,128)(2,1)S(1)} %shard_map.128.mine_ref, bf16[512,512]{1,0:T(8,128)(2,1)S(1)} %collective-permute-done.17.other_ref, f32[8,128]{1,0:T(8,128)S(1)} %get-tuple-element.84.graft_ref), custom_call_target="tpu_custom_call" | custom-call | flops 268435456 | bytes 1 | tf_op jit(solution)/shard_map/pallas_call | solution.py:375
  54.2 2.5 %collective-permute-start.20 = (bf16[64,512]{1,0:T(8,128)(2,1)S(1)}, bf16[64,512]{1,0:T(8,128)(2,1)S(1)}, u32[]{:S(2)}, u32[]{:S(2)}) collective-permute-start(bf16[64,512]{1,0:T(8,128)(2,1)S(1)} %get-tuple-element.92), channel_id=1, source_target_pairs={{0,4},{1,5},{2,6},{3,7},{4,0},{5,1},{6,2},{7,3},{8,12},{9,13},{10,... | collective-permute-start | bytes 196616 | tf_op jit(solution)/shard_map/ppermute | solution.py:53
  56.8 1.9 %collective-permute-start.21 = (bf16[64,512]{1,0:T(8,128)(2,1)S(1)}, bf16[64,512]{1,0:T(8,128)(2,1)S(1)}, u32[]{:S(2)}, u32[]{:S(2)}) collective-permute-start(bf16[64,512]{1,0:T(8,128)(2,1)S(1)} %get-tuple-element.93), channel_id=1, source_target_pairs={{0,6},{1,7},{2,4},{3,5},{4,2},{5,3},{6,0},{7,1},{8,14},{9,15},{10,... | collective-permute-start | bytes 196616 | tf_op jit(solution)/shard_map/ppermute | solution.py:53
  58.6 2.8 %shard_map.132 = (f32[2,512,512]{2,1,0:T(8,128)}, f32[2,512,512]{2,1,0:T(8,128)}, f32[8,128]{1,0:T(8,128)S(1)}) custom-call(f32[2,512,512]{2,1,0:T(8,128)S(1)} %copy-done, f32[2,512,512]{2,1,0:T(8,128)S(1)} %copy-done.1, bf16[64,512]{1,0:T(8,128)(2,1)S(1)} %get-tuple-element.90.after_ref.refs_0_, bf16[4,2,256,128]{3,2,1,0:T(8,128)(2,1)S(1)} %get-tuple-element.94.keep_ref, ...), custom_call_target="tpu_custom_call" | custom-call | flops 1 | bytes 1 | tf_op jit(solution)/shard_map/pallas_call | solution.py:426
  61.4 1.5 %collective-permute-done.20.refs_2_ = bf16[64,512]{1,0:T(8,128)(2,1)S(1)} collective-permute-done((bf16[64,512]{1,0:T(8,128)(2,1)S(1)}, bf16[64,512]{1,0:T(8,128)(2,1)S(1)}, u32[]{:S(2)}, u32[]{:S(2)}) %collective-permute-start.20) | collective-permute-done | bytes 65568 | tf_op jit(solution)/shard_map/ppermute | solution.py:53
  63.7 1.3 %collective-permute-start.22 = (bf16[2,64,512]{2,1,0:T(8,128)(2,1)S(1)}, bf16[2,64,512]{2,1,0:T(8,128)(2,1)S(1)}, u32[]{:S(2)}, u32[]{:S(2)}) collective-permute-start(bf16[2,64,512]{2,1,0:T(8,128)(2,1)S(1)} %shard_map.133.after_ref.refs_0_), channel_id=1, source_target_pairs={{0,8},{8,0},{16,24},{24,16},{1,9},{9,1},{17,25},{25,17},{2,10},{10... | collective-permute-start | bytes 393224 | tf_op jit(solution)/shard_map/ppermute | solution.py:53
  65.1 1.0 %collective-permute-start.23 = (bf16[2,64,512]{2,1,0:T(8,128)(2,1)S(1)}, bf16[2,64,512]{2,1,0:T(8,128)(2,1)S(1)}, u32[]{:S(2)}, u32[]{:S(2)}) collective-permute-start(bf16[2,64,512]{2,1,0:T(8,128)(2,1)S(1)} %shard_map.133.after_ref.refs_0_), channel_id=1, source_target_pairs={{0,16},{8,24},{16,0},{24,8},{1,17},{9,25},{17,1},{25,9},{2,18},{10... | collective-permute-start | bytes 393224 | tf_op jit(solution)/shard_map/ppermute | solution.py:53
  66.1 1.2 %collective-permute-start.24 = (bf16[2,64,512]{2,1,0:T(8,128)(2,1)S(1)}, bf16[2,64,512]{2,1,0:T(8,128)(2,1)S(1)}, u32[]{:S(2)}, u32[]{:S(2)}) collective-permute-start(bf16[2,64,512]{2,1,0:T(8,128)(2,1)S(1)} %shard_map.133.after_ref.refs_0_), channel_id=1, source_target_pairs={{0,24},{8,16},{16,8},{24,0},{1,25},{9,17},{17,9},{25,1},{2,26},{10... | collective-permute-start | bytes 393224 | tf_op jit(solution)/shard_map/ppermute | solution.py:53
  67.3 1.6 %shard_map.134 = (f32[8,64,512]{2,1,0:T(8,128)}, f32[2,8,8192]{2,1,0:T(8,128)}, bf16[2,8,8192]{2,1,0:T(8,128)(2,1)}, f32[8,128]{1,0:T(8,128)S(1)}) custom-call(f32[8,64,512]{2,1,0:T(8,128)S(1)} %copy-done.2, f32[2,8,8192]{2,1,0:T(8,128)S(1)} %copy-done.3, bf16[2,64,512]{2,1,0:T(8,128)(2,1)S(1)} %shard_map.133.after_ref.refs_0_, ...), custom_call_target="tpu_custom_call" | custom-call | flops 1 | bytes 1 | tf_op jit(solution)/shard_map/pallas_call | solution.py:492
  68.9 1.0 %collective-permute-done.22.refs_1_ = bf16[2,64,512]{2,1,0:T(8,128)(2,1)S(1)} collective-permute-done((bf16[2,64,512]{2,1,0:T(8,128)(2,1)S(1)}, bf16[2,64,512]{2,1,0:T(8,128)(2,1)S(1)}, u32[]{:S(2)}, u32[]{:S(2)}) %collective-permute-start.22) | collective-permute-done | bytes 131104 | tf_op jit(solution)/shard_map/ppermute | solution.py:53
  70.3 1.6 %collective-permute-done.24.refs_3_ = bf16[2,64,512]{2,1,0:T(8,128)(2,1)S(1)} collective-permute-done((bf16[2,64,512]{2,1,0:T(8,128)(2,1)S(1)}, bf16[2,64,512]{2,1,0:T(8,128)(2,1)S(1)}, u32[]{:S(2)}, u32[]{:S(2)}) %collective-permute-start.24) | collective-permute-done | bytes 131104 | tf_op jit(solution)/shard_map/ppermute | solution.py:53
  72.0 1.4 %shard_map.135 = bf16[8,64,512]{2,1,0:T(8,128)(2,1)} custom-call(s32[1,128]{1,0:T(1,128)S(1)} %get-tuple-element.54.slot_ref, bf16[2,64,512]{2,1,0:T(8,128)(2,1)S(1)} %shard_map.133.after_ref.refs_0_, bf16[2,64,512]{2,1,0:T(8,128)(2,1)S(1)} %collective-permute-done.22.refs_1_, bf16[2,64,512]{2,1,0:T(8,128)(2,1)S(1)} %collective-permute-done.23.refs_2_, ...), custom_call_target="tpu_custom_call" | custom-call | flops 1 | bytes 1 | tf_op jit(solution)/shard_map/pallas_call | solution.py:527
  (48 shorter events, 7.8 us)
Async XLA Ops:
  0.6 27.6 %collective-permute-start.8 = (f32[2,512,512]{2,1,0:T(8,128)}, f32[2,512,512]{2,1,0:T(8,128)S(1)}, u32[]{:S(2)}, u32[]{:S(2)}) collective-permute-start(f32[2,512,512]{2,1,0:T(8,128)} %right_ref.1), channel_id=1, source_target_pairs={{0,1},{1,0},{2,3},{3,2},{4,5},{5,4},{6,7},{7,6},{8,9},{9,8},{10,11... | collective-permute-start | bytes 6291464 | tf_op jit(solution)/shard_map/ppermute | solution.py:53
  2.4 8.3 %collective-permute-start = (bf16[768,128]{1,0:T(8,128)(2,1)S(1)}, bf16[768,128]{1,0:T(8,128)(2,1)S(1)}, u32[]{:S(2)}, u32[]{:S(2)}) collective-permute-start(bf16[768,128]{1,0:T(8,128)(2,1)S(1)} %get-tuple-element.56), channel_id=1, source_target_pairs={{0,8},{8,0},{16,24},{24,16},{1,9},{9,1},{17,25},{25,17},{2,10},{10... | collective-permute-start | bytes 589832 | tf_op jit(solution)/shard_map/ppermute | solution.py:53
  5.0 11.2 %collective-permute-start.1 = (bf16[768,128]{1,0:T(8,128)(2,1)S(1)}, bf16[768,128]{1,0:T(8,128)(2,1)S(1)}, u32[]{:S(2)}, u32[]{:S(2)}) collective-permute-start(bf16[768,128]{1,0:T(8,128)(2,1)S(1)} %get-tuple-element.57), channel_id=1, source_target_pairs={{0,16},{8,24},{16,0},{24,8},{1,17},{9,25},{17,1},{25,9},{2,18},{10... | collective-permute-start | bytes 589832 | tf_op jit(solution)/shard_map/ppermute | solution.py:53
  6.5 9.7 %collective-permute-start.2 = (bf16[768,128]{1,0:T(8,128)(2,1)S(1)}, bf16[768,128]{1,0:T(8,128)(2,1)S(1)}, u32[]{:S(2)}, u32[]{:S(2)}) collective-permute-start(bf16[768,128]{1,0:T(8,128)(2,1)S(1)} %get-tuple-element.58), channel_id=1, source_target_pairs={{0,24},{8,16},{16,8},{24,0},{1,25},{9,17},{17,9},{25,1},{2,26},{10... | collective-permute-start | bytes 589832 | tf_op jit(solution)/shard_map/ppermute | solution.py:53
  17.1 5.7 %collective-permute-start.3 = (bf16[272,128]{1,0:T(8,128)(2,1)S(1)}, bf16[272,128]{1,0:T(8,128)(2,1)S(1)}, u32[]{:S(2)}, u32[]{:S(2)}) collective-permute-start(bf16[272,128]{1,0:T(8,128)(2,1)S(1)} %get-tuple-element.60), channel_id=1, source_target_pairs={{0,2},{1,3},{2,0},{3,1},{4,6},{5,7},{6,4},{7,5},{8,10},{9,11},{10,... | collective-permute-start | bytes 208904 | tf_op jit(solution)/shard_map/ppermute | solution.py:53
  18.7 7.2 %collective-permute-start.4 = (bf16[272,128]{1,0:T(8,128)(2,1)S(1)}, bf16[272,128]{1,0:T(8,128)(2,1)S(1)}, u32[]{:S(2)}, u32[]{:S(2)}) collective-permute-start(bf16[272,128]{1,0:T(8,128)(2,1)S(1)} %get-tuple-element.61), channel_id=1, source_target_pairs={{0,4},{1,5},{2,6},{3,7},{4,0},{5,1},{6,2},{7,3},{8,12},{9,13},{10,... | collective-permute-start | bytes 208904 | tf_op jit(solution)/shard_map/ppermute | solution.py:53
  21.3 6.1 %collective-permute-start.5 = (bf16[272,128]{1,0:T(8,128)(2,1)S(1)}, bf16[272,128]{1,0:T(8,128)(2,1)S(1)}, u32[]{:S(2)}, u32[]{:S(2)}) collective-permute-start(bf16[272,128]{1,0:T(8,128)(2,1)S(1)} %get-tuple-element.62), channel_id=1, source_target_pairs={{0,6},{1,7},{2,4},{3,5},{4,2},{5,3},{6,0},{7,1},{8,14},{9,15},{10,... | collective-permute-start | bytes 208904 | tf_op jit(solution)/shard_map/ppermute | solution.py:53
  21.5 6.7 %collective-permute-start.6 = (bf16[384,128]{1,0:T(8,128)(2,1)S(1)}, bf16[384,128]{1,0:T(8,128)(2,1)S(1)}, u32[]{:S(2)}, u32[]{:S(2)}) collective-permute-start(bf16[384,128]{1,0:T(8,128)(2,1)S(1)} %get-tuple-element.75.refs_0_), channel_id=1, source_target_pairs={{0,8},{8,0},{16,24},{24,16},{1,9},{9,1},{17,25},{25,17},{2,10},{10... | collective-permute-start | bytes 294920 | tf_op jit(solution)/shard_map/ppermute | solution.py:53
  22.7 5.4 %collective-permute-start.7 = (bf16[384,128]{1,0:T(8,128)(2,1)S(1)}, bf16[384,128]{1,0:T(8,128)(2,1)S(1)}, u32[]{:S(2)}, u32[]{:S(2)}) collective-permute-start(bf16[384,128]{1,0:T(8,128)(2,1)S(1)} %get-tuple-element.76.refs_1_), channel_id=1, source_target_pairs={{0,16},{8,24},{16,0},{24,8},{1,17},{9,25},{17,1},{25,9},{2,18},{10... | collective-permute-start | bytes 294920 | tf_op jit(solution)/shard_map/ppermute | solution.py:53
  28.2 5.6 %collective-permute-start.9 = (bf16[272,128]{1,0:T(8,128)(2,1)S(1)}, bf16[272,128]{1,0:T(8,128)(2,1)S(1)}, u32[]{:S(2)}, u32[]{:S(2)}) collective-permute-start(bf16[272,128]{1,0:T(8,128)(2,1)S(1)} %get-tuple-element.78), channel_id=1, source_target_pairs={{0,8},{8,0},{16,24},{24,16},{1,9},{9,1},{17,25},{25,17},{2,10},{10... | collective-permute-start | bytes 208904 | tf_op jit(solution)/shard_map/ppermute | solution.py:53
  29.6 4.3 %collective-permute-start.10 = (bf16[272,128]{1,0:T(8,128)(2,1)S(1)}, bf16[272,128]{1,0:T(8,128)(2,1)S(1)}, u32[]{:S(2)}, u32[]{:S(2)}) collective-permute-start(bf16[272,128]{1,0:T(8,128)(2,1)S(1)} %get-tuple-element.79), channel_id=1, source_target_pairs={{0,16},{8,24},{16,0},{24,8},{1,17},{9,25},{17,1},{25,9},{2,18},{10... | collective-permute-start | bytes 208904 | tf_op jit(solution)/shard_map/ppermute | solution.py:53
  30.3 5.2 %collective-permute-start.11 = (bf16[272,128]{1,0:T(8,128)(2,1)S(1)}, bf16[272,128]{1,0:T(8,128)(2,1)S(1)}, u32[]{:S(2)}, u32[]{:S(2)}) collective-permute-start(bf16[272,128]{1,0:T(8,128)(2,1)S(1)} %get-tuple-element.80), channel_id=1, source_target_pairs={{0,24},{8,16},{16,8},{24,0},{1,25},{9,17},{17,9},{25,1},{2,26},{10... | collective-permute-start | bytes 208904 | tf_op jit(solution)/shard_map/ppermute | solution.py:53
  31.8 5.2 %collective-permute-start.13 = (bf16[512,128]{1,0:T(8,128)(2,1)S(1)}, bf16[512,128]{1,0:T(8,128)(2,1)S(1)}, u32[]{:S(2)}, u32[]{:S(2)}) collective-permute-start(bf16[512,128]{1,0:T(8,128)(2,1)S(1)} %get-tuple-element.82.refs_1_), channel_id=1, source_target_pairs={{0,16},{8,24},{16,0},{24,8},{1,17},{9,25},{17,1},{25,9},{2,18},{10... | collective-permute-start | bytes 393224 | tf_op jit(solution)/shard_map/ppermute | solution.py:53
  33.3 6.4 %collective-permute-start.12 = (bf16[512,128]{1,0:T(8,128)(2,1)S(1)}, bf16[512,128]{1,0:T(8,128)(2,1)S(1)}, u32[]{:S(2)}, u32[]{:S(2)}) collective-permute-start(bf16[512,128]{1,0:T(8,128)(2,1)S(1)} %get-tuple-element.81.refs_0_), channel_id=1, source_target_pairs={{0,8},{8,0},{16,24},{24,16},{1,9},{9,1},{17,25},{25,17},{2,10},{10... | collective-permute-start | bytes 393224 | tf_op jit(solution)/shard_map/ppermute | solution.py:53
  37.0 6.0 %copy-start = (f32[2,512,512]{2,1,0:T(8,128)S(1)}, f32[2,512,512]{2,1,0:T(8,128)}, u32[]{:S(2)}) copy-start(f32[2,512,512]{2,1,0:T(8,128)} %left_ref.3) | copy-start | bytes 6291460
  39.7 11.4 %collective-permute-start.16 = (bf16[1792,128]{1,0:T(8,128)(2,1)S(1)}, bf16[1792,128]{1,0:T(8,128)(2,1)S(1)}, u32[]{:S(2)}, u32[]{:S(2)}) collective-permute-start(bf16[1792,128]{1,0:T(8,128)(2,1)S(1)} %shard_map.127), channel_id=1, source_target_pairs={{0,8},{8,0},{16,24},{24,16},{1,9},{9,1},{17,25},{25,17},{2,10},{10... | collective-permute-start | bytes 1376264 | tf_op jit(solution)/shard_map/ppermute | solution.py:53
  39.8 11.3 %collective-permute-start.15 = (bf16[1792,128]{1,0:T(8,128)(2,1)S(1)}, bf16[1792,128]{1,0:T(8,128)(2,1)S(1)}, u32[]{:S(2)}, u32[]{:S(2)}) collective-permute-start(bf16[1792,128]{1,0:T(8,128)(2,1)S(1)} %shard_map.126), channel_id=1, source_target_pairs={{0,16},{8,24},{16,0},{24,8},{1,17},{9,25},{17,1},{25,9},{2,18},{10... | collective-permute-start | bytes 1376264 | tf_op jit(solution)/shard_map/ppermute | solution.py:53
  41.4 1.6 %collective-permute-start.14 = (bf16[4,272,128]{2,1,0:T(8,128)(2,1)S(1)}, bf16[4,272,128]{2,1,0:T(8,128)(2,1)S(1)}, u32[]{:S(2)}, u32[]{:S(2)}) collective-permute-start(bf16[4,272,128]{2,1,0:T(8,128)(2,1)S(1)} %shard_map.124.mine_ref.refs_1_), channel_id=1, source_target_pairs={{0,1},{1,0},{2,3},{3,2},{4,5},{5,4},{6,7},{7,6},{8,9},{9,8},{10,11... | collective-permute-start | bytes 835592 | tf_op jit(solution)/shard_map/ppermute | solution.py:53
  51.1 7.5 %copy-start.1 = (f32[2,512,512]{2,1,0:T(8,128)S(1)}, f32[2,512,512]{2,1,0:T(8,128)}, u32[]{:S(2)}) copy-start(f32[2,512,512]{2,1,0:T(8,128)} %right_ref.1) | copy-start | bytes 6291460
  51.1 2.0 %collective-permute-start.17 = (bf16[512,512]{1,0:T(8,128)(2,1)S(1)}, bf16[512,512]{1,0:T(8,128)(2,1)S(1)}, u32[]{:S(2)}, u32[]{:S(2)}) collective-permute-start(bf16[512,512]{1,0:T(8,128)(2,1)S(1)} %shard_map.128.mine_ref), channel_id=1, source_target_pairs={{0,1},{1,0},{2,3},{3,2},{4,5},{5,4},{6,7},{7,6},{8,9},{9,8},{10,11... | collective-permute-start | bytes 1572872 | tf_op jit(solution)/shard_map/ppermute | solution.py:53
  51.4 2.8 %collective-permute-start.18 = (bf16[4,2,256,128]{3,2,1,0:T(8,128)(2,1)S(1)}, bf16[4,2,256,128]{3,2,1,0:T(8,128)(2,1)S(1)}, u32[]{:S(2)}, u32[]{:S(2)}) collective-permute-start(bf16[4,2,256,128]{3,2,1,0:T(8,128)(2,1)S(1)} %get-tuple-element.89), channel_id=1, source_target_pairs={{0,1},{1,0},{2,3},{3,2},{4,5},{5,4},{6,7},{7,6},{8,9},{9,8},{10,11... | collective-permute-start | bytes 1572872 | tf_op jit(solution)/shard_map/ppermute | solution.py:53
  54.2 7.3 %collective-permute-start.19 = (bf16[64,512]{1,0:T(8,128)(2,1)S(1)}, bf16[64,512]{1,0:T(8,128)(2,1)S(1)}, u32[]{:S(2)}, u32[]{:S(2)}) collective-permute-start(bf16[64,512]{1,0:T(8,128)(2,1)S(1)} %get-tuple-element.91), channel_id=1, source_target_pairs={{0,2},{1,3},{2,0},{3,1},{4,6},{5,7},{6,4},{7,5},{8,10},{9,11},{10,... | collective-permute-start | bytes 196616 | tf_op jit(solution)/shard_map/ppermute | solution.py:53
  54.2 8.7 %collective-permute-start.20 = (bf16[64,512]{1,0:T(8,128)(2,1)S(1)}, bf16[64,512]{1,0:T(8,128)(2,1)S(1)}, u32[]{:S(2)}, u32[]{:S(2)}) collective-permute-start(bf16[64,512]{1,0:T(8,128)(2,1)S(1)} %get-tuple-element.92), channel_id=1, source_target_pairs={{0,4},{1,5},{2,6},{3,7},{4,0},{5,1},{6,2},{7,3},{8,12},{9,13},{10,... | collective-permute-start | bytes 196616 | tf_op jit(solution)/shard_map/ppermute | solution.py:53
  56.8 6.2 %collective-permute-start.21 = (bf16[64,512]{1,0:T(8,128)(2,1)S(1)}, bf16[64,512]{1,0:T(8,128)(2,1)S(1)}, u32[]{:S(2)}, u32[]{:S(2)}) collective-permute-start(bf16[64,512]{1,0:T(8,128)(2,1)S(1)} %get-tuple-element.93), channel_id=1, source_target_pairs={{0,6},{1,7},{2,4},{3,5},{4,2},{5,3},{6,0},{7,1},{8,14},{9,15},{10,... | collective-permute-start | bytes 196616 | tf_op jit(solution)/shard_map/ppermute | solution.py:53
  58.6 8.7 %copy-start.2 = (f32[8,64,512]{2,1,0:T(8,128)S(1)}, f32[8,64,512]{2,1,0:T(8,128)}, u32[]{:S(2)}) copy-start(f32[8,64,512]{2,1,0:T(8,128)} %accum_ref.1) | copy-start | bytes 3145732
  58.6 8.7 %copy-start.3 = (f32[2,8,8192]{2,1,0:T(8,128)S(1)}, f32[2,8,8192]{2,1,0:T(8,128)}, u32[]{:S(2)}) copy-start(f32[2,8,8192]{2,1,0:T(8,128)} %vocab_ref.1) | copy-start | bytes 1572868
  63.7 6.1 %collective-permute-start.22 = (bf16[2,64,512]{2,1,0:T(8,128)(2,1)S(1)}, bf16[2,64,512]{2,1,0:T(8,128)(2,1)S(1)}, u32[]{:S(2)}, u32[]{:S(2)}) collective-permute-start(bf16[2,64,512]{2,1,0:T(8,128)(2,1)S(1)} %shard_map.133.after_ref.refs_0_), channel_id=1, source_target_pairs={{0,8},{8,0},{16,24},{24,16},{1,9},{9,1},{17,25},{25,17},{2,10},{10... | collective-permute-start | bytes 393224 | tf_op jit(solution)/shard_map/ppermute | solution.py:53
  65.1 5.3 %collective-permute-start.23 = (bf16[2,64,512]{2,1,0:T(8,128)(2,1)S(1)}, bf16[2,64,512]{2,1,0:T(8,128)(2,1)S(1)}, u32[]{:S(2)}, u32[]{:S(2)}) collective-permute-start(bf16[2,64,512]{2,1,0:T(8,128)(2,1)S(1)} %shard_map.133.after_ref.refs_0_), channel_id=1, source_target_pairs={{0,16},{8,24},{16,0},{24,8},{1,17},{9,25},{17,1},{25,9},{2,18},{10... | collective-permute-start | bytes 393224 | tf_op jit(solution)/shard_map/ppermute | solution.py:53
  66.1 5.9 %collective-permute-start.24 = (bf16[2,64,512]{2,1,0:T(8,128)(2,1)S(1)}, bf16[2,64,512]{2,1,0:T(8,128)(2,1)S(1)}, u32[]{:S(2)}, u32[]{:S(2)}) collective-permute-start(bf16[2,64,512]{2,1,0:T(8,128)(2,1)S(1)} %shard_map.133.after_ref.refs_0_), channel_id=1, source_target_pairs={{0,24},{8,16},{16,8},{24,0},{1,25},{9,17},{17,9},{25,1},{2,26},{10... | collective-permute-start | bytes 393224 | tf_op jit(solution)/shard_map/ppermute | solution.py:53
where the time goes:
time: 73.6 us; the launch traced here: 73.4 us
  starting transfers between devices  27.2 us (37%)
  waiting for transfers between devices  25.7 us (35%)
  Pallas kernels  18.6 us (25%)
  local copies, waits for them, and re-layouts  0.99 us (1%)
  between operations  0.84 us (1%)
    ppermute x25, starting transfers between devices, exchange(): return lax.ppermute(values, axis, [(i, i ^ mask) for i in range(size)])  27.2 us
    ppermute x25, waiting for transfers between devices, exchange(): return lax.ppermute(values, axis, [(i, i ^ mask) for i in range(size)])  25.7 us
    pallas_call x1, Pallas kernels, on_device(): call(root_body, [shape(square, BF16), shape((8, cols), F32)], [SMEM, VMEM...  8.05 us
    pallas_call x1, Pallas kernels, on_device(): pl.pallas_call(stats_body, grid=(most,), out_shape=[shape(left_stats.shap...  2.81 us
    pallas_call x1, Pallas kernels, on_device(): call(accum_body, [shape(graft_accum.shape, F32), shape(vocab_accum.shape,...  1.56 us
  transfers between devices with their start and end apart: 25, of which 14 were waited for; matrix products, arithmetic and copies ran while one was open for 1% of the time, Pallas kernels for 22%

commit v1 on v0

--- a/solution.py
+++ b/solution.py
@@ -15,6 +15,7 @@
 HBM = pl.BlockSpec(memory_space=pltpu.HBM)
 MIB = 1 << 20
 LONG = 4 * 10**9
+SWAP = 1
 
 
 def shape(dims, dtype):
@@ -116,15 +117,25 @@
             visit(s, block, count)
             count = count + jnp.where(block >= 0, 1, 0)
 
-    def local_slots(slot_ref, who, local_of):
-        plane_here = place()[1]
-        for j in range(reps):
-            local_of[j] = 0
+    at_local, at_place, at_block = 0, reps, reps + planes
+    width = -(-(at_block + blocks) // 128) * 128
+
+    def book_body(slot_ref, out_ref, who):
+        rep_here, plane_here, _ = place()
+        line = lax.broadcasted_iota(jnp.int32, out_ref.shape, 1)
+        out_ref[...] = jnp.where((line >= at_place) & (line < at_block), -1, 0)
 
         def visit(s, block, count):
-            @pl.when((block >= 0) & (plane_here == s // per))
+            @pl.when(block >= 0)
             def _():
-                local_of[count % reps] = s % per
+                entry = out_ref[...]
+                here = (plane_here == s // per) & (line == at_local + count % reps)
+                entry = jnp.where(here, s % per, entry)
+                near = (count % reps == rep_here) & (
+                    line == at_place + (plane_here ^ (s // per))
+                )
+                entry = jnp.where(near, count // reps, entry)
+                out_ref[...] = jnp.where(line == at_block + count, block, entry)
 
         ranked(slot_ref, who, visit)
 
@@ -161,7 +172,12 @@
     terms = [pieces[0]] + [exchange(pieces[k], "rep", k, reps) for k in rep_partners]
     payload_rows = per * rows + TAIL
 
-    book = [pltpu.SMEM((slots,), jnp.int32), pltpu.SMEM((reps,), jnp.int32)]
+    book = call(
+        book_body,
+        shape((1, width), jnp.int32),
+        [SMEM],
+        scratch=[pltpu.SMEM((slots,), jnp.int32)],
+    )(table)
 
     def sum_body(slot_ref, *refs):
         term_refs, accum_ref, share_refs = refs[:reps], refs[reps], refs[reps + 1 : reps + 3]
@@ -225,10 +241,9 @@
     def route_body(slot_ref, *refs):
         in_refs = refs[:planes]
         out_refs = refs[planes : planes + reps]
-        half_refs = refs[planes + reps : planes + reps + most]
-        parts, tail, who, local_of = refs[planes + reps + most :]
+        whole_ref, rest_refs = refs[planes + reps], refs[planes + reps + 1 : planes + 2 * reps]
+        parts, tail = refs[planes + 2 * reps :]
         rep_here = place()[0]
-        local_slots(slot_ref, who, local_of)
         total = jnp.zeros((per, cols), F32)
         for ref in in_refs:
             bits = ref[per * rows :, :].astype(F32)
@@ -237,7 +252,7 @@
         parts[:per, :] = total
         tail[...] = jnp.zeros_like(tail)
         for j in range(reps):
-            local = local_of[rep_here ^ j]
+            local = slot_ref[0, at_local + (rep_here ^ j)]
             for s in range(per):
 
                 @pl.when(local == s)
@@ -250,44 +265,49 @@
             for t, term in enumerate(three_terms(parts[pl.ds(local, 1), :])):
                 tail[t : t + 1, :] = term
             out_refs[j][planes * rows :, :] = tail[...].astype(BF16)
+        piece = planes * rows
         for k in range(planes):
-            for m in range(most):
-                for side in range(2):
-                    s = side * most + m
-                    at = (side * planes + k) * rows
-                    half_refs[m][at : at + rows, :] = in_refs[k][s * rows : (s + 1) * rows, :]
-
-    half = shape((2 * planes * rows, cols), BF16)
+            for s in range(per):
+                at = s * piece + k * rows
+                whole_ref[at : at + rows, :] = in_refs[k][s * rows : (s + 1) * rows, :]
+        for j in rep_partners:
+            for i in range(per - 1):
+                first = (slot_ref[0, at_local + (rep_here ^ j)] + 1 + i) % per * piece
+                rest_refs[j - 1][i * piece : (i + 1) * piece, :] = whole_ref[
+                    pl.ds(pl.multiple_of(first, piece), piece), :
+                ]
+
+    piece_rows = planes * rows
     routed = call(
         route_body,
-        [shape((part_rows, cols), BF16)] * reps + [half] * most,
+        [shape((part_rows, cols), BF16)] * reps
+        + [shape((per * piece_rows, cols), BF16)]
+        + [shape(((per - 1) * piece_rows, cols), BF16)] * (reps - 1),
         [SMEM] + [VMEM] * planes,
-        scratch=[pltpu.VMEM((8, cols), F32), pltpu.VMEM((TAIL, cols), F32)] + book,
-    )(table, *arrived)
+        scratch=[pltpu.VMEM((8, cols), F32), pltpu.VMEM((TAIL, cols), F32)],
+    )(book, *arrived)
     routed = late(routed, *share_firsts, right_other)
-    parts, halves = routed[:reps], routed[reps:]
+    parts, whole, rests = routed[:reps], routed[reps], routed[reps + 1 :]
 
     met = [parts[0]] + [exchange(parts[j], "rep", j, reps) for j in rep_partners]
-    firsts = [exchange(halves[m], "rep", ways[m][0], reps) for m in range(2)]
-    mine = late([jnp.stack(met)], *firsts)[0]
-    other = exchange(mine, "fsdp", 1, indices)
-    half_rows = 2 * planes * rows
-    lasts = []
-    for m in range(2):
-        arrays = (halves[m], firsts[m], shares[m], share_firsts[m])
-        joined = jnp.concatenate([array.reshape(-1, cols) for array in arrays])
-        lasts.append(exchange(fence([joined], mine)[0], "rep", ways[m][1], reps))
+    mine = [jnp.stack(met[i : i + SWAP]) for i in range(0, reps, SWAP)]
+    other = [exchange(array, "fsdp", 1, indices) for array in mine]
+
+    rests_met = [exchange(rests[j - 1], "rep", j, reps) for j in rep_partners]
 
     def assemble(grad, rep_here, plane_here, core_here, piece, k, j):
         row = pl.multiple_of((2 * (plane_here ^ k) + core_here) * rows, rows)
         col = pl.multiple_of((rep_here ^ j) * cols, cols)
         grad[pl.ds(row, rows), pl.ds(col, cols)] = piece.astype(scratch_type)
 
-    def root_body(slot_ref, mine_ref, other_ref, left_ref, right_ref,
-                  out_ref, graft_ref, grad, matrix, start, who, local_of, sem):
+    swaps = len(mine)
+
+    def root_body(slot_ref, *refs):
+        mine_refs, other_refs = refs[:swaps], refs[swaps : 2 * swaps]
+        left_ref, right_ref, out_ref, graft_ref, grad, matrix, start, sem = refs[2 * swaps :]
         rep_here, plane_here, core_here = place()
-        local_slots(slot_ref, who, local_of)
-        owner, at = local_of[rep_here] // most, local_of[rep_here] % most
+        local = slot_ref[0, at_local + rep_here]
+        owner, at = local // most, local % most
 
         @pl.when(owner == core_here)
         def _():
@@ -299,11 +319,12 @@
 
         graft = jnp.zeros((1, cols), F32)
         for j in range(reps):
-            for ref, side in ((mine_ref, core_here), (other_ref, 1 - core_here)):
+            for swap_refs, side in ((mine_refs, core_here), (other_refs, 1 - core_here)):
+                ref = swap_refs[j // SWAP].at[j % SWAP]
                 for k in range(planes):
                     assemble(grad, rep_here, plane_here, side,
-                             ref[j, k * rows : (k + 1) * rows, :], k, j)
-                bits = ref[j, planes * rows :, :].astype(F32)
+                             ref[k * rows : (k + 1) * rows, :], k, j)
+                bits = ref[planes * rows :, :].astype(F32)
                 graft = graft + jnp.sum(bits[:8], axis=0, keepdims=True)
         line = lax.broadcasted_iota(jnp.int32, graft_ref.shape, 0)
         first = jnp.where(owner == core_here, 1.0, 0.0)
@@ -337,18 +358,17 @@
     root, graft_sum = call(
         root_body,
         [shape(square, BF16), shape((8, cols), F32)],
-        [SMEM, VMEM, VMEM, ANY, ANY],
+        [SMEM] + [VMEM] * (2 * swaps) + [ANY, ANY],
         scratch=[
             pltpu.VMEM(square, scratch_type),
             pltpu.VMEM(square, F32),
             pltpu.VMEM(square, F32),
-        ]
-        + book
-        + [pltpu.SemaphoreType.DMA],
+            pltpu.SemaphoreType.DMA,
+        ],
         flops=1,
         vmem=20,
-    )(table, mine, other, left_stats, right_other)
-    root = fence([root], *lasts)[0]
+    )(book, *mine, *other, left_stats, right_other)
+    root = fence([root], *rests_met)[0]
     root_other = exchange(root, "fsdp", 1, indices)
 
     def finish_body(mine_ref, other_ref, graft_ref, *refs):
@@ -380,31 +400,45 @@
         flops=2 * order**3,
     )(root, root_other, graft_sum)
 
-    def side_body(*refs):
-        keep_ref, give_ref = refs[6:]
-        core_here = place()[2]
-        side_rows = planes * rows
-        for m in range(2):
-            own_ref, first_ref, last_ref = refs[m], refs[2 + m], refs[4 + m]
-            near, far = ways[m]
-            places = (
-                (0, own_ref, 0),
-                (near, first_ref, 0),
-                (far, last_ref, 0),
-                (near ^ far, last_ref, half_rows),
-            )
-            for j, ref, at in places:
-                for target, side in ((keep_ref, core_here), (give_ref, 1 - core_here)):
-                    first = pl.multiple_of(at + side * side_rows, side_rows)
-                    target[j, m] = ref[pl.ds(first, side_rows), :]
-
-    side = shape((reps, most, planes * rows, cols), BF16)
-    keep, give = call(side_body, [side, side], [VMEM] * 6)(*halves, *firsts, *lasts)
+    def side_body(slot_ref, whole_ref, *refs):
+        met_refs, rest_refs = refs[: reps - 1], refs[reps - 1 : 2 * reps - 2]
+        keep_ref, give_ref, held = refs[2 * reps - 2 :]
+        rep_here, _, core_here = place()
+        local = slot_ref[0, at_local + rep_here]
+        for s in range(per):
+            held[0, s] = whole_ref[s * piece_rows : (s + 1) * piece_rows, :]
+        for j in rep_partners:
+            held[j, local] = met_refs[j - 1][:piece_rows, :]
+            for i in range(per - 1):
+                held[j, (local + 1 + i) % per] = rest_refs[j - 1][
+                    i * piece_rows : (i + 1) * piece_rows, :
+                ]
+        for j in range(reps):
+            for m in range(most):
+                keep_ref[j, m] = held[j, core_here * most + m]
+                give_ref[j, m] = held[j, (1 - core_here) * most + m]
+
+    side = shape((reps, most, piece_rows, cols), BF16)
+    keep, give = call(
+        side_body,
+        [side, side],
+        [SMEM] + [VMEM] * (2 * reps - 1),
+        scratch=[pltpu.VMEM((reps, per, piece_rows, cols), BF16)],
+    )(book, whole, *met[1:], *rests_met)
     other_side = exchange(give, "fsdp", 1, indices)
-    slabs = fence(slabs, other_side)
 
     returned = [slabs[0]] + [
         exchange(slabs[k], "fsdp", 2 * k, indices) for k in plane_partners
+    ]
+
+    share_lasts = [
+        exchange(
+            fence([jnp.concatenate([shares[m], share_firsts[m]])], slabs[0])[0],
+            "rep",
+            ways[m][1],
+            reps,
+        )
+        for m in range(2)
     ]
 
     def stats_body(left_ref, right_ref, after_ref, keep_ref, other_ref,
@@ -437,26 +471,20 @@
     )(left_stats, right_stats, slabs[0], keep, other_side)
 
     def pick_body(slot_ref, *refs):
-        out_ref, who = refs[-2:]
-        rep_here, plane_here, _ = place()
-
-        def visit(s, block, count):
-            @pl.when((block >= 0) & (count % reps == rep_here))
+        out_ref = refs[-1]
+        for k in range(planes):
+            spot = slot_ref[0, at_place + k]
+
+            @pl.when(spot >= 0)
             def _():
-                for k in range(planes):
-
-                    @pl.when(plane_here == (s // per) ^ k)
-                    def _():
-                        out_ref[count // reps] = refs[k][...]
-
-        ranked(slot_ref, who, visit)
+                out_ref[spot] = refs[k][...]
 
     picked = call(
         pick_body,
         shape((share, rows, order), BF16),
         [SMEM] + [VMEM] * planes + [ANY],
-        scratch=book[:1],
-    )(table, *returned, stats_token)
+    )(book, *returned, stats_token)
+    picked = fence(fence([picked], flops=LONG), *share_lasts)[0]
     gathered = [picked] + [exchange(picked, "rep", j, reps) for j in rep_partners]
 
     def accum_body(accum_ref, vocab_ref, after_ref, *refs):
@@ -467,8 +495,8 @@
             ref, base = {
                 0: (refs[m], 0),
                 near: (refs[2 + m], 0),
-                far: (refs[4 + m], 2 * half_rows),
-                near ^ far: (refs[4 + m], 2 * half_rows + share_rows),
+                far: (refs[4 + m], 0),
+                near ^ far: (refs[4 + m], share_rows),
             }[j]
             return ref[base + at : base + at + count, :].astype(F32)
 
@@ -499,22 +527,16 @@
         ],
         [VMEM, VMEM, ANY] + [VMEM] * 6,
         vmem=12,
-    )(graft_accum, vocab_accum, picked, *shares, *share_firsts, *lasts)
+    )(graft_accum, vocab_accum, picked, *shares, *share_firsts, *share_lasts)
 
     def place_body(slot_ref, *refs):
-        out_ref, who, block_of, sem = refs[reps + 1 :]
+        out_ref, sem = refs[reps + 1 :]
         rep_here = place()[0]
 
-        def visit(s, block, count):
-            @pl.when(block >= 0)
-            def _():
-                block_of[count] = block
-
-        ranked(slot_ref, who, visit)
         copies = []
         for j in range(reps):
             for m in range(share):
-                block = block_of[m * reps + (rep_here ^ j)]
+                block = slot_ref[0, at_block + m * reps + (rep_here ^ j)]
                 copies.append(
                     pltpu.make_async_copy(
                         refs[j].at[m], out_ref.at[block], sem.at[j * share + m]
@@ -529,12 +551,8 @@
         shape((blocks, rows, order), BF16),
         [SMEM] + [VMEM] * reps + [ANY],
         out_specs=HBM,
-        scratch=[
-            book[0],
-            pltpu.SMEM((blocks,), jnp.int32),
-            pltpu.SemaphoreType.DMA((blocks,)),
-        ],
-    )(table, *gathered, accum_token)
+        scratch=[pltpu.SemaphoreType.DMA((blocks,))],
+    )(book, *gathered, accum_token)
     return (direction, graft_accum_new, left_new, right_new, vocab_accum_new, vocab_step)
 
 

time: 73.6 us -> 71.5 us (0.971)
  waiting for transfers between devices: 25.7 us -> 20.2 us
  starting transfers between devices: 27.2 us -> 29.6 us
  Pallas kernels: 18.6 us -> 19.6 us
    ppermute x25 -> x29, waiting for transfers between devices: 25.7 us -> 20.2 us  [exchange(): return lax.ppermute(values, axis, [(i, i ^ mask) for i in range(size)])]
    ppermute x25 -> x29, starting transfers between devices: 27.2 us -> 29.6 us  [exchange(): return lax.ppermute(values, axis, [(i, i ^ mask) for i in range(size)])]
    pallas_call x3 -> x4, Pallas kernels: 8.87 us -> 10.1 us  [the longest x1 8 us: on_device(): call(root_body, [shape(square, BF16), shape((8, cols), F32)], [SMEM] + [V...]
  transfers between devices with their start and end apart: 25 -> 29, of which waited for: 14 -> 16; matrix products, arithmetic and copies ran while one was open for 1% -> 1% of each run, Pallas kernels for 22% -> 26%
where the time goes in v1:
time: 71.5 us; the launch traced here: 71.3 us
  starting transfers between devices  29.6 us (41%)
  waiting for transfers between devices  20.2 us (28%)
  Pallas kernels  19.6 us (27%)
  local copies, waits for them, and re-layouts  0.99 us (1%)
  between operations  0.83 us (1%)
    ppermute x29, starting transfers between devices, exchange(): return lax.ppermute(values, axis, [(i, i ^ mask) for i in range(size)])  29.6 us
    ppermute x29, waiting for transfers between devices, exchange(): return lax.ppermute(values, axis, [(i, i ^ mask) for i in range(size)])  20.2 us
    pallas_call x1, Pallas kernels, on_device(): call(root_body, [shape(square, BF16), shape((8, cols), F32)], [SMEM] + [V...  8 us
    pallas_call x1, Pallas kernels, on_device(): pl.pallas_call(stats_body, grid=(most,), out_shape=[shape(left_stats.shap...  2.79 us
    pallas_call x1, Pallas kernels, on_device(): call(accum_body, [shape(graft_accum.shape, F32), shape(vocab_accum.shape,...  1.56 us
  transfers between devices with their start and end apart: 29, of which 16 were waited for; matrix products, arithmetic and copies ran while one was open for 1% of the time, Pallas kernels for 26%

profile of v1, /device:TPU:0, one launch (start us, length us, event | category | flops | bytes accessed | tf_op | source)
XLA Modules:
  0.0 71.3 jit_solution(8176329008983106208)
XLA Ops:
  1.1 1.3 %shard_map.118 = (bf16[768,128]{1,0:T(8,128)(2,1)S(1)}, bf16[768,128]{1,0:T(8,128)(2,1)S(1)}, bf16[768,128]{1,0:T(8,128)(2,1)S(1)}, bf16[768,128]{1,0:T(8,128)(2,1)S(1)}, s32[1,128]{1,0:T(1,128)S(1)}) custom-call(s32[8]{0:T(128)} %slot_ref.1, bf16[8,64,512]{2,1,0:T(8,128)(2,1)} %bitcast.14, bf16[2,8,8192]{2,1,0:T(8,128)(2,1)} %bitcast.15), custom_call_target="tpu_custom_call" | custom-call | flops 1 | bytes 1 | tf_op jit(solution)/shard_map/pallas_call | solution.py:160
  2.4 2.6 %collective-permute-start = (bf16[768,128]{1,0:T(8,128)(2,1)S(1)}, bf16[768,128]{1,0:T(8,128)(2,1)S(1)}, u32[]{:S(2)}, u32[]{:S(2)}) collective-permute-start(bf16[768,128]{1,0:T(8,128)(2,1)S(1)} %get-tuple-element.58), channel_id=1, source_target_pairs={{0,8},{8,0},{16,24},{24,16},{1,9},{9,1},{17,25},{25,17},{2,10},{10... | collective-permute-start | bytes 589832 | tf_op jit(solution)/shard_map/ppermute | solution.py:54
  5.0 1.5 %collective-permute-start.1 = (bf16[768,128]{1,0:T(8,128)(2,1)S(1)}, bf16[768,128]{1,0:T(8,128)(2,1)S(1)}, u32[]{:S(2)}, u32[]{:S(2)}) collective-permute-start(bf16[768,128]{1,0:T(8,128)(2,1)S(1)} %get-tuple-element.59), channel_id=1, source_target_pairs={{0,16},{8,24},{16,0},{24,8},{1,17},{9,25},{17,1},{25,9},{2,18},{10... | collective-permute-start | bytes 589832 | tf_op jit(solution)/shard_map/ppermute | solution.py:54
  6.5 1.0 %constant_dynamic-slice_fusion.refs_4_ = f32[8,64,128]{2,1,0:T(8,128)S(1)} fusion(f32[8,64,512]{2,1,0:T(8,128)} %accum_ref.1, s32[]{:T(128)S(6)} %select_n.3), kind=kLoop, calls=%fused_computation.2 | loop fusion | bytes 524292 | tf_op jit(solution)/shard_map/dynamic_slice | solution.py:168
  7.5 3.2 %collective-permute-done.refs_1_ = bf16[768,128]{1,0:T(8,128)(2,1)S(1)} collective-permute-done((bf16[768,128]{1,0:T(8,128)(2,1)S(1)}, bf16[768,128]{1,0:T(8,128)(2,1)S(1)}, u32[]{:S(2)}, u32[]{:S(2)}) %collective-permute-start) | collective-permute-done | bytes 196640 | tf_op jit(solution)/shard_map/ppermute | solution.py:54
  10.7 5.5 %collective-permute-done.1.refs_2_ = bf16[768,128]{1,0:T(8,128)(2,1)S(1)} collective-permute-done((bf16[768,128]{1,0:T(8,128)(2,1)S(1)}, bf16[768,128]{1,0:T(8,128)(2,1)S(1)}, u32[]{:S(2)}, u32[]{:S(2)}) %collective-permute-start.1) | collective-permute-done | bytes 196640 | tf_op jit(solution)/shard_map/ppermute | solution.py:54
  16.2 0.8 %shard_map.120 = (bf16[384,128]{1,0:T(8,128)(2,1)S(1)}, bf16[384,128]{1,0:T(8,128)(2,1)S(1)}, bf16[272,128]{1,0:T(8,128)(2,1)S(1)}, bf16[272,128]{1,0:T(8,128)(2...) custom-call(s32[1,128]{1,0:T(1,128)S(1)} %get-tuple-element.56.slot_ref, ...), custom_call_target="tpu_custom_call" | custom-call | flops 1 | bytes 1 | tf_op jit(solution)/shard_map/pallas_call | solution.py:221
  17.1 1.6 %collective-permute-start.3 = (bf16[272,128]{1,0:T(8,128)(2,1)S(1)}, bf16[272,128]{1,0:T(8,128)(2,1)S(1)}, u32[]{:S(2)}, u32[]{:S(2)}) collective-permute-start(bf16[272,128]{1,0:T(8,128)(2,1)S(1)} %get-tuple-element.62), channel_id=1, source_target_pairs={{0,2},{1,3},{2,0},{3,1},{4,6},{5,7},{6,4},{7,5},{8,10},{9,11},{10,... | collective-permute-start | bytes 208904 | tf_op jit(solution)/shard_map/ppermute | solution.py:54
  18.7 2.6 %collective-permute-start.4 = (bf16[272,128]{1,0:T(8,128)(2,1)S(1)}, bf16[272,128]{1,0:T(8,128)(2,1)S(1)}, u32[]{:S(2)}, u32[]{:S(2)}) collective-permute-start(bf16[272,128]{1,0:T(8,128)(2,1)S(1)} %get-tuple-element.63), channel_id=1, source_target_pairs={{0,4},{1,5},{2,6},{3,7},{4,0},{5,1},{6,2},{7,3},{8,12},{9,13},{10,... | collective-permute-start | bytes 208904 | tf_op jit(solution)/shard_map/ppermute | solution.py:54
  21.5 0.8 %shard_map.119.slot_ref = s32[1,128]{1,0:T(1,128)S(1)} custom-call(s32[1,128]{1,0:T(1,128)S(1)} %get-tuple-element.56.slot_ref), custom_call_target="tpu_custom_call" | custom-call | flops 1 | bytes 1 | tf_op jit(solution)/shard_map/pallas_call | solution.py:175
  22.3 1.3 %collective-permute-start.6 = (bf16[384,128]{1,0:T(8,128)(2,1)S(1)}, bf16[384,128]{1,0:T(8,128)(2,1)S(1)}, u32[]{:S(2)}, u32[]{:S(2)}) collective-permute-start(bf16[384,128]{1,0:T(8,128)(2,1)S(1)} %get-tuple-element.81.refs_0_), channel_id=1, source_target_pairs={{0,8},{8,0},{16,24},{24,16},{1,9},{9,1},{17,25},{25,17},{2,10},{10... | collective-permute-start | bytes 294920 | tf_op jit(solution)/shard_map/ppermute | solution.py:54
  23.6 0.8 %collective-permute-start.7 = (bf16[384,128]{1,0:T(8,128)(2,1)S(1)}, bf16[384,128]{1,0:T(8,128)(2,1)S(1)}, u32[]{:S(2)}, u32[]{:S(2)}) collective-permute-start(bf16[384,128]{1,0:T(8,128)(2,1)S(1)} %get-tuple-element.82.refs_1_), channel_id=1, source_target_pairs={{0,16},{8,24},{16,0},{24,8},{1,17},{9,25},{17,1},{25,9},{2,18},{10... | collective-permute-start | bytes 294920 | tf_op jit(solution)/shard_map/ppermute | solution.py:54
  24.4 1.5 %collective-permute-done.4.refs_2_ = bf16[272,128]{1,0:T(8,128)(2,1)S(1)} collective-permute-done((bf16[272,128]{1,0:T(8,128)(2,1)S(1)}, bf16[272,128]{1,0:T(8,128)(2,1)S(1)}, u32[]{:S(2)}, u32[]{:S(2)}) %collective-permute-start.4) | collective-permute-done | bytes 69664 | tf_op jit(solution)/shard_map/ppermute | solution.py:54
  25.9 1.5 %collective-permute-done.5.refs_3_ = bf16[272,128]{1,0:T(8,128)(2,1)S(1)} collective-permute-done((bf16[272,128]{1,0:T(8,128)(2,1)S(1)}, bf16[272,128]{1,0:T(8,128)(2,1)S(1)}, u32[]{:S(2)}, u32[]{:S(2)}) %collective-permute-start.5) | collective-permute-done | bytes 69664 | tf_op jit(solution)/shard_map/ppermute | solution.py:54
  28.2 1.6 %collective-permute-start.10 = (bf16[272,128]{1,0:T(8,128)(2,1)S(1)}, bf16[272,128]{1,0:T(8,128)(2,1)S(1)}, u32[]{:S(2)}, u32[]{:S(2)}) collective-permute-start(bf16[272,128]{1,0:T(8,128)(2,1)S(1)} %get-tuple-element.85), channel_id=1, source_target_pairs={{0,16},{8,24},{16,0},{24,8},{1,17},{9,25},{17,1},{25,9},{2,18},{10... | collective-permute-start | bytes 208904 | tf_op jit(solution)/shard_map/ppermute | solution.py:54
  29.8 1.3 %collective-permute-start.11 = (bf16[272,128]{1,0:T(8,128)(2,1)S(1)}, bf16[272,128]{1,0:T(8,128)(2,1)S(1)}, u32[]{:S(2)}, u32[]{:S(2)}) collective-permute-start(bf16[272,128]{1,0:T(8,128)(2,1)S(1)} %get-tuple-element.86), channel_id=1, source_target_pairs={{0,24},{8,16},{16,8},{24,0},{1,25},{9,17},{17,9},{25,1},{2,26},{10... | collective-permute-start | bytes 208904 | tf_op jit(solution)/shard_map/ppermute | solution.py:54
  31.7 1.3 %collective-permute-start.16 = (bf16[768,128]{1,0:T(8,128)(2,1)S(1)}, bf16[768,128]{1,0:T(8,128)(2,1)S(1)}, u32[]{:S(2)}, u32[]{:S(2)}) collective-permute-start(bf16[768,128]{1,0:T(8,128)(2,1)S(1)} %get-tuple-element.88), channel_id=1, source_target_pairs={{0,8},{8,0},{16,24},{24,16},{1,9},{9,1},{17,25},{25,17},{2,10},{10... | collective-permute-start | bytes 589832 | tf_op jit(solution)/shard_map/ppermute | solution.py:54
  33.1 0.9 %collective-permute-start.17 = (bf16[768,128]{1,0:T(8,128)(2,1)S(1)}, bf16[768,128]{1,0:T(8,128)(2,1)S(1)}, u32[]{:S(2)}, u32[]{:S(2)}) collective-permute-start(bf16[768,128]{1,0:T(8,128)(2,1)S(1)} %get-tuple-element.89), channel_id=1, source_target_pairs={{0,16},{8,24},{16,0},{24,8},{1,17},{9,25},{17,1},{25,9},{2,18},{10... | collective-permute-start | bytes 589832 | tf_op jit(solution)/shard_map/ppermute | solution.py:54
  34.0 1.2 %collective-permute-start.18 = (bf16[768,128]{1,0:T(8,128)(2,1)S(1)}, bf16[768,128]{1,0:T(8,128)(2,1)S(1)}, u32[]{:S(2)}, u32[]{:S(2)}) collective-permute-start(bf16[768,128]{1,0:T(8,128)(2,1)S(1)} %get-tuple-element.90), channel_id=1, source_target_pairs={{0,24},{8,16},{16,8},{24,0},{1,25},{9,17},{17,9},{25,1},{2,26},{10... | collective-permute-start | bytes 589832 | tf_op jit(solution)/shard_map/ppermute | solution.py:54
  36.4 0.7 %collective-permute-done.12.refs_4_ = bf16[1,272,128]{2,1,0:T(8,128)(2,1)S(1)} collective-permute-done((bf16[1,272,128]{2,1,0:T(8,128)(2,1)S(1)}, bf16[1,272,128]{2,1,0:T(8,128)(2,1)S(1)}, u32[]{:S(2)}, u32[]{:S(2)}) %collective-permute-start.12) | collective-permute-done | bytes 69664 | tf_op jit(solution)/shard_map/ppermute | solution.py:54
  38.8 8.0 %shard_map.124 = (bf16[512,512]{1,0:T(8,128)(2,1)S(1)}, f32[8,128]{1,0:T(8,128)S(1)}) custom-call(s32[1,128]{1,0:T(1,128)S(1)} %shard_map.119.slot_ref, bf16[1,272,128]{2,1,0:T(8,128)(2,1)S(1)} %bitcast.13, bf16[1,272,128]{2,1,0:T(8,128)(2,1)S(1)} %bitcast.11, bf16[1,272,128]{2,1,0:T(8,128)(2,1)S(1)} %bitcast.7, bf16[1,272,128]{2,1,0:T(8,128)(2,1)S(1)} %bitcast.9, ...), custom_call_target="tpu_custom_call" | custom-call | flops 1 | bytes 1 | tf_op jit(solution)/shard_map/pallas_call | solution.py:358
  48.9 1.1 %shard_map.126 = (bf16[64,512]{1,0:T(8,128)(2,1)S(1)}, bf16[64,512]{1,0:T(8,128)(2,1)S(1)}, bf16[64,512]{1,0:T(8,128)(2,1)S(1)}, bf16[64,512]{1,0:T(8,128)(2,1)S(1)}) custom-call(bf16[512,512]{1,0:T(8,128)(2,1)S(1)} %shard_map.125.mine_ref, bf16[512,512]{1,0:T(8,128)(2,1)S(1)} %collective-permute-done.19.other_ref, f32[8,128]{1,0:T(8,128)S(1)} %get-tuple-element.91.graft_ref), custom_call_target="tpu_custom_call" | custom-call | flops 268435456 | bytes 1 | tf_op jit(solution)/shard_map/pallas_call | solution.py:395
  50.6 4.6 %collective-permute-start.21 = (bf16[64,512]{1,0:T(8,128)(2,1)S(1)}, bf16[64,512]{1,0:T(8,128)(2,1)S(1)}, u32[]{:S(2)}, u32[]{:S(2)}) collective-permute-start(bf16[64,512]{1,0:T(8,128)(2,1)S(1)} %get-tuple-element.94), channel_id=1, source_target_pairs={{0,4},{1,5},{2,6},{3,7},{4,0},{5,1},{6,2},{7,3},{8,12},{9,13},{10,... | collective-permute-start | bytes 196616 | tf_op jit(solution)/shard_map/ppermute | solution.py:54
  55.2 0.8 %collective-permute-start.24 = (bf16[768,128]{1,0:T(8,128)(2,1)S(1)}, bf16[768,128]{1,0:T(8,128)(2,1)S(1)}, u32[]{:S(2)}, u32[]{:S(2)}) collective-permute-start(bf16[768,128]{1,0:T(8,128)(2,1)S(1)} %shard_map.131), channel_id=1, source_target_pairs={{0,16},{8,24},{16,0},{24,8},{1,17},{9,25},{17,1},{25,9},{2,18},{10... | collective-permute-start | bytes 589832 | tf_op jit(solution)/shard_map/ppermute | solution.py:54
  56.8 2.8 %shard_map.128 = (f32[2,512,512]{2,1,0:T(8,128)}, f32[2,512,512]{2,1,0:T(8,128)}, f32[8,128]{1,0:T(8,128)S(1)}) custom-call(f32[2,512,512]{2,1,0:T(8,128)S(1)} %copy-done, f32[2,512,512]{2,1,0:T(8,128)S(1)} %copy-done.1, bf16[64,512]{1,0:T(8,128)(2,1)S(1)} %get-tuple-element.92.after_ref.refs_0_.refs_1_, ...), custom_call_target="tpu_custom_call" | custom-call | flops 1 | bytes 1 | tf_op jit(solution)/shard_map/pallas_call | solution.py:460
  59.6 1.7 %collective-permute-done.22.refs_3_ = bf16[64,512]{1,0:T(8,128)(2,1)S(1)} collective-permute-done((bf16[64,512]{1,0:T(8,128)(2,1)S(1)}, bf16[64,512]{1,0:T(8,128)(2,1)S(1)}, u32[]{:S(2)}, u32[]{:S(2)}) %collective-permute-start.22) | collective-permute-done | bytes 65568 | tf_op jit(solution)/shard_map/ppermute | solution.py:54
  62.7 1.2 %collective-permute-start.27 = (bf16[2,64,512]{2,1,0:T(8,128)(2,1)S(1)}, bf16[2,64,512]{2,1,0:T(8,128)(2,1)S(1)}, u32[]{:S(2)}, u32[]{:S(2)}) collective-permute-start(bf16[2,64,512]{2,1,0:T(8,128)(2,1)S(1)} %shard_map.133.after_ref.refs_0_), channel_id=1, source_target_pairs={{0,16},{8,24},{16,0},{24,8},{1,17},{9,25},{17,1},{25,9},{2,18},{10... | collective-permute-start | bytes 393224 | tf_op jit(solution)/shard_map/ppermute | solution.py:54
  63.9 1.6 %collective-permute-start.28 = (bf16[2,64,512]{2,1,0:T(8,128)(2,1)S(1)}, bf16[2,64,512]{2,1,0:T(8,128)(2,1)S(1)}, u32[]{:S(2)}, u32[]{:S(2)}) collective-permute-start(bf16[2,64,512]{2,1,0:T(8,128)(2,1)S(1)} %shard_map.133.after_ref.refs_0_), channel_id=1, source_target_pairs={{0,24},{8,16},{16,8},{24,0},{1,25},{9,17},{17,9},{25,1},{2,26},{10... | collective-permute-start | bytes 393224 | tf_op jit(solution)/shard_map/ppermute | solution.py:54
  65.5 1.6 %shard_map.134 = (f32[8,64,512]{2,1,0:T(8,128)}, f32[2,8,8192]{2,1,0:T(8,128)}, bf16[2,8,8192]{2,1,0:T(8,128)(2,1)}, f32[8,128]{1,0:T(8,128)S(1)}) custom-call(f32[8,64,512]{2,1,0:T(8,128)S(1)} %copy-done.2, f32[2,8,8192]{2,1,0:T(8,128)S(1)} %copy-done.3, bf16[2,64,512]{2,1,0:T(8,128)(2,1)S(1)} %shard_map.133.after_ref.refs_0_, ...), custom_call_target="tpu_custom_call" | custom-call | flops 1 | bytes 1 | tf_op jit(solution)/shard_map/pallas_call | solution.py:520
  67.6 0.9 %collective-permute-done.27.refs_2_ = bf16[2,64,512]{2,1,0:T(8,128)(2,1)S(1)} collective-permute-done((bf16[2,64,512]{2,1,0:T(8,128)(2,1)S(1)}, bf16[2,64,512]{2,1,0:T(8,128)(2,1)S(1)}, u32[]{:S(2)}, u32[]{:S(2)}) %collective-permute-start.27) | collective-permute-done | bytes 131104 | tf_op jit(solution)/shard_map/ppermute | solution.py:54
  68.5 1.4 %collective-permute-done.28.refs_3_ = bf16[2,64,512]{2,1,0:T(8,128)(2,1)S(1)} collective-permute-done((bf16[2,64,512]{2,1,0:T(8,128)(2,1)S(1)}, bf16[2,64,512]{2,1,0:T(8,128)(2,1)S(1)}, u32[]{:S(2)}, u32[]{:S(2)}) %collective-permute-start.28) | collective-permute-done | bytes 131104 | tf_op jit(solution)/shard_map/ppermute | solution.py:54
  69.9 1.4 %shard_map.135 = bf16[8,64,512]{2,1,0:T(8,128)(2,1)} custom-call(s32[1,128]{1,0:T(1,128)S(1)} %shard_map.119.slot_ref, bf16[2,64,512]{2,1,0:T(8,128)(2,1)S(1)} %shard_map.133.after_ref.refs_0_, bf16[2,64,512]{2,1,0:T(8,128)(2,1)S(1)} %collective-permute-done.26.refs_1_, bf16[2,64,512]{2,1,0:T(8,128)(2,1)S(1)} %collective-permute-done.27.refs_2_, ...), custom_call_target="tpu_custom_call" | custom-call | flops 1 | bytes 1 | tf_op jit(solution)/shard_map/pallas_call | solution.py:549
  (55 shorter events, 10.4 us)
Async XLA Ops:
  0.6 27.6 %collective-permute-start.8 = (f32[2,512,512]{2,1,0:T(8,128)}, f32[2,512,512]{2,1,0:T(8,128)S(1)}, u32[]{:S(2)}, u32[]{:S(2)}) collective-permute-start(f32[2,512,512]{2,1,0:T(8,128)} %right_ref.1), channel_id=1, source_target_pairs={{0,1},{1,0},{2,3},{3,2},{4,5},{5,4},{6,7},{7,6},{8,9},{9,8},{10,11... | collective-permute-start | bytes 6291464 | tf_op jit(solution)/shard_map/ppermute | solution.py:54
  2.4 8.3 %collective-permute-start = (bf16[768,128]{1,0:T(8,128)(2,1)S(1)}, bf16[768,128]{1,0:T(8,128)(2,1)S(1)}, u32[]{:S(2)}, u32[]{:S(2)}) collective-permute-start(bf16[768,128]{1,0:T(8,128)(2,1)S(1)} %get-tuple-element.58), channel_id=1, source_target_pairs={{0,8},{8,0},{16,24},{24,16},{1,9},{9,1},{17,25},{25,17},{2,10},{10... | collective-permute-start | bytes 589832 | tf_op jit(solution)/shard_map/ppermute | solution.py:54
  5.0 11.2 %collective-permute-start.1 = (bf16[768,128]{1,0:T(8,128)(2,1)S(1)}, bf16[768,128]{1,0:T(8,128)(2,1)S(1)}, u32[]{:S(2)}, u32[]{:S(2)}) collective-permute-start(bf16[768,128]{1,0:T(8,128)(2,1)S(1)} %get-tuple-element.59), channel_id=1, source_target_pairs={{0,16},{8,24},{16,0},{24,8},{1,17},{9,25},{17,1},{25,9},{2,18},{10... | collective-permute-start | bytes 589832 | tf_op jit(solution)/shard_map/ppermute | solution.py:54
  6.5 9.7 %collective-permute-start.2 = (bf16[768,128]{1,0:T(8,128)(2,1)S(1)}, bf16[768,128]{1,0:T(8,128)(2,1)S(1)}, u32[]{:S(2)}, u32[]{:S(2)}) collective-permute-start(bf16[768,128]{1,0:T(8,128)(2,1)S(1)} %get-tuple-element.60), channel_id=1, source_target_pairs={{0,24},{8,16},{16,8},{24,0},{1,25},{9,17},{17,9},{25,1},{2,26},{10... | collective-permute-start | bytes 589832 | tf_op jit(solution)/shard_map/ppermute | solution.py:54
  17.1 6.5 %collective-permute-start.3 = (bf16[272,128]{1,0:T(8,128)(2,1)S(1)}, bf16[272,128]{1,0:T(8,128)(2,1)S(1)}, u32[]{:S(2)}, u32[]{:S(2)}) collective-permute-start(bf16[272,128]{1,0:T(8,128)(2,1)S(1)} %get-tuple-element.62), channel_id=1, source_target_pairs={{0,2},{1,3},{2,0},{3,1},{4,6},{5,7},{6,4},{7,5},{8,10},{9,11},{10,... | collective-permute-start | bytes 208904 | tf_op jit(solution)/shard_map/ppermute | solution.py:54
  18.7 7.2 %collective-permute-start.4 = (bf16[272,128]{1,0:T(8,128)(2,1)S(1)}, bf16[272,128]{1,0:T(8,128)(2,1)S(1)}, u32[]{:S(2)}, u32[]{:S(2)}) collective-permute-start(bf16[272,128]{1,0:T(8,128)(2,1)S(1)} %get-tuple-element.63), channel_id=1, source_target_pairs={{0,4},{1,5},{2,6},{3,7},{4,0},{5,1},{6,2},{7,3},{8,12},{9,13},{10,... | collective-permute-start | bytes 208904 | tf_op jit(solution)/shard_map/ppermute | solution.py:54
  21.3 6.1 %collective-permute-start.5 = (bf16[272,128]{1,0:T(8,128)(2,1)S(1)}, bf16[272,128]{1,0:T(8,128)(2,1)S(1)}, u32[]{:S(2)}, u32[]{:S(2)}) collective-permute-start(bf16[272,128]{1,0:T(8,128)(2,1)S(1)} %get-tuple-element.64), channel_id=1, source_target_pairs={{0,6},{1,7},{2,4},{3,5},{4,2},{5,3},{6,0},{7,1},{8,14},{9,15},{10,... | collective-permute-start | bytes 208904 | tf_op jit(solution)/shard_map/ppermute | solution.py:54
  22.3 5.9 %collective-permute-start.6 = (bf16[384,128]{1,0:T(8,128)(2,1)S(1)}, bf16[384,128]{1,0:T(8,128)(2,1)S(1)}, u32[]{:S(2)}, u32[]{:S(2)}) collective-permute-start(bf16[384,128]{1,0:T(8,128)(2,1)S(1)} %get-tuple-element.81.refs_0_), channel_id=1, source_target_pairs={{0,8},{8,0},{16,24},{24,16},{1,9},{9,1},{17,25},{25,17},{2,10},{10... | collective-permute-start | bytes 294920 | tf_op jit(solution)/shard_map/ppermute | solution.py:54
  23.6 4.6 %collective-permute-start.7 = (bf16[384,128]{1,0:T(8,128)(2,1)S(1)}, bf16[384,128]{1,0:T(8,128)(2,1)S(1)}, u32[]{:S(2)}, u32[]{:S(2)}) collective-permute-start(bf16[384,128]{1,0:T(8,128)(2,1)S(1)} %get-tuple-element.82.refs_1_), channel_id=1, source_target_pairs={{0,16},{8,24},{16,0},{24,8},{1,17},{9,25},{17,1},{25,9},{2,18},{10... | collective-permute-start | bytes 294920 | tf_op jit(solution)/shard_map/ppermute | solution.py:54
  28.1 10.7 %copy-start = (f32[2,512,512]{2,1,0:T(8,128)S(1)}, f32[2,512,512]{2,1,0:T(8,128)}, u32[]{:S(2)}) copy-start(f32[2,512,512]{2,1,0:T(8,128)} %left_ref.1) | copy-start | bytes 6291460
  28.2 5.8 %collective-permute-start.10 = (bf16[272,128]{1,0:T(8,128)(2,1)S(1)}, bf16[272,128]{1,0:T(8,128)(2,1)S(1)}, u32[]{:S(2)}, u32[]{:S(2)}) collective-permute-start(bf16[272,128]{1,0:T(8,128)(2,1)S(1)} %get-tuple-element.85), channel_id=1, source_target_pairs={{0,16},{8,24},{16,0},{24,8},{1,17},{9,25},{17,1},{25,9},{2,18},{10... | collective-permute-start | bytes 208904 | tf_op jit(solution)/shard_map/ppermute | solution.py:54
  29.8 6.1 %collective-permute-start.11 = (bf16[272,128]{1,0:T(8,128)(2,1)S(1)}, bf16[272,128]{1,0:T(8,128)(2,1)S(1)}, u32[]{:S(2)}, u32[]{:S(2)}) collective-permute-start(bf16[272,128]{1,0:T(8,128)(2,1)S(1)} %get-tuple-element.86), channel_id=1, source_target_pairs={{0,24},{8,16},{16,8},{24,0},{1,25},{9,17},{17,9},{25,1},{2,26},{10... | collective-permute-start | bytes 208904 | tf_op jit(solution)/shard_map/ppermute | solution.py:54
  31.0 5.3 %collective-permute-start.9 = (bf16[272,128]{1,0:T(8,128)(2,1)S(1)}, bf16[272,128]{1,0:T(8,128)(2,1)S(1)}, u32[]{:S(2)}, u32[]{:S(2)}) collective-permute-start(bf16[272,128]{1,0:T(8,128)(2,1)S(1)} %get-tuple-element.84), channel_id=1, source_target_pairs={{0,8},{8,0},{16,24},{24,16},{1,9},{9,1},{17,25},{25,17},{2,10},{10... | collective-permute-start | bytes 208904 | tf_op jit(solution)/shard_map/ppermute | solution.py:54
  31.7 15.1 %collective-permute-start.16 = (bf16[768,128]{1,0:T(8,128)(2,1)S(1)}, bf16[768,128]{1,0:T(8,128)(2,1)S(1)}, u32[]{:S(2)}, u32[]{:S(2)}) collective-permute-start(bf16[768,128]{1,0:T(8,128)(2,1)S(1)} %get-tuple-element.88), channel_id=1, source_target_pairs={{0,8},{8,0},{16,24},{24,16},{1,9},{9,1},{17,25},{25,17},{2,10},{10... | collective-permute-start | bytes 589832 | tf_op jit(solution)/shard_map/ppermute | solution.py:54
  33.1 13.8 %collective-permute-start.17 = (bf16[768,128]{1,0:T(8,128)(2,1)S(1)}, bf16[768,128]{1,0:T(8,128)(2,1)S(1)}, u32[]{:S(2)}, u32[]{:S(2)}) collective-permute-start(bf16[768,128]{1,0:T(8,128)(2,1)S(1)} %get-tuple-element.89), channel_id=1, source_target_pairs={{0,16},{8,24},{16,0},{24,8},{1,17},{9,25},{17,1},{25,9},{2,18},{10... | collective-permute-start | bytes 589832 | tf_op jit(solution)/shard_map/ppermute | solution.py:54
  34.0 12.9 %collective-permute-start.18 = (bf16[768,128]{1,0:T(8,128)(2,1)S(1)}, bf16[768,128]{1,0:T(8,128)(2,1)S(1)}, u32[]{:S(2)}, u32[]{:S(2)}) collective-permute-start(bf16[768,128]{1,0:T(8,128)(2,1)S(1)} %get-tuple-element.90), channel_id=1, source_target_pairs={{0,24},{8,16},{16,8},{24,0},{1,25},{9,17},{17,9},{25,1},{2,26},{10... | collective-permute-start | bytes 589832 | tf_op jit(solution)/shard_map/ppermute | solution.py:54
  35.9 1.3 %collective-permute-start.12 = (bf16[1,272,128]{2,1,0:T(8,128)(2,1)S(1)}, bf16[1,272,128]{2,1,0:T(8,128)(2,1)S(1)}, u32[]{:S(2)}, u32[]{:S(2)}) collective-permute-start(bf16[1,272,128]{2,1,0:T(8,128)(2,1)S(1)} %bitcast.12), channel_id=1, source_target_pairs={{0,1},{1,0},{2,3},{3,2},{4,5},{5,4},{6,7},{7,6},{8,9},{9,8},{10,11... | collective-permute-start | bytes 208904 | tf_op jit(solution)/shard_map/ppermute | solution.py:54
  36.3 1.3 %collective-permute-start.13 = (bf16[1,272,128]{2,1,0:T(8,128)(2,1)S(1)}, bf16[1,272,128]{2,1,0:T(8,128)(2,1)S(1)}, u32[]{:S(2)}, u32[]{:S(2)}) collective-permute-start(bf16[1,272,128]{2,1,0:T(8,128)(2,1)S(1)} %bitcast.10), channel_id=1, source_target_pairs={{0,1},{1,0},{2,3},{3,2},{4,5},{5,4},{6,7},{7,6},{8,9},{9,8},{10,11... | collective-permute-start | bytes 208904 | tf_op jit(solution)/shard_map/ppermute | solution.py:54
  37.2 1.3 %collective-permute-start.14 = (bf16[1,272,128]{2,1,0:T(8,128)(2,1)S(1)}, bf16[1,272,128]{2,1,0:T(8,128)(2,1)S(1)}, u32[]{:S(2)}, u32[]{:S(2)}) collective-permute-start(bf16[1,272,128]{2,1,0:T(8,128)(2,1)S(1)} %bitcast.6), channel_id=1, source_target_pairs={{0,1},{1,0},{2,3},{3,2},{4,5},{5,4},{6,7},{7,6},{8,9},{9,8},{10,11... | collective-permute-start | bytes 208904 | tf_op jit(solution)/shard_map/ppermute | solution.py:54
  37.6 1.3 %collective-permute-start.15 = (bf16[1,272,128]{2,1,0:T(8,128)(2,1)S(1)}, bf16[1,272,128]{2,1,0:T(8,128)(2,1)S(1)}, u32[]{:S(2)}, u32[]{:S(2)}) collective-permute-start(bf16[1,272,128]{2,1,0:T(8,128)(2,1)S(1)} %bitcast.8), channel_id=1, source_target_pairs={{0,1},{1,0},{2,3},{3,2},{4,5},{5,4},{6,7},{7,6},{8,9},{9,8},{10,11... | collective-permute-start | bytes 208904 | tf_op jit(solution)/shard_map/ppermute | solution.py:54
  46.9 9.9 %copy-start.1 = (f32[2,512,512]{2,1,0:T(8,128)S(1)}, f32[2,512,512]{2,1,0:T(8,128)}, u32[]{:S(2)}) copy-start(f32[2,512,512]{2,1,0:T(8,128)} %right_ref.1) | copy-start | bytes 6291460
  46.9 2.0 %collective-permute-start.19 = (bf16[512,512]{1,0:T(8,128)(2,1)S(1)}, bf16[512,512]{1,0:T(8,128)(2,1)S(1)}, u32[]{:S(2)}, u32[]{:S(2)}) collective-permute-start(bf16[512,512]{1,0:T(8,128)(2,1)S(1)} %shard_map.125.mine_ref), channel_id=1, source_target_pairs={{0,1},{1,0},{2,3},{3,2},{4,5},{5,4},{6,7},{7,6},{8,9},{9,8},{10,11... | collective-permute-start | bytes 1572872 | tf_op jit(solution)/shard_map/ppermute | solution.py:54
  47.8 8.3 %collective-permute-start.23 = (bf16[4,2,256,128]{3,2,1,0:T(8,128)(2,1)S(1)}, bf16[4,2,256,128]{3,2,1,0:T(8,128)(2,1)S(1)}, u32[]{:S(2)}, u32[]{:S(2)}) collective-permute-start(bf16[4,2,256,128]{3,2,1,0:T(8,128)(2,1)S(1)} %get-tuple-element.98), channel_id=1, source_target_pairs={{0,1},{1,0},{2,3},{3,2},{4,5},{5,4},{6,7},{7,6},{8,9},{9,8},{10,11... | collective-permute-start | bytes 1572872 | tf_op jit(solution)/shard_map/ppermute | solution.py:54
  50.0 9.6 %collective-permute-start.20 = (bf16[64,512]{1,0:T(8,128)(2,1)S(1)}, bf16[64,512]{1,0:T(8,128)(2,1)S(1)}, u32[]{:S(2)}, u32[]{:S(2)}) collective-permute-start(bf16[64,512]{1,0:T(8,128)(2,1)S(1)} %get-tuple-element.93), channel_id=1, source_target_pairs={{0,2},{1,3},{2,0},{3,1},{4,6},{5,7},{6,4},{7,5},{8,10},{9,11},{10,... | collective-permute-start | bytes 196616 | tf_op jit(solution)/shard_map/ppermute | solution.py:54
  50.6 8.9 %collective-permute-start.21 = (bf16[64,512]{1,0:T(8,128)(2,1)S(1)}, bf16[64,512]{1,0:T(8,128)(2,1)S(1)}, u32[]{:S(2)}, u32[]{:S(2)}) collective-permute-start(bf16[64,512]{1,0:T(8,128)(2,1)S(1)} %get-tuple-element.94), channel_id=1, source_target_pairs={{0,4},{1,5},{2,6},{3,7},{4,0},{5,1},{6,2},{7,3},{8,12},{9,13},{10,... | collective-permute-start | bytes 196616 | tf_op jit(solution)/shard_map/ppermute | solution.py:54
  55.2 6.1 %collective-permute-start.22 = (bf16[64,512]{1,0:T(8,128)(2,1)S(1)}, bf16[64,512]{1,0:T(8,128)(2,1)S(1)}, u32[]{:S(2)}, u32[]{:S(2)}) collective-permute-start(bf16[64,512]{1,0:T(8,128)(2,1)S(1)} %get-tuple-element.95), channel_id=1, source_target_pairs={{0,6},{1,7},{2,4},{3,5},{4,2},{5,3},{6,0},{7,1},{8,14},{9,15},{10,... | collective-permute-start | bytes 196616 | tf_op jit(solution)/shard_map/ppermute | solution.py:54
  55.2 6.7 %collective-permute-start.24 = (bf16[768,128]{1,0:T(8,128)(2,1)S(1)}, bf16[768,128]{1,0:T(8,128)(2,1)S(1)}, u32[]{:S(2)}, u32[]{:S(2)}) collective-permute-start(bf16[768,128]{1,0:T(8,128)(2,1)S(1)} %shard_map.131), channel_id=1, source_target_pairs={{0,16},{8,24},{16,0},{24,8},{1,17},{9,25},{17,1},{25,9},{2,18},{10... | collective-permute-start | bytes 589832 | tf_op jit(solution)/shard_map/ppermute | solution.py:54
  56.0 5.9 %collective-permute-start.25 = (bf16[768,128]{1,0:T(8,128)(2,1)S(1)}, bf16[768,128]{1,0:T(8,128)(2,1)S(1)}, u32[]{:S(2)}, u32[]{:S(2)}) collective-permute-start(bf16[768,128]{1,0:T(8,128)(2,1)S(1)} %shard_map.132), channel_id=1, source_target_pairs={{0,8},{8,0},{16,24},{24,16},{1,9},{9,1},{17,25},{25,17},{2,10},{10... | collective-permute-start | bytes 589832 | tf_op jit(solution)/shard_map/ppermute | solution.py:54
  61.9 3.6 %copy-start.2 = (f32[8,64,512]{2,1,0:T(8,128)S(1)}, f32[8,64,512]{2,1,0:T(8,128)}, u32[]{:S(2)}) copy-start(f32[8,64,512]{2,1,0:T(8,128)} %accum_ref.1) | copy-start | bytes 3145732
  62.0 5.6 %collective-permute-start.26 = (bf16[2,64,512]{2,1,0:T(8,128)(2,1)S(1)}, bf16[2,64,512]{2,1,0:T(8,128)(2,1)S(1)}, u32[]{:S(2)}, u32[]{:S(2)}) collective-permute-start(bf16[2,64,512]{2,1,0:T(8,128)(2,1)S(1)} %shard_map.133.after_ref.refs_0_), channel_id=1, source_target_pairs={{0,8},{8,0},{16,24},{24,16},{1,9},{9,1},{17,25},{25,17},{2,10},{10... | collective-permute-start | bytes 393224 | tf_op jit(solution)/shard_map/ppermute | solution.py:54
  62.7 5.8 %collective-permute-start.27 = (bf16[2,64,512]{2,1,0:T(8,128)(2,1)S(1)}, bf16[2,64,512]{2,1,0:T(8,128)(2,1)S(1)}, u32[]{:S(2)}, u32[]{:S(2)}) collective-permute-start(bf16[2,64,512]{2,1,0:T(8,128)(2,1)S(1)} %shard_map.133.after_ref.refs_0_), channel_id=1, source_target_pairs={{0,16},{8,24},{16,0},{24,8},{1,17},{9,25},{17,1},{25,9},{2,18},{10... | collective-permute-start | bytes 393224 | tf_op jit(solution)/shard_map/ppermute | solution.py:54
  63.9 6.0 %collective-permute-start.28 = (bf16[2,64,512]{2,1,0:T(8,128)(2,1)S(1)}, bf16[2,64,512]{2,1,0:T(8,128)(2,1)S(1)}, u32[]{:S(2)}, u32[]{:S(2)}) collective-permute-start(bf16[2,64,512]{2,1,0:T(8,128)(2,1)S(1)} %shard_map.133.after_ref.refs_0_), channel_id=1, source_target_pairs={{0,24},{8,16},{16,8},{24,0},{1,25},{9,17},{17,9},{25,1},{2,26},{10... | collective-permute-start | bytes 393224 | tf_op jit(solution)/shard_map/ppermute | solution.py:54
  (1 other events, 3.6 us)

commit v2 on v1

--- a/solution.py
+++ b/solution.py
@@ -34,14 +34,14 @@
     )
 
 
-def dot(left, right):
-    return jnp.dot(left, right, preferred_element_type=F32)
+def dot(left, right, left_axis=1, right_axis=0):
+    return lax.dot_general(
+        left, right, (((left_axis,), (right_axis,)), ((), ())), preferred_element_type=F32
+    )
 
 
 def gram(value, axis):
-    return lax.dot_general(
-        value, value, (((axis,), (axis,)), ((), ())), preferred_element_type=F32
-    )
+    return dot(value, value, axis, axis)
 
 
 def three_terms(value):
@@ -300,7 +300,7 @@
         col = pl.multiple_of((rep_here ^ j) * cols, cols)
         grad[pl.ds(row, rows), pl.ds(col, cols)] = piece.astype(scratch_type)
 
-    swaps = len(mine)
+    swaps, side = len(mine), order // 2
 
     def root_body(slot_ref, *refs):
         mine_refs, other_refs = refs[:swaps], refs[swaps : 2 * swaps]
@@ -319,10 +319,10 @@
 
         graft = jnp.zeros((1, cols), F32)
         for j in range(reps):
-            for swap_refs, side in ((mine_refs, core_here), (other_refs, 1 - core_here)):
+            for swap_refs, which in ((mine_refs, core_here), (other_refs, 1 - core_here)):
                 ref = swap_refs[j // SWAP].at[j % SWAP]
                 for k in range(planes):
-                    assemble(grad, rep_here, plane_here, side,
+                    assemble(grad, rep_here, plane_here, which,
                              ref[k * rows : (k + 1) * rows, :], k, j)
                 bits = ref[planes * rows :, :].astype(F32)
                 graft = graft + jnp.sum(bits[:8], axis=0, keepdims=True)
@@ -334,25 +334,45 @@
         @pl.when(owner == core_here)
         def _():
             value = grad[...].astype(BF16)
-            matrix[...] += gram(value, 1)
+            matrix[:side, :] += dot(value[:side], value, 1, 1)
+            matrix[side:, side:] += gram(value[side:], 1)
             start[...] = value.astype(F32)
 
         @pl.when(owner != core_here)
         def _():
-            matrix[...] += gram(grad[...].astype(BF16), 0)
+            value = grad[...].astype(BF16)
+            matrix[:side, :] += dot(value[:, :side], value, 0, 0)
+            matrix[side:, side:] += gram(value[:, side:], 0)
             line = lax.broadcasted_iota(jnp.int32, square, 0)
             start[...] = (line == lax.broadcasted_iota(jnp.int32, square, 1)).astype(F32)
 
-        scaled = matrix[...]
-        scaled = scaled / jnp.sqrt(jnp.sum(scaled * scaled))
+        upper, corner = matrix[:side, :], matrix[side:, side:]
+        total = jnp.sum(upper[:, :side] * upper[:, :side]) + jnp.sum(corner * corner)
+        total = total + 2.0 * jnp.sum(upper[:, side:] * upper[:, side:])
+        upper, corner = upper / jnp.sqrt(total), corner / jnp.sqrt(total)
         result = start[...]
+
+        def lower(top, last):
+            return jnp.concatenate([top[:, side:].T, last], axis=1)
+
         for iteration in range(ITERS):
-            low = scaled.astype(BF16)
+            top = upper.astype(BF16)
+            bottom = lower(top, corner.astype(BF16))
+            low = jnp.concatenate([top, bottom], axis=0)
             result = 1.25 * result - 0.25 * dot(low, result.astype(BF16))
             if iteration + 1 < ITERS:
-                step = (dot(low, low) * 0.0625 - 0.625 * scaled).astype(BF16)
-                twice = 1.5625 * scaled + dot(low, step)
-                scaled = 1.5625 * twice + dot(twice.astype(BF16), step)
+                step_top = (dot(top, low) * 0.0625 - 0.625 * upper).astype(BF16)
+                step_last = dot(bottom, low[:, side:]) * 0.0625 - 0.625 * corner
+                step = jnp.concatenate(
+                    [step_top, lower(step_top, step_last.astype(BF16))], axis=0
+                )
+                twice_top = 1.5625 * upper + dot(top, step)
+                twice_last = 1.5625 * corner + dot(bottom, step[:, side:])
+                twice_low = twice_top.astype(BF16)
+                upper = 1.5625 * twice_top + dot(twice_low, step)
+                corner = 1.5625 * twice_last + dot(
+                    lower(twice_low, twice_last.astype(BF16)), step[:, side:]
+                )
         out_ref[...] = result.astype(BF16)
 
     root, graft_sum = call(
@@ -365,7 +385,7 @@
             pltpu.VMEM(square, F32),
             pltpu.SemaphoreType.DMA,
         ],
-        flops=1,
+        flops=10**9,
         vmem=20,
     )(book, *mine, *other, left_stats, right_other)
     root = fence([root], *rests_met)[0]
@@ -418,10 +438,10 @@
                 keep_ref[j, m] = held[j, core_here * most + m]
                 give_ref[j, m] = held[j, (1 - core_here) * most + m]
 
-    side = shape((reps, most, piece_rows, cols), BF16)
+    held_shape = shape((reps, most, piece_rows, cols), BF16)
     keep, give = call(
         side_body,
-        [side, side],
+        [held_shape, held_shape],
         [SMEM] + [VMEM] * (2 * reps - 1),
         scratch=[pltpu.VMEM((reps, per, piece_rows, cols), BF16)],
     )(book, whole, *met[1:], *rests_met)

time: 71.5 us -> 70.2 us (0.982)
    pallas_call x1, Pallas kernels: 8 us -> 7.22 us  [on_device(): call(root_body, [shape(square, BF16), shape((8, cols), F32)], [SMEM] + [V...]
  transfers between devices with their start and end apart: 29 -> 29, of which waited for: 16 -> 14; matrix products, arithmetic and copies ran while one was open for 1% -> 1% of each run, Pallas kernels for 26% -> 25%
where the time goes in v2:
time: 70.2 us; the launch traced here: 70 us
  starting transfers between devices  29.7 us (42%)
  waiting for transfers between devices  19.6 us (28%)
  Pallas kernels  18.9 us (27%)
  local copies, waits for them, and re-layouts  0.99 us (1%)
  between operations  0.84 us (1%)
    ppermute x29, starting transfers between devices, exchange(): return lax.ppermute(values, axis, [(i, i ^ mask) for i in range(size)])  29.7 us
    ppermute x29, waiting for transfers between devices, exchange(): return lax.ppermute(values, axis, [(i, i ^ mask) for i in range(size)])  19.6 us
    pallas_call x1, Pallas kernels, on_device(): call(root_body, [shape(square, BF16), shape((8, cols), F32)], [SMEM] + [V...  7.22 us
    pallas_call x1, Pallas kernels, on_device(): pl.pallas_call(stats_body, grid=(most,), out_shape=[shape(left_stats.shap...  2.78 us
    pallas_call x1, Pallas kernels, on_device(): call(accum_body, [shape(graft_accum.shape, F32), shape(vocab_accum.shape,...  1.56 us
  transfers between devices with their start and end apart: 29, of which 14 were waited for; matrix products, arithmetic and copies ran while one was open for 1% of the time, Pallas kernels for 25%

profile of v2, /device:TPU:0, one launch (start us, length us, event | category | flops | bytes accessed | tf_op | source)
XLA Modules:
  0.0 70.0 jit_solution(15275651896030822305)
XLA Ops:
  1.1 1.3 %shard_map.118 = (bf16[768,128]{1,0:T(8,128)(2,1)S(1)}, bf16[768,128]{1,0:T(8,128)(2,1)S(1)}, bf16[768,128]{1,0:T(8,128)(2,1)S(1)}, bf16[768,128]{1,0:T(8,128)(2,1)S(1)}, s32[1,128]{1,0:T(1,128)S(1)}) custom-call(s32[8]{0:T(128)} %slot_ref.1, bf16[8,64,512]{2,1,0:T(8,128)(2,1)} %bitcast.14, bf16[2,8,8192]{2,1,0:T(8,128)(2,1)} %bitcast.15), custom_call_target="tpu_custom_call" | custom-call | flops 1 | bytes 1 | tf_op jit(solution)/shard_map/pallas_call | solution.py:160
  2.4 2.6 %collective-permute-start = (bf16[768,128]{1,0:T(8,128)(2,1)S(1)}, bf16[768,128]{1,0:T(8,128)(2,1)S(1)}, u32[]{:S(2)}, u32[]{:S(2)}) collective-permute-start(bf16[768,128]{1,0:T(8,128)(2,1)S(1)} %get-tuple-element.58), channel_id=1, source_target_pairs={{0,8},{8,0},{16,24},{24,16},{1,9},{9,1},{17,25},{25,17},{2,10},{10... | collective-permute-start | bytes 589832 | tf_op jit(solution)/shard_map/ppermute | solution.py:54
  5.0 1.5 %collective-permute-start.1 = (bf16[768,128]{1,0:T(8,128)(2,1)S(1)}, bf16[768,128]{1,0:T(8,128)(2,1)S(1)}, u32[]{:S(2)}, u32[]{:S(2)}) collective-permute-start(bf16[768,128]{1,0:T(8,128)(2,1)S(1)} %get-tuple-element.59), channel_id=1, source_target_pairs={{0,16},{8,24},{16,0},{24,8},{1,17},{9,25},{17,1},{25,9},{2,18},{10... | collective-permute-start | bytes 589832 | tf_op jit(solution)/shard_map/ppermute | solution.py:54
  6.5 1.0 %constant_dynamic-slice_fusion.refs_4_ = f32[8,64,128]{2,1,0:T(8,128)S(1)} fusion(f32[8,64,512]{2,1,0:T(8,128)} %accum_ref.1, s32[]{:T(128)S(6)} %select_n.3), kind=kLoop, calls=%fused_computation.2 | loop fusion | bytes 524292 | tf_op jit(solution)/shard_map/dynamic_slice | solution.py:168
  7.5 3.2 %collective-permute-done.refs_1_ = bf16[768,128]{1,0:T(8,128)(2,1)S(1)} collective-permute-done((bf16[768,128]{1,0:T(8,128)(2,1)S(1)}, bf16[768,128]{1,0:T(8,128)(2,1)S(1)}, u32[]{:S(2)}, u32[]{:S(2)}) %collective-permute-start) | collective-permute-done | bytes 196640 | tf_op jit(solution)/shard_map/ppermute | solution.py:54
  10.7 5.5 %collective-permute-done.1.refs_2_ = bf16[768,128]{1,0:T(8,128)(2,1)S(1)} collective-permute-done((bf16[768,128]{1,0:T(8,128)(2,1)S(1)}, bf16[768,128]{1,0:T(8,128)(2,1)S(1)}, u32[]{:S(2)}, u32[]{:S(2)}) %collective-permute-start.1) | collective-permute-done | bytes 196640 | tf_op jit(solution)/shard_map/ppermute | solution.py:54
  16.2 0.8 %shard_map.120 = (bf16[384,128]{1,0:T(8,128)(2,1)S(1)}, bf16[384,128]{1,0:T(8,128)(2,1)S(1)}, bf16[272,128]{1,0:T(8,128)(2,1)S(1)}, bf16[272,128]{1,0:T(8,128)(2...) custom-call(s32[1,128]{1,0:T(1,128)S(1)} %get-tuple-element.56.slot_ref, ...), custom_call_target="tpu_custom_call" | custom-call | flops 1 | bytes 1 | tf_op jit(solution)/shard_map/pallas_call | solution.py:221
  17.1 1.6 %collective-permute-start.3 = (bf16[272,128]{1,0:T(8,128)(2,1)S(1)}, bf16[272,128]{1,0:T(8,128)(2,1)S(1)}, u32[]{:S(2)}, u32[]{:S(2)}) collective-permute-start(bf16[272,128]{1,0:T(8,128)(2,1)S(1)} %get-tuple-element.62), channel_id=1, source_target_pairs={{0,2},{1,3},{2,0},{3,1},{4,6},{5,7},{6,4},{7,5},{8,10},{9,11},{10,... | collective-permute-start | bytes 208904 | tf_op jit(solution)/shard_map/ppermute | solution.py:54
  18.7 2.6 %collective-permute-start.4 = (bf16[272,128]{1,0:T(8,128)(2,1)S(1)}, bf16[272,128]{1,0:T(8,128)(2,1)S(1)}, u32[]{:S(2)}, u32[]{:S(2)}) collective-permute-start(bf16[272,128]{1,0:T(8,128)(2,1)S(1)} %get-tuple-element.63), channel_id=1, source_target_pairs={{0,4},{1,5},{2,6},{3,7},{4,0},{5,1},{6,2},{7,3},{8,12},{9,13},{10,... | collective-permute-start | bytes 208904 | tf_op jit(solution)/shard_map/ppermute | solution.py:54
  22.3 1.3 %collective-permute-start.6 = (bf16[384,128]{1,0:T(8,128)(2,1)S(1)}, bf16[384,128]{1,0:T(8,128)(2,1)S(1)}, u32[]{:S(2)}, u32[]{:S(2)}) collective-permute-start(bf16[384,128]{1,0:T(8,128)(2,1)S(1)} %get-tuple-element.81.refs_0_), channel_id=1, source_target_pairs={{0,8},{8,0},{16,24},{24,16},{1,9},{9,1},{17,25},{25,17},{2,10},{10... | collective-permute-start | bytes 294920 | tf_op jit(solution)/shard_map/ppermute | solution.py:54
  23.6 0.8 %collective-permute-start.7 = (bf16[384,128]{1,0:T(8,128)(2,1)S(1)}, bf16[384,128]{1,0:T(8,128)(2,1)S(1)}, u32[]{:S(2)}, u32[]{:S(2)}) collective-permute-start(bf16[384,128]{1,0:T(8,128)(2,1)S(1)} %get-tuple-element.82.refs_1_), channel_id=1, source_target_pairs={{0,16},{8,24},{16,0},{24,8},{1,17},{9,25},{17,1},{25,9},{2,18},{10... | collective-permute-start | bytes 294920 | tf_op jit(solution)/shard_map/ppermute | solution.py:54
  24.4 1.5 %collective-permute-done.4.refs_2_ = bf16[272,128]{1,0:T(8,128)(2,1)S(1)} collective-permute-done((bf16[272,128]{1,0:T(8,128)(2,1)S(1)}, bf16[272,128]{1,0:T(8,128)(2,1)S(1)}, u32[]{:S(2)}, u32[]{:S(2)}) %collective-permute-start.4) | collective-permute-done | bytes 69664 | tf_op jit(solution)/shard_map/ppermute | solution.py:54
  25.9 1.5 %collective-permute-done.5.refs_3_ = bf16[272,128]{1,0:T(8,128)(2,1)S(1)} collective-permute-done((bf16[272,128]{1,0:T(8,128)(2,1)S(1)}, bf16[272,128]{1,0:T(8,128)(2,1)S(1)}, u32[]{:S(2)}, u32[]{:S(2)}) %collective-permute-start.5) | collective-permute-done | bytes 69664 | tf_op jit(solution)/shard_map/ppermute | solution.py:54
  28.2 1.4 %collective-permute-start.9 = (bf16[272,128]{1,0:T(8,128)(2,1)S(1)}, bf16[272,128]{1,0:T(8,128)(2,1)S(1)}, u32[]{:S(2)}, u32[]{:S(2)}) collective-permute-start(bf16[272,128]{1,0:T(8,128)(2,1)S(1)} %get-tuple-element.84), channel_id=1, source_target_pairs={{0,8},{8,0},{16,24},{24,16},{1,9},{9,1},{17,25},{25,17},{2,10},{10... | collective-permute-start | bytes 208904 | tf_op jit(solution)/shard_map/ppermute | solution.py:54
  29.6 0.9 %collective-permute-start.10 = (bf16[272,128]{1,0:T(8,128)(2,1)S(1)}, bf16[272,128]{1,0:T(8,128)(2,1)S(1)}, u32[]{:S(2)}, u32[]{:S(2)}) collective-permute-start(bf16[272,128]{1,0:T(8,128)(2,1)S(1)} %get-tuple-element.85), channel_id=1, source_target_pairs={{0,16},{8,24},{16,0},{24,8},{1,17},{9,25},{17,1},{25,9},{2,18},{10... | collective-permute-start | bytes 208904 | tf_op jit(solution)/shard_map/ppermute | solution.py:54
  30.5 1.2 %collective-permute-start.11 = (bf16[272,128]{1,0:T(8,128)(2,1)S(1)}, bf16[272,128]{1,0:T(8,128)(2,1)S(1)}, u32[]{:S(2)}, u32[]{:S(2)}) collective-permute-start(bf16[272,128]{1,0:T(8,128)(2,1)S(1)} %get-tuple-element.86), channel_id=1, source_target_pairs={{0,24},{8,16},{16,8},{24,0},{1,25},{9,17},{17,9},{25,1},{2,26},{10... | collective-permute-start | bytes 208904 | tf_op jit(solution)/shard_map/ppermute | solution.py:54
  32.6 1.3 %collective-permute-start.16 = (bf16[768,128]{1,0:T(8,128)(2,1)S(1)}, bf16[768,128]{1,0:T(8,128)(2,1)S(1)}, u32[]{:S(2)}, u32[]{:S(2)}) collective-permute-start(bf16[768,128]{1,0:T(8,128)(2,1)S(1)} %get-tuple-element.88), channel_id=1, source_target_pairs={{0,8},{8,0},{16,24},{24,16},{1,9},{9,1},{17,25},{25,17},{2,10},{10... | collective-permute-start | bytes 589832 | tf_op jit(solution)/shard_map/ppermute | solution.py:54
  33.9 0.9 %collective-permute-start.17 = (bf16[768,128]{1,0:T(8,128)(2,1)S(1)}, bf16[768,128]{1,0:T(8,128)(2,1)S(1)}, u32[]{:S(2)}, u32[]{:S(2)}) collective-permute-start(bf16[768,128]{1,0:T(8,128)(2,1)S(1)} %get-tuple-element.89), channel_id=1, source_target_pairs={{0,16},{8,24},{16,0},{24,8},{1,17},{9,25},{17,1},{25,9},{2,18},{10... | collective-permute-start | bytes 589832 | tf_op jit(solution)/shard_map/ppermute | solution.py:54
  34.8 0.9 %collective-permute-done.11.refs_2_ = bf16[272,128]{1,0:T(8,128)(2,1)S(1)} collective-permute-done((bf16[272,128]{1,0:T(8,128)(2,1)S(1)}, bf16[272,128]{1,0:T(8,128)(2,1)S(1)}, u32[]{:S(2)}, u32[]{:S(2)}) %collective-permute-start.11) | collective-permute-done | bytes 69664 | tf_op jit(solution)/shard_map/ppermute | solution.py:54
  35.7 1.2 %collective-permute-start.18 = (bf16[768,128]{1,0:T(8,128)(2,1)S(1)}, bf16[768,128]{1,0:T(8,128)(2,1)S(1)}, u32[]{:S(2)}, u32[]{:S(2)}) collective-permute-start(bf16[768,128]{1,0:T(8,128)(2,1)S(1)} %get-tuple-element.90), channel_id=1, source_target_pairs={{0,24},{8,16},{16,8},{24,0},{1,25},{9,17},{17,9},{25,1},{2,26},{10... | collective-permute-start | bytes 589832 | tf_op jit(solution)/shard_map/ppermute | solution.py:54
  38.4 7.2 %shard_map.124 = (bf16[512,512]{1,0:T(8,128)(2,1)S(1)}, f32[8,128]{1,0:T(8,128)S(1)}) custom-call(s32[1,128]{1,0:T(1,128)S(1)} %shard_map.119.slot_ref, bf16[1,272,128]{2,1,0:T(8,128)(2,1)S(1)} %bitcast.13, bf16[1,272,128]{2,1,0:T(8,128)(2,1)S(1)} %bitcast.7, bf16[1,272,128]{2,1,0:T(8,128)(2,1)S(1)} %bitcast.9, bf16[1,272,128]{2,1,0:T(8,128)(2,1)S(1)} %bitcast.11, ...), custom_call_target="tpu_custom_call" | custom-call | flops 1000000000 | bytes 1 | tf_op jit(solution)/shard_map/pallas_call | solution.py:378
  47.7 1.1 %shard_map.126 = (bf16[64,512]{1,0:T(8,128)(2,1)S(1)}, bf16[64,512]{1,0:T(8,128)(2,1)S(1)}, bf16[64,512]{1,0:T(8,128)(2,1)S(1)}, bf16[64,512]{1,0:T(8,128)(2,1)S(1)}) custom-call(bf16[512,512]{1,0:T(8,128)(2,1)S(1)} %shard_map.125.mine_ref, bf16[512,512]{1,0:T(8,128)(2,1)S(1)} %collective-permute-done.19.other_ref, f32[8,128]{1,0:T(8,128)S(1)} %get-tuple-element.91.graft_ref), custom_call_target="tpu_custom_call" | custom-call | flops 268435456 | bytes 1 | tf_op jit(solution)/shard_map/pallas_call | solution.py:415
  49.4 3.5 %collective-permute-start.21 = (bf16[64,512]{1,0:T(8,128)(2,1)S(1)}, bf16[64,512]{1,0:T(8,128)(2,1)S(1)}, u32[]{:S(2)}, u32[]{:S(2)}) collective-permute-start(bf16[64,512]{1,0:T(8,128)(2,1)S(1)} %get-tuple-element.94), channel_id=1, source_target_pairs={{0,4},{1,5},{2,6},{3,7},{4,0},{5,1},{6,2},{7,3},{8,12},{9,13},{10,... | collective-permute-start | bytes 196616 | tf_op jit(solution)/shard_map/ppermute | solution.py:54
  53.2 1.6 %collective-permute-start.24 = (bf16[768,128]{1,0:T(8,128)(2,1)S(1)}, bf16[768,128]{1,0:T(8,128)(2,1)S(1)}, u32[]{:S(2)}, u32[]{:S(2)}) collective-permute-start(bf16[768,128]{1,0:T(8,128)(2,1)S(1)} %shard_map.131), channel_id=1, source_target_pairs={{0,16},{8,24},{16,0},{24,8},{1,17},{9,25},{17,1},{25,9},{2,18},{10... | collective-permute-start | bytes 589832 | tf_op jit(solution)/shard_map/ppermute | solution.py:54
  55.5 2.8 %shard_map.128 = (f32[2,512,512]{2,1,0:T(8,128)}, f32[2,512,512]{2,1,0:T(8,128)}, f32[8,128]{1,0:T(8,128)S(1)}) custom-call(f32[2,512,512]{2,1,0:T(8,128)S(1)} %copy-done, f32[2,512,512]{2,1,0:T(8,128)S(1)} %copy-done.1, bf16[64,512]{1,0:T(8,128)(2,1)S(1)} %get-tuple-element.92.after_ref.refs_0_.refs_1_, ...), custom_call_target="tpu_custom_call" | custom-call | flops 1 | bytes 1 | tf_op jit(solution)/shard_map/pallas_call | solution.py:480
  59.7 1.2 %collective-permute-done.25.refs_2_.refs_5_ = bf16[768,128]{1,0:T(8,128)(2,1)S(1)} collective-permute-done((bf16[768,128]{1,0:T(8,128)(2,1)S(1)}, bf16[768,128]{1,0:T(8,128)(2,1)S(1)}, u32[]{:S(2)}, u32[]{:S(2)}) %collective-permute-start.25) | collective-permute-done | bytes 196640 | tf_op jit(solution)/shard_map/ppermute | solution.py:54
  61.6 1.1 %collective-permute-start.27 = (bf16[2,64,512]{2,1,0:T(8,128)(2,1)S(1)}, bf16[2,64,512]{2,1,0:T(8,128)(2,1)S(1)}, u32[]{:S(2)}, u32[]{:S(2)}) collective-permute-start(bf16[2,64,512]{2,1,0:T(8,128)(2,1)S(1)} %shard_map.133.after_ref.refs_0_), channel_id=1, source_target_pairs={{0,16},{8,24},{16,0},{24,8},{1,17},{9,25},{17,1},{25,9},{2,18},{10... | collective-permute-start | bytes 393224 | tf_op jit(solution)/shard_map/ppermute | solution.py:54
  62.7 1.6 %collective-permute-start.28 = (bf16[2,64,512]{2,1,0:T(8,128)(2,1)S(1)}, bf16[2,64,512]{2,1,0:T(8,128)(2,1)S(1)}, u32[]{:S(2)}, u32[]{:S(2)}) collective-permute-start(bf16[2,64,512]{2,1,0:T(8,128)(2,1)S(1)} %shard_map.133.after_ref.refs_0_), channel_id=1, source_target_pairs={{0,24},{8,16},{16,8},{24,0},{1,25},{9,17},{17,9},{25,1},{2,26},{10... | collective-permute-start | bytes 393224 | tf_op jit(solution)/shard_map/ppermute | solution.py:54
  64.4 1.6 %shard_map.134 = (f32[8,64,512]{2,1,0:T(8,128)}, f32[2,8,8192]{2,1,0:T(8,128)}, bf16[2,8,8192]{2,1,0:T(8,128)(2,1)}, f32[8,128]{1,0:T(8,128)S(1)}) custom-call(f32[8,64,512]{2,1,0:T(8,128)S(1)} %copy-done.2, f32[2,8,8192]{2,1,0:T(8,128)S(1)} %copy-done.3, bf16[2,64,512]{2,1,0:T(8,128)(2,1)S(1)} %shard_map.133.after_ref.refs_0_, ...), custom_call_target="tpu_custom_call" | custom-call | flops 1 | bytes 1 | tf_op jit(solution)/shard_map/pallas_call | solution.py:540
  66.2 1.0 %collective-permute-done.27.refs_2_ = bf16[2,64,512]{2,1,0:T(8,128)(2,1)S(1)} collective-permute-done((bf16[2,64,512]{2,1,0:T(8,128)(2,1)S(1)}, bf16[2,64,512]{2,1,0:T(8,128)(2,1)S(1)}, u32[]{:S(2)}, u32[]{:S(2)}) %collective-permute-start.27) | collective-permute-done | bytes 131104 | tf_op jit(solution)/shard_map/ppermute | solution.py:54
  67.2 1.4 %collective-permute-done.28.refs_3_ = bf16[2,64,512]{2,1,0:T(8,128)(2,1)S(1)} collective-permute-done((bf16[2,64,512]{2,1,0:T(8,128)(2,1)S(1)}, bf16[2,64,512]{2,1,0:T(8,128)(2,1)S(1)}, u32[]{:S(2)}, u32[]{:S(2)}) %collective-permute-start.28) | collective-permute-done | bytes 131104 | tf_op jit(solution)/shard_map/ppermute | solution.py:54
  68.6 1.4 %shard_map.135 = bf16[8,64,512]{2,1,0:T(8,128)(2,1)} custom-call(s32[1,128]{1,0:T(1,128)S(1)} %shard_map.119.slot_ref, bf16[2,64,512]{2,1,0:T(8,128)(2,1)S(1)} %shard_map.133.after_ref.refs_0_, bf16[2,64,512]{2,1,0:T(8,128)(2,1)S(1)} %collective-permute-done.26.refs_1_, bf16[2,64,512]{2,1,0:T(8,128)(2,1)S(1)} %collective-permute-done.27.refs_2_, ...), custom_call_target="tpu_custom_call" | custom-call | flops 1 | bytes 1 | tf_op jit(solution)/shard_map/pallas_call | solution.py:569
  (55 shorter events, 10.6 us)
Async XLA Ops:
  0.6 27.5 %collective-permute-start.8 = (f32[2,512,512]{2,1,0:T(8,128)}, f32[2,512,512]{2,1,0:T(8,128)S(1)}, u32[]{:S(2)}, u32[]{:S(2)}) collective-permute-start(f32[2,512,512]{2,1,0:T(8,128)} %right_ref.1), channel_id=1, source_target_pairs={{0,1},{1,0},{2,3},{3,2},{4,5},{5,4},{6,7},{7,6},{8,9},{9,8},{10,11... | collective-permute-start | bytes 6291464 | tf_op jit(solution)/shard_map/ppermute | solution.py:54
  2.4 8.3 %collective-permute-start = (bf16[768,128]{1,0:T(8,128)(2,1)S(1)}, bf16[768,128]{1,0:T(8,128)(2,1)S(1)}, u32[]{:S(2)}, u32[]{:S(2)}) collective-permute-start(bf16[768,128]{1,0:T(8,128)(2,1)S(1)} %get-tuple-element.58), channel_id=1, source_target_pairs={{0,8},{8,0},{16,24},{24,16},{1,9},{9,1},{17,25},{25,17},{2,10},{10... | collective-permute-start | bytes 589832 | tf_op jit(solution)/shard_map/ppermute | solution.py:54
  5.0 11.2 %collective-permute-start.1 = (bf16[768,128]{1,0:T(8,128)(2,1)S(1)}, bf16[768,128]{1,0:T(8,128)(2,1)S(1)}, u32[]{:S(2)}, u32[]{:S(2)}) collective-permute-start(bf16[768,128]{1,0:T(8,128)(2,1)S(1)} %get-tuple-element.59), channel_id=1, source_target_pairs={{0,16},{8,24},{16,0},{24,8},{1,17},{9,25},{17,1},{25,9},{2,18},{10... | collective-permute-start | bytes 589832 | tf_op jit(solution)/shard_map/ppermute | solution.py:54
  6.5 9.7 %collective-permute-start.2 = (bf16[768,128]{1,0:T(8,128)(2,1)S(1)}, bf16[768,128]{1,0:T(8,128)(2,1)S(1)}, u32[]{:S(2)}, u32[]{:S(2)}) collective-permute-start(bf16[768,128]{1,0:T(8,128)(2,1)S(1)} %get-tuple-element.60), channel_id=1, source_target_pairs={{0,24},{8,16},{16,8},{24,0},{1,25},{9,17},{17,9},{25,1},{2,26},{10... | collective-permute-start | bytes 589832 | tf_op jit(solution)/shard_map/ppermute | solution.py:54
  17.1 6.5 %collective-permute-start.3 = (bf16[272,128]{1,0:T(8,128)(2,1)S(1)}, bf16[272,128]{1,0:T(8,128)(2,1)S(1)}, u32[]{:S(2)}, u32[]{:S(2)}) collective-permute-start(bf16[272,128]{1,0:T(8,128)(2,1)S(1)} %get-tuple-element.62), channel_id=1, source_target_pairs={{0,2},{1,3},{2,0},{3,1},{4,6},{5,7},{6,4},{7,5},{8,10},{9,11},{10,... | collective-permute-start | bytes 208904 | tf_op jit(solution)/shard_map/ppermute | solution.py:54
  18.7 7.2 %collective-permute-start.4 = (bf16[272,128]{1,0:T(8,128)(2,1)S(1)}, bf16[272,128]{1,0:T(8,128)(2,1)S(1)}, u32[]{:S(2)}, u32[]{:S(2)}) collective-permute-start(bf16[272,128]{1,0:T(8,128)(2,1)S(1)} %get-tuple-element.63), channel_id=1, source_target_pairs={{0,4},{1,5},{2,6},{3,7},{4,0},{5,1},{6,2},{7,3},{8,12},{9,13},{10,... | collective-permute-start | bytes 208904 | tf_op jit(solution)/shard_map/ppermute | solution.py:54
  21.3 6.1 %collective-permute-start.5 = (bf16[272,128]{1,0:T(8,128)(2,1)S(1)}, bf16[272,128]{1,0:T(8,128)(2,1)S(1)}, u32[]{:S(2)}, u32[]{:S(2)}) collective-permute-start(bf16[272,128]{1,0:T(8,128)(2,1)S(1)} %get-tuple-element.64), channel_id=1, source_target_pairs={{0,6},{1,7},{2,4},{3,5},{4,2},{5,3},{6,0},{7,1},{8,14},{9,15},{10,... | collective-permute-start | bytes 208904 | tf_op jit(solution)/shard_map/ppermute | solution.py:54
  22.3 5.9 %collective-permute-start.6 = (bf16[384,128]{1,0:T(8,128)(2,1)S(1)}, bf16[384,128]{1,0:T(8,128)(2,1)S(1)}, u32[]{:S(2)}, u32[]{:S(2)}) collective-permute-start(bf16[384,128]{1,0:T(8,128)(2,1)S(1)} %get-tuple-element.81.refs_0_), channel_id=1, source_target_pairs={{0,8},{8,0},{16,24},{24,16},{1,9},{9,1},{17,25},{25,17},{2,10},{10... | collective-permute-start | bytes 294920 | tf_op jit(solution)/shard_map/ppermute | solution.py:54
  23.6 4.6 %collective-permute-start.7 = (bf16[384,128]{1,0:T(8,128)(2,1)S(1)}, bf16[384,128]{1,0:T(8,128)(2,1)S(1)}, u32[]{:S(2)}, u32[]{:S(2)}) collective-permute-start(bf16[384,128]{1,0:T(8,128)(2,1)S(1)} %get-tuple-element.82.refs_1_), channel_id=1, source_target_pairs={{0,16},{8,24},{16,0},{24,8},{1,17},{9,25},{17,1},{25,9},{2,18},{10... | collective-permute-start | bytes 294920 | tf_op jit(solution)/shard_map/ppermute | solution.py:54
  28.1 10.2 %copy-start = (f32[2,512,512]{2,1,0:T(8,128)S(1)}, f32[2,512,512]{2,1,0:T(8,128)}, u32[]{:S(2)}) copy-start(f32[2,512,512]{2,1,0:T(8,128)} %left_ref.1) | copy-start | bytes 6291460
  28.2 4.4 %collective-permute-start.9 = (bf16[272,128]{1,0:T(8,128)(2,1)S(1)}, bf16[272,128]{1,0:T(8,128)(2,1)S(1)}, u32[]{:S(2)}, u32[]{:S(2)}) collective-permute-start(bf16[272,128]{1,0:T(8,128)(2,1)S(1)} %get-tuple-element.84), channel_id=1, source_target_pairs={{0,8},{8,0},{16,24},{24,16},{1,9},{9,1},{17,25},{25,17},{2,10},{10... | collective-permute-start | bytes 208904 | tf_op jit(solution)/shard_map/ppermute | solution.py:54
  29.6 4.3 %collective-permute-start.10 = (bf16[272,128]{1,0:T(8,128)(2,1)S(1)}, bf16[272,128]{1,0:T(8,128)(2,1)S(1)}, u32[]{:S(2)}, u32[]{:S(2)}) collective-permute-start(bf16[272,128]{1,0:T(8,128)(2,1)S(1)} %get-tuple-element.85), channel_id=1, source_target_pairs={{0,16},{8,24},{16,0},{24,8},{1,17},{9,25},{17,1},{25,9},{2,18},{10... | collective-permute-start | bytes 208904 | tf_op jit(solution)/shard_map/ppermute | solution.py:54
  30.5 5.2 %collective-permute-start.11 = (bf16[272,128]{1,0:T(8,128)(2,1)S(1)}, bf16[272,128]{1,0:T(8,128)(2,1)S(1)}, u32[]{:S(2)}, u32[]{:S(2)}) collective-permute-start(bf16[272,128]{1,0:T(8,128)(2,1)S(1)} %get-tuple-element.86), channel_id=1, source_target_pairs={{0,24},{8,16},{16,8},{24,0},{1,25},{9,17},{17,9},{25,1},{2,26},{10... | collective-permute-start | bytes 208904 | tf_op jit(solution)/shard_map/ppermute | solution.py:54
  31.7 5.2 %collective-permute-start.12 = (bf16[1,272,128]{2,1,0:T(8,128)(2,1)S(1)}, bf16[1,272,128]{2,1,0:T(8,128)(2,1)S(1)}, u32[]{:S(2)}, u32[]{:S(2)}) collective-permute-start(bf16[1,272,128]{2,1,0:T(8,128)(2,1)S(1)} %bitcast.12), channel_id=1, source_target_pairs={{0,1},{1,0},{2,3},{3,2},{4,5},{5,4},{6,7},{7,6},{8,9},{9,8},{10,11... | collective-permute-start | bytes 208904 | tf_op jit(solution)/shard_map/ppermute | solution.py:54
  32.6 4.4 %collective-permute-start.13 = (bf16[1,272,128]{2,1,0:T(8,128)(2,1)S(1)}, bf16[1,272,128]{2,1,0:T(8,128)(2,1)S(1)}, u32[]{:S(2)}, u32[]{:S(2)}) collective-permute-start(bf16[1,272,128]{2,1,0:T(8,128)(2,1)S(1)} %bitcast.6), channel_id=1, source_target_pairs={{0,1},{1,0},{2,3},{3,2},{4,5},{5,4},{6,7},{7,6},{8,9},{9,8},{10,11... | collective-permute-start | bytes 208904 | tf_op jit(solution)/shard_map/ppermute | solution.py:54
  32.6 13.0 %collective-permute-start.16 = (bf16[768,128]{1,0:T(8,128)(2,1)S(1)}, bf16[768,128]{1,0:T(8,128)(2,1)S(1)}, u32[]{:S(2)}, u32[]{:S(2)}) collective-permute-start(bf16[768,128]{1,0:T(8,128)(2,1)S(1)} %get-tuple-element.88), channel_id=1, source_target_pairs={{0,8},{8,0},{16,24},{24,16},{1,9},{9,1},{17,25},{25,17},{2,10},{10... | collective-permute-start | bytes 589832 | tf_op jit(solution)/shard_map/ppermute | solution.py:54
  33.9 11.7 %collective-permute-start.17 = (bf16[768,128]{1,0:T(8,128)(2,1)S(1)}, bf16[768,128]{1,0:T(8,128)(2,1)S(1)}, u32[]{:S(2)}, u32[]{:S(2)}) collective-permute-start(bf16[768,128]{1,0:T(8,128)(2,1)S(1)} %get-tuple-element.89), channel_id=1, source_target_pairs={{0,16},{8,24},{16,0},{24,8},{1,17},{9,25},{17,1},{25,9},{2,18},{10... | collective-permute-start | bytes 589832 | tf_op jit(solution)/shard_map/ppermute | solution.py:54
  35.7 9.9 %collective-permute-start.18 = (bf16[768,128]{1,0:T(8,128)(2,1)S(1)}, bf16[768,128]{1,0:T(8,128)(2,1)S(1)}, u32[]{:S(2)}, u32[]{:S(2)}) collective-permute-start(bf16[768,128]{1,0:T(8,128)(2,1)S(1)} %get-tuple-element.90), channel_id=1, source_target_pairs={{0,24},{8,16},{16,8},{24,0},{1,25},{9,17},{17,9},{25,1},{2,26},{10... | collective-permute-start | bytes 589832 | tf_op jit(solution)/shard_map/ppermute | solution.py:54
  36.9 1.3 %collective-permute-start.14 = (bf16[1,272,128]{2,1,0:T(8,128)(2,1)S(1)}, bf16[1,272,128]{2,1,0:T(8,128)(2,1)S(1)}, u32[]{:S(2)}, u32[]{:S(2)}) collective-permute-start(bf16[1,272,128]{2,1,0:T(8,128)(2,1)S(1)} %bitcast.8), channel_id=1, source_target_pairs={{0,1},{1,0},{2,3},{3,2},{4,5},{5,4},{6,7},{7,6},{8,9},{9,8},{10,11... | collective-permute-start | bytes 208904 | tf_op jit(solution)/shard_map/ppermute | solution.py:54
  37.0 1.4 %collective-permute-start.15 = (bf16[1,272,128]{2,1,0:T(8,128)(2,1)S(1)}, bf16[1,272,128]{2,1,0:T(8,128)(2,1)S(1)}, u32[]{:S(2)}, u32[]{:S(2)}) collective-permute-start(bf16[1,272,128]{2,1,0:T(8,128)(2,1)S(1)} %bitcast.10), channel_id=1, source_target_pairs={{0,1},{1,0},{2,3},{3,2},{4,5},{5,4},{6,7},{7,6},{8,9},{9,8},{10,11... | collective-permute-start | bytes 208904 | tf_op jit(solution)/shard_map/ppermute | solution.py:54
  45.6 9.9 %copy-start.1 = (f32[2,512,512]{2,1,0:T(8,128)S(1)}, f32[2,512,512]{2,1,0:T(8,128)}, u32[]{:S(2)}) copy-start(f32[2,512,512]{2,1,0:T(8,128)} %right_ref.1) | copy-start | bytes 6291460
  45.7 2.0 %collective-permute-start.19 = (bf16[512,512]{1,0:T(8,128)(2,1)S(1)}, bf16[512,512]{1,0:T(8,128)(2,1)S(1)}, u32[]{:S(2)}, u32[]{:S(2)}) collective-permute-start(bf16[512,512]{1,0:T(8,128)(2,1)S(1)} %shard_map.125.mine_ref), channel_id=1, source_target_pairs={{0,1},{1,0},{2,3},{3,2},{4,5},{5,4},{6,7},{7,6},{8,9},{9,8},{10,11... | collective-permute-start | bytes 1572872 | tf_op jit(solution)/shard_map/ppermute | solution.py:54
  46.8 8.0 %collective-permute-start.23 = (bf16[4,2,256,128]{3,2,1,0:T(8,128)(2,1)S(1)}, bf16[4,2,256,128]{3,2,1,0:T(8,128)(2,1)S(1)}, u32[]{:S(2)}, u32[]{:S(2)}) collective-permute-start(bf16[4,2,256,128]{3,2,1,0:T(8,128)(2,1)S(1)} %get-tuple-element.98), channel_id=1, source_target_pairs={{0,1},{1,0},{2,3},{3,2},{4,5},{5,4},{6,7},{7,6},{8,9},{9,8},{10,11... | collective-permute-start | bytes 1572872 | tf_op jit(solution)/shard_map/ppermute | solution.py:54
  48.7 9.6 %collective-permute-start.20 = (bf16[64,512]{1,0:T(8,128)(2,1)S(1)}, bf16[64,512]{1,0:T(8,128)(2,1)S(1)}, u32[]{:S(2)}, u32[]{:S(2)}) collective-permute-start(bf16[64,512]{1,0:T(8,128)(2,1)S(1)} %get-tuple-element.93), channel_id=1, source_target_pairs={{0,2},{1,3},{2,0},{3,1},{4,6},{5,7},{6,4},{7,5},{8,10},{9,11},{10,... | collective-permute-start | bytes 196616 | tf_op jit(solution)/shard_map/ppermute | solution.py:54
  49.4 8.9 %collective-permute-start.21 = (bf16[64,512]{1,0:T(8,128)(2,1)S(1)}, bf16[64,512]{1,0:T(8,128)(2,1)S(1)}, u32[]{:S(2)}, u32[]{:S(2)}) collective-permute-start(bf16[64,512]{1,0:T(8,128)(2,1)S(1)} %get-tuple-element.94), channel_id=1, source_target_pairs={{0,4},{1,5},{2,6},{3,7},{4,0},{5,1},{6,2},{7,3},{8,12},{9,13},{10,... | collective-permute-start | bytes 196616 | tf_op jit(solution)/shard_map/ppermute | solution.py:54
  52.9 6.1 %collective-permute-start.22 = (bf16[64,512]{1,0:T(8,128)(2,1)S(1)}, bf16[64,512]{1,0:T(8,128)(2,1)S(1)}, u32[]{:S(2)}, u32[]{:S(2)}) collective-permute-start(bf16[64,512]{1,0:T(8,128)(2,1)S(1)} %get-tuple-element.95), channel_id=1, source_target_pairs={{0,6},{1,7},{2,4},{3,5},{4,2},{5,3},{6,0},{7,1},{8,14},{9,15},{10,... | collective-permute-start | bytes 196616 | tf_op jit(solution)/shard_map/ppermute | solution.py:54
  53.2 6.4 %collective-permute-start.24 = (bf16[768,128]{1,0:T(8,128)(2,1)S(1)}, bf16[768,128]{1,0:T(8,128)(2,1)S(1)}, u32[]{:S(2)}, u32[]{:S(2)}) collective-permute-start(bf16[768,128]{1,0:T(8,128)(2,1)S(1)} %shard_map.131), channel_id=1, source_target_pairs={{0,16},{8,24},{16,0},{24,8},{1,17},{9,25},{17,1},{25,9},{2,18},{10... | collective-permute-start | bytes 589832 | tf_op jit(solution)/shard_map/ppermute | solution.py:54
  54.8 6.0 %collective-permute-start.25 = (bf16[768,128]{1,0:T(8,128)(2,1)S(1)}, bf16[768,128]{1,0:T(8,128)(2,1)S(1)}, u32[]{:S(2)}, u32[]{:S(2)}) collective-permute-start(bf16[768,128]{1,0:T(8,128)(2,1)S(1)} %shard_map.132), channel_id=1, source_target_pairs={{0,8},{8,0},{16,24},{24,16},{1,9},{9,1},{17,25},{25,17},{2,10},{10... | collective-permute-start | bytes 589832 | tf_op jit(solution)/shard_map/ppermute | solution.py:54
  59.6 4.7 %copy-start.2 = (f32[8,64,512]{2,1,0:T(8,128)S(1)}, f32[8,64,512]{2,1,0:T(8,128)}, u32[]{:S(2)}) copy-start(f32[8,64,512]{2,1,0:T(8,128)} %accum_ref.1) | copy-start | bytes 3145732
  60.9 5.4 %collective-permute-start.26 = (bf16[2,64,512]{2,1,0:T(8,128)(2,1)S(1)}, bf16[2,64,512]{2,1,0:T(8,128)(2,1)S(1)}, u32[]{:S(2)}, u32[]{:S(2)}) collective-permute-start(bf16[2,64,512]{2,1,0:T(8,128)(2,1)S(1)} %shard_map.133.after_ref.refs_0_), channel_id=1, source_target_pairs={{0,8},{8,0},{16,24},{24,16},{1,9},{9,1},{17,25},{25,17},{2,10},{10... | collective-permute-start | bytes 393224 | tf_op jit(solution)/shard_map/ppermute | solution.py:54
  61.6 5.6 %collective-permute-start.27 = (bf16[2,64,512]{2,1,0:T(8,128)(2,1)S(1)}, bf16[2,64,512]{2,1,0:T(8,128)(2,1)S(1)}, u32[]{:S(2)}, u32[]{:S(2)}) collective-permute-start(bf16[2,64,512]{2,1,0:T(8,128)(2,1)S(1)} %shard_map.133.after_ref.refs_0_), channel_id=1, source_target_pairs={{0,16},{8,24},{16,0},{24,8},{1,17},{9,25},{17,1},{25,9},{2,18},{10... | collective-permute-start | bytes 393224 | tf_op jit(solution)/shard_map/ppermute | solution.py:54
  62.7 5.9 %collective-permute-start.28 = (bf16[2,64,512]{2,1,0:T(8,128)(2,1)S(1)}, bf16[2,64,512]{2,1,0:T(8,128)(2,1)S(1)}, u32[]{:S(2)}, u32[]{:S(2)}) collective-permute-start(bf16[2,64,512]{2,1,0:T(8,128)(2,1)S(1)} %shard_map.133.after_ref.refs_0_), channel_id=1, source_target_pairs={{0,24},{8,16},{16,8},{24,0},{1,25},{9,17},{17,9},{25,1},{2,26},{10... | collective-permute-start | bytes 393224 | tf_op jit(solution)/shard_map/ppermute | solution.py:54
  (1 other events, 4.7 us)

commit v3 on v2

--- a/solution.py
+++ b/solution.py
@@ -446,6 +446,7 @@
         scratch=[pltpu.VMEM((reps, per, piece_rows, cols), BF16)],
     )(book, whole, *met[1:], *rests_met)
     other_side = exchange(give, "fsdp", 1, indices)
+    slabs = fence(slabs, other_side)
 
     returned = [slabs[0]] + [
         exchange(slabs[k], "fsdp", 2 * k, indices) for k in plane_partners
@@ -504,7 +505,7 @@
         shape((share, rows, order), BF16),
         [SMEM] + [VMEM] * planes + [ANY],
     )(book, *returned, stats_token)
-    picked = fence(fence([picked], flops=LONG), *share_lasts)[0]
+    picked = fence([picked], flops=10**8)[0]
     gathered = [picked] + [exchange(picked, "rep", j, reps) for j in rep_partners]
 
     def accum_body(accum_ref, vocab_ref, after_ref, *refs):

time: 70.2 us -> 69.6 us (level)
  transfers between devices with their start and end apart: 29 -> 29, of which waited for: 14 -> 13; matrix products, arithmetic and copies ran while one was open for 1% -> 1% of each run, Pallas kernels for 25% -> 25%
where the time goes in v3:
time: 69.6 us; the launch traced here: 69.4 us
  starting transfers between devices  29.7 us (43%)
  waiting for transfers between devices  19.1 us (27%)
  Pallas kernels  18.9 us (27%)
  local copies, waits for them, and re-layouts  0.98 us (1%)
  between operations  0.82 us (1%)
    ppermute x29, starting transfers between devices, exchange(): return lax.ppermute(values, axis, [(i, i ^ mask) for i in range(size)])  29.7 us
    ppermute x29, waiting for transfers between devices, exchange(): return lax.ppermute(values, axis, [(i, i ^ mask) for i in range(size)])  19.1 us
    pallas_call x1, Pallas kernels, on_device(): call(root_body, [shape(square, BF16), shape((8, cols), F32)], [SMEM] + [V...  7.2 us
    pallas_call x1, Pallas kernels, on_device(): pl.pallas_call(stats_body, grid=(most,), out_shape=[shape(left_stats.shap...  2.82 us
    pallas_call x1, Pallas kernels, on_device(): call(accum_body, [shape(graft_accum.shape, F32), shape(vocab_accum.shape,...  1.57 us
    pallas_call x1, Pallas kernels, on_device(): call(place_body, shape((blocks, rows, order), BF16), [SMEM] + [VMEM] * re...  1.4 us
  transfers between devices with their start and end apart: 29, of which 13 were waited for; matrix products, arithmetic and copies ran while one was open for 1% of the time, Pallas kernels for 25%

profile of v3, /device:TPU:0, one launch (start us, length us, event | category | flops | bytes accessed | tf_op | source)
XLA Modules:
  0.0 69.4 jit_solution(1715693660036292699)
XLA Ops:
  1.1 1.3 %shard_map.118 = (bf16[768,128]{1,0:T(8,128)(2,1)S(1)}, bf16[768,128]{1,0:T(8,128)(2,1)S(1)}, bf16[768,128]{1,0:T(8,128)(2,1)S(1)}, bf16[768,128]{1,0:T(8,128)(2,1)S(1)}, s32[1,128]{1,0:T(1,128)S(1)}) custom-call(s32[8]{0:T(128)} %slot_ref.1, bf16[8,64,512]{2,1,0:T(8,128)(2,1)} %bitcast.14, bf16[2,8,8192]{2,1,0:T(8,128)(2,1)} %bitcast.15), custom_call_target="tpu_custom_call" | custom-call | flops 1 | bytes 1 | tf_op jit(solution)/shard_map/pallas_call | solution.py:160
  2.4 2.6 %collective-permute-start = (bf16[768,128]{1,0:T(8,128)(2,1)S(1)}, bf16[768,128]{1,0:T(8,128)(2,1)S(1)}, u32[]{:S(2)}, u32[]{:S(2)}) collective-permute-start(bf16[768,128]{1,0:T(8,128)(2,1)S(1)} %get-tuple-element.62), channel_id=1, source_target_pairs={{0,8},{8,0},{16,24},{24,16},{1,9},{9,1},{17,25},{25,17},{2,10},{10... | collective-permute-start | bytes 589832 | tf_op jit(solution)/shard_map/ppermute | solution.py:54
  5.0 1.5 %collective-permute-start.1 = (bf16[768,128]{1,0:T(8,128)(2,1)S(1)}, bf16[768,128]{1,0:T(8,128)(2,1)S(1)}, u32[]{:S(2)}, u32[]{:S(2)}) collective-permute-start(bf16[768,128]{1,0:T(8,128)(2,1)S(1)} %get-tuple-element.63), channel_id=1, source_target_pairs={{0,16},{8,24},{16,0},{24,8},{1,17},{9,25},{17,1},{25,9},{2,18},{10... | collective-permute-start | bytes 589832 | tf_op jit(solution)/shard_map/ppermute | solution.py:54
  6.5 1.0 %constant_dynamic-slice_fusion.refs_4_ = f32[8,64,128]{2,1,0:T(8,128)S(1)} fusion(f32[8,64,512]{2,1,0:T(8,128)} %accum_ref.1, s32[]{:T(128)S(6)} %select_n.3), kind=kLoop, calls=%fused_computation.2 | loop fusion | bytes 524292 | tf_op jit(solution)/shard_map/dynamic_slice | solution.py:168
  7.5 3.2 %collective-permute-done.refs_1_ = bf16[768,128]{1,0:T(8,128)(2,1)S(1)} collective-permute-done((bf16[768,128]{1,0:T(8,128)(2,1)S(1)}, bf16[768,128]{1,0:T(8,128)(2,1)S(1)}, u32[]{:S(2)}, u32[]{:S(2)}) %collective-permute-start) | collective-permute-done | bytes 196640 | tf_op jit(solution)/shard_map/ppermute | solution.py:54
  10.7 5.5 %collective-permute-done.1.refs_2_ = bf16[768,128]{1,0:T(8,128)(2,1)S(1)} collective-permute-done((bf16[768,128]{1,0:T(8,128)(2,1)S(1)}, bf16[768,128]{1,0:T(8,128)(2,1)S(1)}, u32[]{:S(2)}, u32[]{:S(2)}) %collective-permute-start.1) | collective-permute-done | bytes 196640 | tf_op jit(solution)/shard_map/ppermute | solution.py:54
  16.2 0.8 %shard_map.120 = (bf16[384,128]{1,0:T(8,128)(2,1)S(1)}, bf16[384,128]{1,0:T(8,128)(2,1)S(1)}, bf16[272,128]{1,0:T(8,128)(2,1)S(1)}, bf16[272,128]{1,0:T(8,128)(2...) custom-call(s32[1,128]{1,0:T(1,128)S(1)} %get-tuple-element.60.slot_ref, ...), custom_call_target="tpu_custom_call" | custom-call | flops 1 | bytes 1 | tf_op jit(solution)/shard_map/pallas_call | solution.py:221
  17.1 1.6 %collective-permute-start.3 = (bf16[272,128]{1,0:T(8,128)(2,1)S(1)}, bf16[272,128]{1,0:T(8,128)(2,1)S(1)}, u32[]{:S(2)}, u32[]{:S(2)}) collective-permute-start(bf16[272,128]{1,0:T(8,128)(2,1)S(1)} %get-tuple-element.66), channel_id=1, source_target_pairs={{0,2},{1,3},{2,0},{3,1},{4,6},{5,7},{6,4},{7,5},{8,10},{9,11},{10,... | collective-permute-start | bytes 208904 | tf_op jit(solution)/shard_map/ppermute | solution.py:54
  18.7 2.6 %collective-permute-start.4 = (bf16[272,128]{1,0:T(8,128)(2,1)S(1)}, bf16[272,128]{1,0:T(8,128)(2,1)S(1)}, u32[]{:S(2)}, u32[]{:S(2)}) collective-permute-start(bf16[272,128]{1,0:T(8,128)(2,1)S(1)} %get-tuple-element.67), channel_id=1, source_target_pairs={{0,4},{1,5},{2,6},{3,7},{4,0},{5,1},{6,2},{7,3},{8,12},{9,13},{10,... | collective-permute-start | bytes 208904 | tf_op jit(solution)/shard_map/ppermute | solution.py:54
  22.3 1.3 %collective-permute-start.6 = (bf16[384,128]{1,0:T(8,128)(2,1)S(1)}, bf16[384,128]{1,0:T(8,128)(2,1)S(1)}, u32[]{:S(2)}, u32[]{:S(2)}) collective-permute-start(bf16[384,128]{1,0:T(8,128)(2,1)S(1)} %get-tuple-element.85.refs_0_), channel_id=1, source_target_pairs={{0,8},{8,0},{16,24},{24,16},{1,9},{9,1},{17,25},{25,17},{2,10},{10... | collective-permute-start | bytes 294920 | tf_op jit(solution)/shard_map/ppermute | solution.py:54
  23.6 0.8 %collective-permute-start.7 = (bf16[384,128]{1,0:T(8,128)(2,1)S(1)}, bf16[384,128]{1,0:T(8,128)(2,1)S(1)}, u32[]{:S(2)}, u32[]{:S(2)}) collective-permute-start(bf16[384,128]{1,0:T(8,128)(2,1)S(1)} %get-tuple-element.86.refs_1_), channel_id=1, source_target_pairs={{0,16},{8,24},{16,0},{24,8},{1,17},{9,25},{17,1},{25,9},{2,18},{10... | collective-permute-start | bytes 294920 | tf_op jit(solution)/shard_map/ppermute | solution.py:54
  24.4 1.5 %collective-permute-done.4.refs_2_ = bf16[272,128]{1,0:T(8,128)(2,1)S(1)} collective-permute-done((bf16[272,128]{1,0:T(8,128)(2,1)S(1)}, bf16[272,128]{1,0:T(8,128)(2,1)S(1)}, u32[]{:S(2)}, u32[]{:S(2)}) %collective-permute-start.4) | collective-permute-done | bytes 69664 | tf_op jit(solution)/shard_map/ppermute | solution.py:54
  25.9 1.5 %collective-permute-done.5.refs_3_ = bf16[272,128]{1,0:T(8,128)(2,1)S(1)} collective-permute-done((bf16[272,128]{1,0:T(8,128)(2,1)S(1)}, bf16[272,128]{1,0:T(8,128)(2,1)S(1)}, u32[]{:S(2)}, u32[]{:S(2)}) %collective-permute-start.5) | collective-permute-done | bytes 69664 | tf_op jit(solution)/shard_map/ppermute | solution.py:54
  28.2 1.4 %collective-permute-start.9 = (bf16[272,128]{1,0:T(8,128)(2,1)S(1)}, bf16[272,128]{1,0:T(8,128)(2,1)S(1)}, u32[]{:S(2)}, u32[]{:S(2)}) collective-permute-start(bf16[272,128]{1,0:T(8,128)(2,1)S(1)} %get-tuple-element.88), channel_id=1, source_target_pairs={{0,8},{8,0},{16,24},{24,16},{1,9},{9,1},{17,25},{25,17},{2,10},{10... | collective-permute-start | bytes 208904 | tf_op jit(solution)/shard_map/ppermute | solution.py:54
  29.6 0.9 %collective-permute-start.10 = (bf16[272,128]{1,0:T(8,128)(2,1)S(1)}, bf16[272,128]{1,0:T(8,128)(2,1)S(1)}, u32[]{:S(2)}, u32[]{:S(2)}) collective-permute-start(bf16[272,128]{1,0:T(8,128)(2,1)S(1)} %get-tuple-element.89), channel_id=1, source_target_pairs={{0,16},{8,24},{16,0},{24,8},{1,17},{9,25},{17,1},{25,9},{2,18},{10... | collective-permute-start | bytes 208904 | tf_op jit(solution)/shard_map/ppermute | solution.py:54
  30.5 1.2 %collective-permute-start.11 = (bf16[272,128]{1,0:T(8,128)(2,1)S(1)}, bf16[272,128]{1,0:T(8,128)(2,1)S(1)}, u32[]{:S(2)}, u32[]{:S(2)}) collective-permute-start(bf16[272,128]{1,0:T(8,128)(2,1)S(1)} %get-tuple-element.90), channel_id=1, source_target_pairs={{0,24},{8,16},{16,8},{24,0},{1,25},{9,17},{17,9},{25,1},{2,26},{10... | collective-permute-start | bytes 208904 | tf_op jit(solution)/shard_map/ppermute | solution.py:54
  32.6 1.3 %collective-permute-start.16 = (bf16[768,128]{1,0:T(8,128)(2,1)S(1)}, bf16[768,128]{1,0:T(8,128)(2,1)S(1)}, u32[]{:S(2)}, u32[]{:S(2)}) collective-permute-start(bf16[768,128]{1,0:T(8,128)(2,1)S(1)} %get-tuple-element.92), channel_id=1, source_target_pairs={{0,8},{8,0},{16,24},{24,16},{1,9},{9,1},{17,25},{25,17},{2,10},{10... | collective-permute-start | bytes 589832 | tf_op jit(solution)/shard_map/ppermute | solution.py:54
  33.9 0.9 %collective-permute-start.17 = (bf16[768,128]{1,0:T(8,128)(2,1)S(1)}, bf16[768,128]{1,0:T(8,128)(2,1)S(1)}, u32[]{:S(2)}, u32[]{:S(2)}) collective-permute-start(bf16[768,128]{1,0:T(8,128)(2,1)S(1)} %get-tuple-element.93), channel_id=1, source_target_pairs={{0,16},{8,24},{16,0},{24,8},{1,17},{9,25},{17,1},{25,9},{2,18},{10... | collective-permute-start | bytes 589832 | tf_op jit(solution)/shard_map/ppermute | solution.py:54
  34.8 0.9 %collective-permute-done.11.refs_2_ = bf16[272,128]{1,0:T(8,128)(2,1)S(1)} collective-permute-done((bf16[272,128]{1,0:T(8,128)(2,1)S(1)}, bf16[272,128]{1,0:T(8,128)(2,1)S(1)}, u32[]{:S(2)}, u32[]{:S(2)}) %collective-permute-start.11) | collective-permute-done | bytes 69664 | tf_op jit(solution)/shard_map/ppermute | solution.py:54
  35.7 1.2 %collective-permute-start.18 = (bf16[768,128]{1,0:T(8,128)(2,1)S(1)}, bf16[768,128]{1,0:T(8,128)(2,1)S(1)}, u32[]{:S(2)}, u32[]{:S(2)}) collective-permute-start(bf16[768,128]{1,0:T(8,128)(2,1)S(1)} %get-tuple-element.94), channel_id=1, source_target_pairs={{0,24},{8,16},{16,8},{24,0},{1,25},{9,17},{17,9},{25,1},{2,26},{10... | collective-permute-start | bytes 589832 | tf_op jit(solution)/shard_map/ppermute | solution.py:54
  38.4 7.2 %shard_map.124 = (bf16[512,512]{1,0:T(8,128)(2,1)S(1)}, f32[8,128]{1,0:T(8,128)S(1)}) custom-call(s32[1,128]{1,0:T(1,128)S(1)} %shard_map.119.slot_ref, bf16[1,272,128]{2,1,0:T(8,128)(2,1)S(1)} %bitcast.13, bf16[1,272,128]{2,1,0:T(8,128)(2,1)S(1)} %bitcast.7, bf16[1,272,128]{2,1,0:T(8,128)(2,1)S(1)} %bitcast.9, bf16[1,272,128]{2,1,0:T(8,128)(2,1)S(1)} %bitcast.11, ...), custom_call_target="tpu_custom_call" | custom-call | flops 1000000000 | bytes 1 | tf_op jit(solution)/shard_map/pallas_call | solution.py:378
  47.7 1.1 %shard_map.126 = (bf16[64,512]{1,0:T(8,128)(2,1)S(1)}, bf16[64,512]{1,0:T(8,128)(2,1)S(1)}, bf16[64,512]{1,0:T(8,128)(2,1)S(1)}, bf16[64,512]{1,0:T(8,128)(2,1)S(1)}) custom-call(bf16[512,512]{1,0:T(8,128)(2,1)S(1)} %shard_map.125.mine_ref, bf16[512,512]{1,0:T(8,128)(2,1)S(1)} %collective-permute-done.19.other_ref, f32[8,128]{1,0:T(8,128)S(1)} %get-tuple-element.95.graft_ref), custom_call_target="tpu_custom_call" | custom-call | flops 268435456 | bytes 1 | tf_op jit(solution)/shard_map/pallas_call | solution.py:415
  49.4 3.5 %collective-permute-start.22 = (bf16[64,512]{1,0:T(8,128)(2,1)S(1)}, bf16[64,512]{1,0:T(8,128)(2,1)S(1)}, u32[]{:S(2)}, u32[]{:S(2)}) collective-permute-start(bf16[64,512]{1,0:T(8,128)(2,1)S(1)} %get-tuple-element.104), channel_id=1, source_target_pairs={{0,4},{1,5},{2,6},{3,7},{4,0},{5,1},{6,2},{7,3},{8,12},{9,13},{10,... | collective-permute-start | bytes 196616 | tf_op jit(solution)/shard_map/ppermute | solution.py:54
  53.2 1.6 %collective-permute-start.27 = (bf16[768,128]{1,0:T(8,128)(2,1)S(1)}, bf16[768,128]{1,0:T(8,128)(2,1)S(1)}, u32[]{:S(2)}, u32[]{:S(2)}) collective-permute-start(bf16[768,128]{1,0:T(8,128)(2,1)S(1)} %shard_map.132), channel_id=1, source_target_pairs={{0,16},{8,24},{16,0},{24,8},{1,17},{9,25},{17,1},{25,9},{2,18},{10... | collective-permute-start | bytes 589832 | tf_op jit(solution)/shard_map/ppermute | solution.py:54
  55.5 2.8 %shard_map.129 = (f32[2,512,512]{2,1,0:T(8,128)}, f32[2,512,512]{2,1,0:T(8,128)}, f32[8,128]{1,0:T(8,128)S(1)}) custom-call(f32[2,512,512]{2,1,0:T(8,128)S(1)} %copy-done, f32[2,512,512]{2,1,0:T(8,128)S(1)} %copy-done.1, bf16[64,512]{1,0:T(8,128)(2,1)S(1)} %get-tuple-element.102.after_ref.refs_0_.refs_1_, ...), custom_call_target="tpu_custom_call" | custom-call | flops 1 | bytes 1 | tf_op jit(solution)/shard_map/pallas_call | solution.py:481
  59.6 0.9 %collective-permute-start.24 = (bf16[2,64,512]{2,1,0:T(8,128)(2,1)S(1)}, bf16[2,64,512]{2,1,0:T(8,128)(2,1)S(1)}, u32[]{:S(2)}, u32[]{:S(2)}) collective-permute-start(bf16[2,64,512]{2,1,0:T(8,128)(2,1)S(1)} %shard_map.131.after_ref.refs_0_), channel_id=1, source_target_pairs={{0,8},{8,0},{16,24},{24,16},{1,9},{9,1},{17,25},{25,17},{2,10},{10... | collective-permute-start | bytes 393224 | tf_op jit(solution)/shard_map/ppermute | solution.py:54
  60.5 1.5 %collective-permute-start.25 = (bf16[2,64,512]{2,1,0:T(8,128)(2,1)S(1)}, bf16[2,64,512]{2,1,0:T(8,128)(2,1)S(1)}, u32[]{:S(2)}, u32[]{:S(2)}) collective-permute-start(bf16[2,64,512]{2,1,0:T(8,128)(2,1)S(1)} %shard_map.131.after_ref.refs_0_), channel_id=1, source_target_pairs={{0,16},{8,24},{16,0},{24,8},{1,17},{9,25},{17,1},{25,9},{2,18},{10... | collective-permute-start | bytes 393224 | tf_op jit(solution)/shard_map/ppermute | solution.py:54
  62.0 1.2 %collective-permute-start.26 = (bf16[2,64,512]{2,1,0:T(8,128)(2,1)S(1)}, bf16[2,64,512]{2,1,0:T(8,128)(2,1)S(1)}, u32[]{:S(2)}, u32[]{:S(2)}) collective-permute-start(bf16[2,64,512]{2,1,0:T(8,128)(2,1)S(1)} %shard_map.131.after_ref.refs_0_), channel_id=1, source_target_pairs={{0,24},{8,16},{16,8},{24,0},{1,25},{9,17},{17,9},{25,1},{2,26},{10... | collective-permute-start | bytes 393224 | tf_op jit(solution)/shard_map/ppermute | solution.py:54
  63.2 1.6 %shard_map.134 = (f32[8,64,512]{2,1,0:T(8,128)}, f32[2,8,8192]{2,1,0:T(8,128)}, bf16[2,8,8192]{2,1,0:T(8,128)(2,1)}, f32[8,128]{1,0:T(8,128)S(1)}) custom-call(f32[8,64,512]{2,1,0:T(8,128)S(1)} %copy-done.2, f32[2,8,8192]{2,1,0:T(8,128)S(1)} %copy-done.3, bf16[2,64,512]{2,1,0:T(8,128)(2,1)S(1)} %shard_map.131.after_ref.refs_0_, ...), custom_call_target="tpu_custom_call" | custom-call | flops 1 | bytes 1 | tf_op jit(solution)/shard_map/pallas_call | solution.py:541
  64.8 0.8 %collective-permute-done.24.refs_1_ = bf16[2,64,512]{2,1,0:T(8,128)(2,1)S(1)} collective-permute-done((bf16[2,64,512]{2,1,0:T(8,128)(2,1)S(1)}, bf16[2,64,512]{2,1,0:T(8,128)(2,1)S(1)}, u32[]{:S(2)}, u32[]{:S(2)}) %collective-permute-start.24) | collective-permute-done | bytes 131104 | tf_op jit(solution)/shard_map/ppermute | solution.py:54
  65.6 2.4 %collective-permute-done.25.refs_2_ = bf16[2,64,512]{2,1,0:T(8,128)(2,1)S(1)} collective-permute-done((bf16[2,64,512]{2,1,0:T(8,128)(2,1)S(1)}, bf16[2,64,512]{2,1,0:T(8,128)(2,1)S(1)}, u32[]{:S(2)}, u32[]{:S(2)}) %collective-permute-start.25) | collective-permute-done | bytes 131104 | tf_op jit(solution)/shard_map/ppermute | solution.py:54
  68.0 1.4 %shard_map.135 = bf16[8,64,512]{2,1,0:T(8,128)(2,1)} custom-call(s32[1,128]{1,0:T(1,128)S(1)} %shard_map.119.slot_ref, bf16[2,64,512]{2,1,0:T(8,128)(2,1)S(1)} %shard_map.131.after_ref.refs_0_, bf16[2,64,512]{2,1,0:T(8,128)(2,1)S(1)} %collective-permute-done.24.refs_1_, bf16[2,64,512]{2,1,0:T(8,128)(2,1)S(1)} %collective-permute-done.25.refs_2_, ...), custom_call_target="tpu_custom_call" | custom-call | flops 1 | bytes 1 | tf_op jit(solution)/shard_map/pallas_call | solution.py:570
  (55 shorter events, 9.6 us)
Async XLA Ops:
  0.6 27.6 %collective-permute-start.8 = (f32[2,512,512]{2,1,0:T(8,128)}, f32[2,512,512]{2,1,0:T(8,128)S(1)}, u32[]{:S(2)}, u32[]{:S(2)}) collective-permute-start(f32[2,512,512]{2,1,0:T(8,128)} %right_ref.1), channel_id=1, source_target_pairs={{0,1},{1,0},{2,3},{3,2},{4,5},{5,4},{6,7},{7,6},{8,9},{9,8},{10,11... | collective-permute-start | bytes 6291464 | tf_op jit(solution)/shard_map/ppermute | solution.py:54
  2.4 8.3 %collective-permute-start = (bf16[768,128]{1,0:T(8,128)(2,1)S(1)}, bf16[768,128]{1,0:T(8,128)(2,1)S(1)}, u32[]{:S(2)}, u32[]{:S(2)}) collective-permute-start(bf16[768,128]{1,0:T(8,128)(2,1)S(1)} %get-tuple-element.62), channel_id=1, source_target_pairs={{0,8},{8,0},{16,24},{24,16},{1,9},{9,1},{17,25},{25,17},{2,10},{10... | collective-permute-start | bytes 589832 | tf_op jit(solution)/shard_map/ppermute | solution.py:54
  5.0 11.2 %collective-permute-start.1 = (bf16[768,128]{1,0:T(8,128)(2,1)S(1)}, bf16[768,128]{1,0:T(8,128)(2,1)S(1)}, u32[]{:S(2)}, u32[]{:S(2)}) collective-permute-start(bf16[768,128]{1,0:T(8,128)(2,1)S(1)} %get-tuple-element.63), channel_id=1, source_target_pairs={{0,16},{8,24},{16,0},{24,8},{1,17},{9,25},{17,1},{25,9},{2,18},{10... | collective-permute-start | bytes 589832 | tf_op jit(solution)/shard_map/ppermute | solution.py:54
  6.5 9.7 %collective-permute-start.2 = (bf16[768,128]{1,0:T(8,128)(2,1)S(1)}, bf16[768,128]{1,0:T(8,128)(2,1)S(1)}, u32[]{:S(2)}, u32[]{:S(2)}) collective-permute-start(bf16[768,128]{1,0:T(8,128)(2,1)S(1)} %get-tuple-element.64), channel_id=1, source_target_pairs={{0,24},{8,16},{16,8},{24,0},{1,25},{9,17},{17,9},{25,1},{2,26},{10... | collective-permute-start | bytes 589832 | tf_op jit(solution)/shard_map/ppermute | solution.py:54
  17.1 6.5 %collective-permute-start.3 = (bf16[272,128]{1,0:T(8,128)(2,1)S(1)}, bf16[272,128]{1,0:T(8,128)(2,1)S(1)}, u32[]{:S(2)}, u32[]{:S(2)}) collective-permute-start(bf16[272,128]{1,0:T(8,128)(2,1)S(1)} %get-tuple-element.66), channel_id=1, source_target_pairs={{0,2},{1,3},{2,0},{3,1},{4,6},{5,7},{6,4},{7,5},{8,10},{9,11},{10,... | collective-permute-start | bytes 208904 | tf_op jit(solution)/shard_map/ppermute | solution.py:54
  18.7 7.2 %collective-permute-start.4 = (bf16[272,128]{1,0:T(8,128)(2,1)S(1)}, bf16[272,128]{1,0:T(8,128)(2,1)S(1)}, u32[]{:S(2)}, u32[]{:S(2)}) collective-permute-start(bf16[272,128]{1,0:T(8,128)(2,1)S(1)} %get-tuple-element.67), channel_id=1, source_target_pairs={{0,4},{1,5},{2,6},{3,7},{4,0},{5,1},{6,2},{7,3},{8,12},{9,13},{10,... | collective-permute-start | bytes 208904 | tf_op jit(solution)/shard_map/ppermute | solution.py:54
  21.3 6.1 %collective-permute-start.5 = (bf16[272,128]{1,0:T(8,128)(2,1)S(1)}, bf16[272,128]{1,0:T(8,128)(2,1)S(1)}, u32[]{:S(2)}, u32[]{:S(2)}) collective-permute-start(bf16[272,128]{1,0:T(8,128)(2,1)S(1)} %get-tuple-element.68), channel_id=1, source_target_pairs={{0,6},{1,7},{2,4},{3,5},{4,2},{5,3},{6,0},{7,1},{8,14},{9,15},{10,... | collective-permute-start | bytes 208904 | tf_op jit(solution)/shard_map/ppermute | solution.py:54
  22.3 5.9 %collective-permute-start.6 = (bf16[384,128]{1,0:T(8,128)(2,1)S(1)}, bf16[384,128]{1,0:T(8,128)(2,1)S(1)}, u32[]{:S(2)}, u32[]{:S(2)}) collective-permute-start(bf16[384,128]{1,0:T(8,128)(2,1)S(1)} %get-tuple-element.85.refs_0_), channel_id=1, source_target_pairs={{0,8},{8,0},{16,24},{24,16},{1,9},{9,1},{17,25},{25,17},{2,10},{10... | collective-permute-start | bytes 294920 | tf_op jit(solution)/shard_map/ppermute | solution.py:54
  23.6 4.6 %collective-permute-start.7 = (bf16[384,128]{1,0:T(8,128)(2,1)S(1)}, bf16[384,128]{1,0:T(8,128)(2,1)S(1)}, u32[]{:S(2)}, u32[]{:S(2)}) collective-permute-start(bf16[384,128]{1,0:T(8,128)(2,1)S(1)} %get-tuple-element.86.refs_1_), channel_id=1, source_target_pairs={{0,16},{8,24},{16,0},{24,8},{1,17},{9,25},{17,1},{25,9},{2,18},{10... | collective-permute-start | bytes 294920 | tf_op jit(solution)/shard_map/ppermute | solution.py:54
  28.1 10.2 %copy-start = (f32[2,512,512]{2,1,0:T(8,128)S(1)}, f32[2,512,512]{2,1,0:T(8,128)}, u32[]{:S(2)}) copy-start(f32[2,512,512]{2,1,0:T(8,128)} %left_ref.1) | copy-start | bytes 6291460
  28.2 4.4 %collective-permute-start.9 = (bf16[272,128]{1,0:T(8,128)(2,1)S(1)}, bf16[272,128]{1,0:T(8,128)(2,1)S(1)}, u32[]{:S(2)}, u32[]{:S(2)}) collective-permute-start(bf16[272,128]{1,0:T(8,128)(2,1)S(1)} %get-tuple-element.88), channel_id=1, source_target_pairs={{0,8},{8,0},{16,24},{24,16},{1,9},{9,1},{17,25},{25,17},{2,10},{10... | collective-permute-start | bytes 208904 | tf_op jit(solution)/shard_map/ppermute | solution.py:54
  29.6 4.3 %collective-permute-start.10 = (bf16[272,128]{1,0:T(8,128)(2,1)S(1)}, bf16[272,128]{1,0:T(8,128)(2,1)S(1)}, u32[]{:S(2)}, u32[]{:S(2)}) collective-permute-start(bf16[272,128]{1,0:T(8,128)(2,1)S(1)} %get-tuple-element.89), channel_id=1, source_target_pairs={{0,16},{8,24},{16,0},{24,8},{1,17},{9,25},{17,1},{25,9},{2,18},{10... | collective-permute-start | bytes 208904 | tf_op jit(solution)/shard_map/ppermute | solution.py:54
  30.5 5.2 %collective-permute-start.11 = (bf16[272,128]{1,0:T(8,128)(2,1)S(1)}, bf16[272,128]{1,0:T(8,128)(2,1)S(1)}, u32[]{:S(2)}, u32[]{:S(2)}) collective-permute-start(bf16[272,128]{1,0:T(8,128)(2,1)S(1)} %get-tuple-element.90), channel_id=1, source_target_pairs={{0,24},{8,16},{16,8},{24,0},{1,25},{9,17},{17,9},{25,1},{2,26},{10... | collective-permute-start | bytes 208904 | tf_op jit(solution)/shard_map/ppermute | solution.py:54
  31.7 5.2 %collective-permute-start.12 = (bf16[1,272,128]{2,1,0:T(8,128)(2,1)S(1)}, bf16[1,272,128]{2,1,0:T(8,128)(2,1)S(1)}, u32[]{:S(2)}, u32[]{:S(2)}) collective-permute-start(bf16[1,272,128]{2,1,0:T(8,128)(2,1)S(1)} %bitcast.12), channel_id=1, source_target_pairs={{0,1},{1,0},{2,3},{3,2},{4,5},{5,4},{6,7},{7,6},{8,9},{9,8},{10,11... | collective-permute-start | bytes 208904 | tf_op jit(solution)/shard_map/ppermute | solution.py:54
  32.6 4.4 %collective-permute-start.13 = (bf16[1,272,128]{2,1,0:T(8,128)(2,1)S(1)}, bf16[1,272,128]{2,1,0:T(8,128)(2,1)S(1)}, u32[]{:S(2)}, u32[]{:S(2)}) collective-permute-start(bf16[1,272,128]{2,1,0:T(8,128)(2,1)S(1)} %bitcast.6), channel_id=1, source_target_pairs={{0,1},{1,0},{2,3},{3,2},{4,5},{5,4},{6,7},{7,6},{8,9},{9,8},{10,11... | collective-permute-start | bytes 208904 | tf_op jit(solution)/shard_map/ppermute | solution.py:54
  32.6 13.0 %collective-permute-start.16 = (bf16[768,128]{1,0:T(8,128)(2,1)S(1)}, bf16[768,128]{1,0:T(8,128)(2,1)S(1)}, u32[]{:S(2)}, u32[]{:S(2)}) collective-permute-start(bf16[768,128]{1,0:T(8,128)(2,1)S(1)} %get-tuple-element.92), channel_id=1, source_target_pairs={{0,8},{8,0},{16,24},{24,16},{1,9},{9,1},{17,25},{25,17},{2,10},{10... | collective-permute-start | bytes 589832 | tf_op jit(solution)/shard_map/ppermute | solution.py:54
  33.9 11.7 %collective-permute-start.17 = (bf16[768,128]{1,0:T(8,128)(2,1)S(1)}, bf16[768,128]{1,0:T(8,128)(2,1)S(1)}, u32[]{:S(2)}, u32[]{:S(2)}) collective-permute-start(bf16[768,128]{1,0:T(8,128)(2,1)S(1)} %get-tuple-element.93), channel_id=1, source_target_pairs={{0,16},{8,24},{16,0},{24,8},{1,17},{9,25},{17,1},{25,9},{2,18},{10... | collective-permute-start | bytes 589832 | tf_op jit(solution)/shard_map/ppermute | solution.py:54
  35.7 9.9 %collective-permute-start.18 = (bf16[768,128]{1,0:T(8,128)(2,1)S(1)}, bf16[768,128]{1,0:T(8,128)(2,1)S(1)}, u32[]{:S(2)}, u32[]{:S(2)}) collective-permute-start(bf16[768,128]{1,0:T(8,128)(2,1)S(1)} %get-tuple-element.94), channel_id=1, source_target_pairs={{0,24},{8,16},{16,8},{24,0},{1,25},{9,17},{17,9},{25,1},{2,26},{10... | collective-permute-start | bytes 589832 | tf_op jit(solution)/shard_map/ppermute | solution.py:54
  37.0 1.3 %collective-permute-start.14 = (bf16[1,272,128]{2,1,0:T(8,128)(2,1)S(1)}, bf16[1,272,128]{2,1,0:T(8,128)(2,1)S(1)}, u32[]{:S(2)}, u32[]{:S(2)}) collective-permute-start(bf16[1,272,128]{2,1,0:T(8,128)(2,1)S(1)} %bitcast.8), channel_id=1, source_target_pairs={{0,1},{1,0},{2,3},{3,2},{4,5},{5,4},{6,7},{7,6},{8,9},{9,8},{10,11... | collective-permute-start | bytes 208904 | tf_op jit(solution)/shard_map/ppermute | solution.py:54
  37.0 1.4 %collective-permute-start.15 = (bf16[1,272,128]{2,1,0:T(8,128)(2,1)S(1)}, bf16[1,272,128]{2,1,0:T(8,128)(2,1)S(1)}, u32[]{:S(2)}, u32[]{:S(2)}) collective-permute-start(bf16[1,272,128]{2,1,0:T(8,128)(2,1)S(1)} %bitcast.10), channel_id=1, source_target_pairs={{0,1},{1,0},{2,3},{3,2},{4,5},{5,4},{6,7},{7,6},{8,9},{9,8},{10,11... | collective-permute-start | bytes 208904 | tf_op jit(solution)/shard_map/ppermute | solution.py:54
  45.6 2.0 %collective-permute-start.19 = (bf16[512,512]{1,0:T(8,128)(2,1)S(1)}, bf16[512,512]{1,0:T(8,128)(2,1)S(1)}, u32[]{:S(2)}, u32[]{:S(2)}) collective-permute-start(bf16[512,512]{1,0:T(8,128)(2,1)S(1)} %shard_map.125.mine_ref), channel_id=1, source_target_pairs={{0,1},{1,0},{2,3},{3,2},{4,5},{5,4},{6,7},{7,6},{8,9},{9,8},{10,11... | collective-permute-start | bytes 1572872 | tf_op jit(solution)/shard_map/ppermute | solution.py:54
  46.1 9.4 %copy-start.1 = (f32[2,512,512]{2,1,0:T(8,128)S(1)}, f32[2,512,512]{2,1,0:T(8,128)}, u32[]{:S(2)}) copy-start(f32[2,512,512]{2,1,0:T(8,128)} %right_ref.1) | copy-start | bytes 6291460
  46.8 2.0 %collective-permute-start.20 = (bf16[4,2,256,128]{3,2,1,0:T(8,128)(2,1)S(1)}, bf16[4,2,256,128]{3,2,1,0:T(8,128)(2,1)S(1)}, u32[]{:S(2)}, u32[]{:S(2)}) collective-permute-start(bf16[4,2,256,128]{3,2,1,0:T(8,128)(2,1)S(1)} %get-tuple-element.101), channel_id=1, source_target_pairs={{0,1},{1,0},{2,3},{3,2},{4,5},{5,4},{6,7},{7,6},{8,9},{9,8},{10,11... | collective-permute-start | bytes 1572872 | tf_op jit(solution)/shard_map/ppermute | solution.py:54
  48.8 9.6 %collective-permute-start.21 = (bf16[64,512]{1,0:T(8,128)(2,1)S(1)}, bf16[64,512]{1,0:T(8,128)(2,1)S(1)}, u32[]{:S(2)}, u32[]{:S(2)}) collective-permute-start(bf16[64,512]{1,0:T(8,128)(2,1)S(1)} %get-tuple-element.103), channel_id=1, source_target_pairs={{0,2},{1,3},{2,0},{3,1},{4,6},{5,7},{6,4},{7,5},{8,10},{9,11},{10,... | collective-permute-start | bytes 196616 | tf_op jit(solution)/shard_map/ppermute | solution.py:54
  49.4 8.9 %collective-permute-start.22 = (bf16[64,512]{1,0:T(8,128)(2,1)S(1)}, bf16[64,512]{1,0:T(8,128)(2,1)S(1)}, u32[]{:S(2)}, u32[]{:S(2)}) collective-permute-start(bf16[64,512]{1,0:T(8,128)(2,1)S(1)} %get-tuple-element.104), channel_id=1, source_target_pairs={{0,4},{1,5},{2,6},{3,7},{4,0},{5,1},{6,2},{7,3},{8,12},{9,13},{10,... | collective-permute-start | bytes 196616 | tf_op jit(solution)/shard_map/ppermute | solution.py:54
  52.9 6.1 %collective-permute-start.23 = (bf16[64,512]{1,0:T(8,128)(2,1)S(1)}, bf16[64,512]{1,0:T(8,128)(2,1)S(1)}, u32[]{:S(2)}, u32[]{:S(2)}) collective-permute-start(bf16[64,512]{1,0:T(8,128)(2,1)S(1)} %get-tuple-element.105), channel_id=1, source_target_pairs={{0,6},{1,7},{2,4},{3,5},{4,2},{5,3},{6,0},{7,1},{8,14},{9,15},{10,... | collective-permute-start | bytes 196616 | tf_op jit(solution)/shard_map/ppermute | solution.py:54
  53.2 9.9 %collective-permute-start.27 = (bf16[768,128]{1,0:T(8,128)(2,1)S(1)}, bf16[768,128]{1,0:T(8,128)(2,1)S(1)}, u32[]{:S(2)}, u32[]{:S(2)}) collective-permute-start(bf16[768,128]{1,0:T(8,128)(2,1)S(1)} %shard_map.132), channel_id=1, source_target_pairs={{0,16},{8,24},{16,0},{24,8},{1,17},{9,25},{17,1},{25,9},{2,18},{10... | collective-permute-start | bytes 589832 | tf_op jit(solution)/shard_map/ppermute | solution.py:54
  54.8 8.4 %collective-permute-start.28 = (bf16[768,128]{1,0:T(8,128)(2,1)S(1)}, bf16[768,128]{1,0:T(8,128)(2,1)S(1)}, u32[]{:S(2)}, u32[]{:S(2)}) collective-permute-start(bf16[768,128]{1,0:T(8,128)(2,1)S(1)} %shard_map.133), channel_id=1, source_target_pairs={{0,8},{8,0},{16,24},{24,16},{1,9},{9,1},{17,25},{25,17},{2,10},{10... | collective-permute-start | bytes 589832 | tf_op jit(solution)/shard_map/ppermute | solution.py:54
  55.5 7.6 %copy-start.3 = (f32[2,8,8192]{2,1,0:T(8,128)S(1)}, f32[2,8,8192]{2,1,0:T(8,128)}, u32[]{:S(2)}) copy-start(f32[2,8,8192]{2,1,0:T(8,128)} %vocab_ref.1) | copy-start | bytes 1572868
  59.6 6.0 %collective-permute-start.24 = (bf16[2,64,512]{2,1,0:T(8,128)(2,1)S(1)}, bf16[2,64,512]{2,1,0:T(8,128)(2,1)S(1)}, u32[]{:S(2)}, u32[]{:S(2)}) collective-permute-start(bf16[2,64,512]{2,1,0:T(8,128)(2,1)S(1)} %shard_map.131.after_ref.refs_0_), channel_id=1, source_target_pairs={{0,8},{8,0},{16,24},{24,16},{1,9},{9,1},{17,25},{25,17},{2,10},{10... | collective-permute-start | bytes 393224 | tf_op jit(solution)/shard_map/ppermute | solution.py:54
  60.5 7.5 %collective-permute-start.25 = (bf16[2,64,512]{2,1,0:T(8,128)(2,1)S(1)}, bf16[2,64,512]{2,1,0:T(8,128)(2,1)S(1)}, u32[]{:S(2)}, u32[]{:S(2)}) collective-permute-start(bf16[2,64,512]{2,1,0:T(8,128)(2,1)S(1)} %shard_map.131.after_ref.refs_0_), channel_id=1, source_target_pairs={{0,16},{8,24},{16,0},{24,8},{1,17},{9,25},{17,1},{25,9},{2,18},{10... | collective-permute-start | bytes 393224 | tf_op jit(solution)/shard_map/ppermute | solution.py:54
  62.0 6.0 %collective-permute-start.26 = (bf16[2,64,512]{2,1,0:T(8,128)(2,1)S(1)}, bf16[2,64,512]{2,1,0:T(8,128)(2,1)S(1)}, u32[]{:S(2)}, u32[]{:S(2)}) collective-permute-start(bf16[2,64,512]{2,1,0:T(8,128)(2,1)S(1)} %shard_map.131.after_ref.refs_0_), channel_id=1, source_target_pairs={{0,24},{8,16},{16,8},{24,0},{1,25},{9,17},{17,9},{25,1},{2,26},{10... | collective-permute-start | bytes 393224 | tf_op jit(solution)/shard_map/ppermute | solution.py:54
  (1 other events, 7.6 us)

commit v4 on v3

--- a/solution.py
+++ b/solution.py
@@ -241,8 +241,7 @@
     def route_body(slot_ref, *refs):
         in_refs = refs[:planes]
         out_refs = refs[planes : planes + reps]
-        whole_ref, rest_refs = refs[planes + reps], refs[planes + reps + 1 : planes + 2 * reps]
-        parts, tail = refs[planes + 2 * reps :]
+        parts, tail = refs[planes + reps :]
         rep_here = place()[0]
         total = jnp.zeros((per, cols), F32)
         for ref in in_refs:
@@ -265,6 +264,9 @@
             for t, term in enumerate(three_terms(parts[pl.ds(local, 1), :])):
                 tail[t : t + 1, :] = term
             out_refs[j][planes * rows :, :] = tail[...].astype(BF16)
+    def rest_body(slot_ref, *refs):
+        in_refs, whole_ref, rest_refs = refs[:planes], refs[planes + 1], refs[planes + 2 :]
+        rep_here = place()[0]
         piece = planes * rows
         for k in range(planes):
             for s in range(per):
@@ -280,19 +282,22 @@
     piece_rows = planes * rows
     routed = call(
         route_body,
-        [shape((part_rows, cols), BF16)] * reps
-        + [shape((per * piece_rows, cols), BF16)]
-        + [shape(((per - 1) * piece_rows, cols), BF16)] * (reps - 1),
+        [shape((part_rows, cols), BF16)] * reps,
         [SMEM] + [VMEM] * planes,
         scratch=[pltpu.VMEM((8, cols), F32), pltpu.VMEM((TAIL, cols), F32)],
     )(book, *arrived)
-    routed = late(routed, *share_firsts, right_other)
-    parts, whole, rests = routed[:reps], routed[reps], routed[reps + 1 :]
+    parts = late(routed, *share_firsts, right_other)
 
     met = [parts[0]] + [exchange(parts[j], "rep", j, reps) for j in rep_partners]
     mine = [jnp.stack(met[i : i + SWAP]) for i in range(0, reps, SWAP)]
     other = [exchange(array, "fsdp", 1, indices) for array in mine]
 
+    whole, *rests = call(
+        rest_body,
+        [shape((per * piece_rows, cols), BF16)]
+        + [shape(((per - 1) * piece_rows, cols), BF16)] * (reps - 1),
+        [SMEM] + [VMEM] * planes + [ANY],
+    )(book, *arrived, parts[0])
     rests_met = [exchange(rests[j - 1], "rep", j, reps) for j in rep_partners]
 
     def assemble(grad, rep_here, plane_here, core_here, piece, k, j):

time: 69.6 us -> 69.5 us (level)
  waiting for transfers between devices: 19.1 us -> 18.4 us
  transfers between devices with their start and end apart: 29 -> 29, of which waited for: 13 -> 15; matrix products, arithmetic and copies ran while one was open for 1% -> 1% of each run, Pallas kernels for 25% -> 26%
where the time goes in v4:
time: 69.5 us; the launch traced here: 69.3 us
  starting transfers between devices  29.6 us (43%)
  Pallas kernels  19.4 us (28%)
  waiting for transfers between devices  18.4 us (26%)
  local copies, waits for them, and re-layouts  0.98 us (1%)
  between operations  0.81 us (1%)
    ppermute x29, starting transfers between devices, exchange(): return lax.ppermute(values, axis, [(i, i ^ mask) for i in range(size)])  29.6 us
    ppermute x29, waiting for transfers between devices, exchange(): return lax.ppermute(values, axis, [(i, i ^ mask) for i in range(size)])  18.4 us
    pallas_call x1, Pallas kernels, on_device(): call(root_body, [shape(square, BF16), shape((8, cols), F32)], [SMEM] + [V...  7.21 us
    pallas_call x1, Pallas kernels, on_device(): pl.pallas_call(stats_body, grid=(most,), out_shape=[shape(left_stats.shap...  2.8 us
    pallas_call x1, Pallas kernels, on_device(): call(accum_body, [shape(graft_accum.shape, F32), shape(vocab_accum.shape,...  1.57 us
    pallas_call x1, Pallas kernels, on_device(): call(place_body, shape((blocks, rows, order), BF16), [SMEM] + [VMEM] * re...  1.4 us
  transfers between devices with their start and end apart: 29, of which 15 were waited for; matrix products, arithmetic and copies ran while one was open for 1% of the time, Pallas kernels for 26%

profile of v4, /device:TPU:0, one launch (start us, length us, event | category | flops | bytes accessed | tf_op | source)
XLA Modules:
  0.0 69.3 jit_solution(17849999779262638394)
XLA Ops:
  1.1 1.3 %shard_map.118 = (bf16[768,128]{1,0:T(8,128)(2,1)S(1)}, bf16[768,128]{1,0:T(8,128)(2,1)S(1)}, bf16[768,128]{1,0:T(8,128)(2,1)S(1)}, bf16[768,128]{1,0:T(8,128)(2,1)S(1)}, s32[1,128]{1,0:T(1,128)S(1)}) custom-call(s32[8]{0:T(128)} %slot_ref.1, bf16[8,64,512]{2,1,0:T(8,128)(2,1)} %bitcast.14, bf16[2,8,8192]{2,1,0:T(8,128)(2,1)} %bitcast.15), custom_call_target="tpu_custom_call" | custom-call | flops 1 | bytes 1 | tf_op jit(solution)/shard_map/pallas_call | solution.py:160
  2.4 2.6 %collective-permute-start = (bf16[768,128]{1,0:T(8,128)(2,1)S(1)}, bf16[768,128]{1,0:T(8,128)(2,1)S(1)}, u32[]{:S(2)}, u32[]{:S(2)}) collective-permute-start(bf16[768,128]{1,0:T(8,128)(2,1)S(1)} %get-tuple-element.54), channel_id=1, source_target_pairs={{0,8},{8,0},{16,24},{24,16},{1,9},{9,1},{17,25},{25,17},{2,10},{10... | collective-permute-start | bytes 589832 | tf_op jit(solution)/shard_map/ppermute | solution.py:54
  5.0 1.5 %collective-permute-start.1 = (bf16[768,128]{1,0:T(8,128)(2,1)S(1)}, bf16[768,128]{1,0:T(8,128)(2,1)S(1)}, u32[]{:S(2)}, u32[]{:S(2)}) collective-permute-start(bf16[768,128]{1,0:T(8,128)(2,1)S(1)} %get-tuple-element.55), channel_id=1, source_target_pairs={{0,16},{8,24},{16,0},{24,8},{1,17},{9,25},{17,1},{25,9},{2,18},{10... | collective-permute-start | bytes 589832 | tf_op jit(solution)/shard_map/ppermute | solution.py:54
  6.5 1.0 %constant_dynamic-slice_fusion.refs_4_ = f32[8,64,128]{2,1,0:T(8,128)S(1)} fusion(f32[8,64,512]{2,1,0:T(8,128)} %accum_ref.1, s32[]{:T(128)S(6)} %select_n.3), kind=kLoop, calls=%fused_computation.2 | loop fusion | bytes 524292 | tf_op jit(solution)/shard_map/dynamic_slice | solution.py:168
  7.5 3.2 %collective-permute-done.refs_1_ = bf16[768,128]{1,0:T(8,128)(2,1)S(1)} collective-permute-done((bf16[768,128]{1,0:T(8,128)(2,1)S(1)}, bf16[768,128]{1,0:T(8,128)(2,1)S(1)}, u32[]{:S(2)}, u32[]{:S(2)}) %collective-permute-start) | collective-permute-done | bytes 196640 | tf_op jit(solution)/shard_map/ppermute | solution.py:54
  10.7 5.5 %collective-permute-done.1.refs_2_ = bf16[768,128]{1,0:T(8,128)(2,1)S(1)} collective-permute-done((bf16[768,128]{1,0:T(8,128)(2,1)S(1)}, bf16[768,128]{1,0:T(8,128)(2,1)S(1)}, u32[]{:S(2)}, u32[]{:S(2)}) %collective-permute-start.1) | collective-permute-done | bytes 196640 | tf_op jit(solution)/shard_map/ppermute | solution.py:54
  16.2 0.8 %shard_map.120 = (bf16[384,128]{1,0:T(8,128)(2,1)S(1)}, bf16[384,128]{1,0:T(8,128)(2,1)S(1)}, bf16[272,128]{1,0:T(8,128)(2,1)S(1)}, bf16[272,128]{1,0:T(8,128)(2...) custom-call(s32[1,128]{1,0:T(1,128)S(1)} %get-tuple-element.52.slot_ref, ...), custom_call_target="tpu_custom_call" | custom-call | flops 1 | bytes 1 | tf_op jit(solution)/shard_map/pallas_call | solution.py:221
  17.1 1.6 %collective-permute-start.3 = (bf16[272,128]{1,0:T(8,128)(2,1)S(1)}, bf16[272,128]{1,0:T(8,128)(2,1)S(1)}, u32[]{:S(2)}, u32[]{:S(2)}) collective-permute-start(bf16[272,128]{1,0:T(8,128)(2,1)S(1)} %get-tuple-element.58), channel_id=1, source_target_pairs={{0,2},{1,3},{2,0},{3,1},{4,6},{5,7},{6,4},{7,5},{8,10},{9,11},{10,... | collective-permute-start | bytes 208904 | tf_op jit(solution)/shard_map/ppermute | solution.py:54
  18.7 2.6 %collective-permute-start.4 = (bf16[272,128]{1,0:T(8,128)(2,1)S(1)}, bf16[272,128]{1,0:T(8,128)(2,1)S(1)}, u32[]{:S(2)}, u32[]{:S(2)}) collective-permute-start(bf16[272,128]{1,0:T(8,128)(2,1)S(1)} %get-tuple-element.59), channel_id=1, source_target_pairs={{0,4},{1,5},{2,6},{3,7},{4,0},{5,1},{6,2},{7,3},{8,12},{9,13},{10,... | collective-permute-start | bytes 208904 | tf_op jit(solution)/shard_map/ppermute | solution.py:54
  22.3 1.3 %collective-permute-start.6 = (bf16[384,128]{1,0:T(8,128)(2,1)S(1)}, bf16[384,128]{1,0:T(8,128)(2,1)S(1)}, u32[]{:S(2)}, u32[]{:S(2)}) collective-permute-start(bf16[384,128]{1,0:T(8,128)(2,1)S(1)} %get-tuple-element.69.refs_0_), channel_id=1, source_target_pairs={{0,8},{8,0},{16,24},{24,16},{1,9},{9,1},{17,25},{25,17},{2,10},{10... | collective-permute-start | bytes 294920 | tf_op jit(solution)/shard_map/ppermute | solution.py:54
  23.6 0.8 %collective-permute-start.7 = (bf16[384,128]{1,0:T(8,128)(2,1)S(1)}, bf16[384,128]{1,0:T(8,128)(2,1)S(1)}, u32[]{:S(2)}, u32[]{:S(2)}) collective-permute-start(bf16[384,128]{1,0:T(8,128)(2,1)S(1)} %get-tuple-element.70.refs_1_), channel_id=1, source_target_pairs={{0,16},{8,24},{16,0},{24,8},{1,17},{9,25},{17,1},{25,9},{2,18},{10... | collective-permute-start | bytes 294920 | tf_op jit(solution)/shard_map/ppermute | solution.py:54
  24.4 1.5 %collective-permute-done.4.refs_2_ = bf16[272,128]{1,0:T(8,128)(2,1)S(1)} collective-permute-done((bf16[272,128]{1,0:T(8,128)(2,1)S(1)}, bf16[272,128]{1,0:T(8,128)(2,1)S(1)}, u32[]{:S(2)}, u32[]{:S(2)}) %collective-permute-start.4) | collective-permute-done | bytes 69664 | tf_op jit(solution)/shard_map/ppermute | solution.py:54
  25.9 1.5 %collective-permute-done.5.refs_3_ = bf16[272,128]{1,0:T(8,128)(2,1)S(1)} collective-permute-done((bf16[272,128]{1,0:T(8,128)(2,1)S(1)}, bf16[272,128]{1,0:T(8,128)(2,1)S(1)}, u32[]{:S(2)}, u32[]{:S(2)}) %collective-permute-start.5) | collective-permute-done | bytes 69664 | tf_op jit(solution)/shard_map/ppermute | solution.py:54
  28.2 1.3 %collective-permute-start.9 = (bf16[272,128]{1,0:T(8,128)(2,1)S(1)}, bf16[272,128]{1,0:T(8,128)(2,1)S(1)}, u32[]{:S(2)}, u32[]{:S(2)}) collective-permute-start(bf16[272,128]{1,0:T(8,128)(2,1)S(1)} %get-tuple-element.72), channel_id=1, source_target_pairs={{0,8},{8,0},{16,24},{24,16},{1,9},{9,1},{17,25},{25,17},{2,10},{10... | collective-permute-start | bytes 208904 | tf_op jit(solution)/shard_map/ppermute | solution.py:54
  29.5 1.0 %collective-permute-start.10 = (bf16[272,128]{1,0:T(8,128)(2,1)S(1)}, bf16[272,128]{1,0:T(8,128)(2,1)S(1)}, u32[]{:S(2)}, u32[]{:S(2)}) collective-permute-start(bf16[272,128]{1,0:T(8,128)(2,1)S(1)} %get-tuple-element.73), channel_id=1, source_target_pairs={{0,16},{8,24},{16,0},{24,8},{1,17},{9,25},{17,1},{25,9},{2,18},{10... | collective-permute-start | bytes 208904 | tf_op jit(solution)/shard_map/ppermute | solution.py:54
  30.5 1.2 %collective-permute-start.11 = (bf16[272,128]{1,0:T(8,128)(2,1)S(1)}, bf16[272,128]{1,0:T(8,128)(2,1)S(1)}, u32[]{:S(2)}, u32[]{:S(2)}) collective-permute-start(bf16[272,128]{1,0:T(8,128)(2,1)S(1)} %get-tuple-element.74), channel_id=1, source_target_pairs={{0,24},{8,16},{16,8},{24,0},{1,25},{9,17},{17,9},{25,1},{2,26},{10... | collective-permute-start | bytes 208904 | tf_op jit(solution)/shard_map/ppermute | solution.py:54
  31.7 0.8 %collective-permute-done.9.refs_0_ = bf16[272,128]{1,0:T(8,128)(2,1)S(1)} collective-permute-done((bf16[272,128]{1,0:T(8,128)(2,1)S(1)}, bf16[272,128]{1,0:T(8,128)(2,1)S(1)}, u32[]{:S(2)}, u32[]{:S(2)}) %collective-permute-start.9) | collective-permute-done | bytes 69664 | tf_op jit(solution)/shard_map/ppermute | solution.py:54
  33.1 1.4 %collective-permute-start.16 = (bf16[768,128]{1,0:T(8,128)(2,1)S(1)}, bf16[768,128]{1,0:T(8,128)(2,1)S(1)}, u32[]{:S(2)}, u32[]{:S(2)}) collective-permute-start(bf16[768,128]{1,0:T(8,128)(2,1)S(1)} %get-tuple-element.76), channel_id=1, source_target_pairs={{0,8},{8,0},{16,24},{24,16},{1,9},{9,1},{17,25},{25,17},{2,10},{10... | collective-permute-start | bytes 589832 | tf_op jit(solution)/shard_map/ppermute | solution.py:54
  34.5 1.0 %collective-permute-start.17 = (bf16[768,128]{1,0:T(8,128)(2,1)S(1)}, bf16[768,128]{1,0:T(8,128)(2,1)S(1)}, u32[]{:S(2)}, u32[]{:S(2)}) collective-permute-start(bf16[768,128]{1,0:T(8,128)(2,1)S(1)} %get-tuple-element.77), channel_id=1, source_target_pairs={{0,16},{8,24},{16,0},{24,8},{1,17},{9,25},{17,1},{25,9},{2,18},{10... | collective-permute-start | bytes 589832 | tf_op jit(solution)/shard_map/ppermute | solution.py:54
  35.7 1.2 %collective-permute-start.18 = (bf16[768,128]{1,0:T(8,128)(2,1)S(1)}, bf16[768,128]{1,0:T(8,128)(2,1)S(1)}, u32[]{:S(2)}, u32[]{:S(2)}) collective-permute-start(bf16[768,128]{1,0:T(8,128)(2,1)S(1)} %get-tuple-element.78), channel_id=1, source_target_pairs={{0,24},{8,16},{16,8},{24,0},{1,25},{9,17},{17,9},{25,1},{2,26},{10... | collective-permute-start | bytes 589832 | tf_op jit(solution)/shard_map/ppermute | solution.py:54
  38.3 7.2 %shard_map.124 = (bf16[512,512]{1,0:T(8,128)(2,1)S(1)}, f32[8,128]{1,0:T(8,128)S(1)}) custom-call(s32[1,128]{1,0:T(1,128)S(1)} %shard_map.119.slot_ref, bf16[1,272,128]{2,1,0:T(8,128)(2,1)S(1)} %bitcast.7, bf16[1,272,128]{2,1,0:T(8,128)(2,1)S(1)} %bitcast.9, bf16[1,272,128]{2,1,0:T(8,128)(2,1)S(1)} %bitcast.11, bf16[1,272,128]{2,1,0:T(8,128)(2,1)S(1)} %bitcast.13, ...), custom_call_target="tpu_custom_call" | custom-call | flops 1000000000 | bytes 1 | tf_op jit(solution)/shard_map/pallas_call | solution.py:383
  47.7 1.1 %shard_map.127 = (bf16[64,512]{1,0:T(8,128)(2,1)S(1)}, bf16[64,512]{1,0:T(8,128)(2,1)S(1)}, bf16[64,512]{1,0:T(8,128)(2,1)S(1)}, bf16[64,512]{1,0:T(8,128)(2,1)S(1)}) custom-call(bf16[512,512]{1,0:T(8,128)(2,1)S(1)} %shard_map.126.mine_ref, bf16[512,512]{1,0:T(8,128)(2,1)S(1)} %collective-permute-done.19.other_ref, f32[8,128]{1,0:T(8,128)S(1)} %get-tuple-element.79.graft_ref), custom_call_target="tpu_custom_call" | custom-call | flops 268435456 | bytes 1 | tf_op jit(solution)/shard_map/pallas_call | solution.py:420
  49.5 3.4 %collective-permute-start.22 = (bf16[64,512]{1,0:T(8,128)(2,1)S(1)}, bf16[64,512]{1,0:T(8,128)(2,1)S(1)}, u32[]{:S(2)}, u32[]{:S(2)}) collective-permute-start(bf16[64,512]{1,0:T(8,128)(2,1)S(1)} %get-tuple-element.88), channel_id=1, source_target_pairs={{0,4},{1,5},{2,6},{3,7},{4,0},{5,1},{6,2},{7,3},{8,12},{9,13},{10,... | collective-permute-start | bytes 196616 | tf_op jit(solution)/shard_map/ppermute | solution.py:54
  53.2 1.5 %collective-permute-start.27 = (bf16[768,128]{1,0:T(8,128)(2,1)S(1)}, bf16[768,128]{1,0:T(8,128)(2,1)S(1)}, u32[]{:S(2)}, u32[]{:S(2)}) collective-permute-start(bf16[768,128]{1,0:T(8,128)(2,1)S(1)} %shard_map.133), channel_id=1, source_target_pairs={{0,16},{8,24},{16,0},{24,8},{1,17},{9,25},{17,1},{25,9},{2,18},{10... | collective-permute-start | bytes 589832 | tf_op jit(solution)/shard_map/ppermute | solution.py:54
  55.6 2.8 %shard_map.130 = (f32[2,512,512]{2,1,0:T(8,128)}, f32[2,512,512]{2,1,0:T(8,128)}, f32[8,128]{1,0:T(8,128)S(1)}) custom-call(f32[2,512,512]{2,1,0:T(8,128)S(1)} %copy-done, f32[2,512,512]{2,1,0:T(8,128)S(1)} %copy-done.1, bf16[64,512]{1,0:T(8,128)(2,1)S(1)} %get-tuple-element.86.after_ref.refs_0_.refs_1_, ...), custom_call_target="tpu_custom_call" | custom-call | flops 1 | bytes 1 | tf_op jit(solution)/shard_map/pallas_call | solution.py:486
  59.6 0.8 %collective-permute-start.24 = (bf16[2,64,512]{2,1,0:T(8,128)(2,1)S(1)}, bf16[2,64,512]{2,1,0:T(8,128)(2,1)S(1)}, u32[]{:S(2)}, u32[]{:S(2)}) collective-permute-start(bf16[2,64,512]{2,1,0:T(8,128)(2,1)S(1)} %shard_map.132.after_ref.refs_0_), channel_id=1, source_target_pairs={{0,8},{8,0},{16,24},{24,16},{1,9},{9,1},{17,25},{25,17},{2,10},{10... | collective-permute-start | bytes 393224 | tf_op jit(solution)/shard_map/ppermute | solution.py:54
  60.5 1.5 %collective-permute-start.25 = (bf16[2,64,512]{2,1,0:T(8,128)(2,1)S(1)}, bf16[2,64,512]{2,1,0:T(8,128)(2,1)S(1)}, u32[]{:S(2)}, u32[]{:S(2)}) collective-permute-start(bf16[2,64,512]{2,1,0:T(8,128)(2,1)S(1)} %shard_map.132.after_ref.refs_0_), channel_id=1, source_target_pairs={{0,16},{8,24},{16,0},{24,8},{1,17},{9,25},{17,1},{25,9},{2,18},{10... | collective-permute-start | bytes 393224 | tf_op jit(solution)/shard_map/ppermute | solution.py:54
  62.0 1.2 %collective-permute-start.26 = (bf16[2,64,512]{2,1,0:T(8,128)(2,1)S(1)}, bf16[2,64,512]{2,1,0:T(8,128)(2,1)S(1)}, u32[]{:S(2)}, u32[]{:S(2)}) collective-permute-start(bf16[2,64,512]{2,1,0:T(8,128)(2,1)S(1)} %shard_map.132.after_ref.refs_0_), channel_id=1, source_target_pairs={{0,24},{8,16},{16,8},{24,0},{1,25},{9,17},{17,9},{25,1},{2,26},{10... | collective-permute-start | bytes 393224 | tf_op jit(solution)/shard_map/ppermute | solution.py:54
  63.2 1.6 %shard_map.135 = (f32[8,64,512]{2,1,0:T(8,128)}, f32[2,8,8192]{2,1,0:T(8,128)}, bf16[2,8,8192]{2,1,0:T(8,128)(2,1)}, f32[8,128]{1,0:T(8,128)S(1)}) custom-call(f32[8,64,512]{2,1,0:T(8,128)S(1)} %copy-done.2, f32[2,8,8192]{2,1,0:T(8,128)S(1)} %copy-done.3, bf16[2,64,512]{2,1,0:T(8,128)(2,1)S(1)} %shard_map.132.after_ref.refs_0_, ...), custom_call_target="tpu_custom_call" | custom-call | flops 1 | bytes 1 | tf_op jit(solution)/shard_map/pallas_call | solution.py:546
  65.5 1.0 %collective-permute-done.25.refs_2_ = bf16[2,64,512]{2,1,0:T(8,128)(2,1)S(1)} collective-permute-done((bf16[2,64,512]{2,1,0:T(8,128)(2,1)S(1)}, bf16[2,64,512]{2,1,0:T(8,128)(2,1)S(1)}, u32[]{:S(2)}, u32[]{:S(2)}) %collective-permute-start.25) | collective-permute-done | bytes 131104 | tf_op jit(solution)/shard_map/ppermute | solution.py:54
  66.5 1.4 %collective-permute-done.26.refs_3_ = bf16[2,64,512]{2,1,0:T(8,128)(2,1)S(1)} collective-permute-done((bf16[2,64,512]{2,1,0:T(8,128)(2,1)S(1)}, bf16[2,64,512]{2,1,0:T(8,128)(2,1)S(1)}, u32[]{:S(2)}, u32[]{:S(2)}) %collective-permute-start.26) | collective-permute-done | bytes 131104 | tf_op jit(solution)/shard_map/ppermute | solution.py:54
  67.9 1.4 %shard_map.136 = bf16[8,64,512]{2,1,0:T(8,128)(2,1)} custom-call(s32[1,128]{1,0:T(1,128)S(1)} %shard_map.119.slot_ref, bf16[2,64,512]{2,1,0:T(8,128)(2,1)S(1)} %shard_map.132.after_ref.refs_0_, bf16[2,64,512]{2,1,0:T(8,128)(2,1)S(1)} %collective-permute-done.24.refs_1_, bf16[2,64,512]{2,1,0:T(8,128)(2,1)S(1)} %collective-permute-done.25.refs_2_, ...), custom_call_target="tpu_custom_call" | custom-call | flops 1 | bytes 1 | tf_op jit(solution)/shard_map/pallas_call | solution.py:575
  (56 shorter events, 10.5 us)
Async XLA Ops:
  0.6 27.5 %collective-permute-start.8 = (f32[2,512,512]{2,1,0:T(8,128)}, f32[2,512,512]{2,1,0:T(8,128)S(1)}, u32[]{:S(2)}, u32[]{:S(2)}) collective-permute-start(f32[2,512,512]{2,1,0:T(8,128)} %right_ref.1), channel_id=1, source_target_pairs={{0,1},{1,0},{2,3},{3,2},{4,5},{5,4},{6,7},{7,6},{8,9},{9,8},{10,11... | collective-permute-start | bytes 6291464 | tf_op jit(solution)/shard_map/ppermute | solution.py:54
  2.4 8.3 %collective-permute-start = (bf16[768,128]{1,0:T(8,128)(2,1)S(1)}, bf16[768,128]{1,0:T(8,128)(2,1)S(1)}, u32[]{:S(2)}, u32[]{:S(2)}) collective-permute-start(bf16[768,128]{1,0:T(8,128)(2,1)S(1)} %get-tuple-element.54), channel_id=1, source_target_pairs={{0,8},{8,0},{16,24},{24,16},{1,9},{9,1},{17,25},{25,17},{2,10},{10... | collective-permute-start | bytes 589832 | tf_op jit(solution)/shard_map/ppermute | solution.py:54
  5.0 11.2 %collective-permute-start.1 = (bf16[768,128]{1,0:T(8,128)(2,1)S(1)}, bf16[768,128]{1,0:T(8,128)(2,1)S(1)}, u32[]{:S(2)}, u32[]{:S(2)}) collective-permute-start(bf16[768,128]{1,0:T(8,128)(2,1)S(1)} %get-tuple-element.55), channel_id=1, source_target_pairs={{0,16},{8,24},{16,0},{24,8},{1,17},{9,25},{17,1},{25,9},{2,18},{10... | collective-permute-start | bytes 589832 | tf_op jit(solution)/shard_map/ppermute | solution.py:54
  6.5 9.7 %collective-permute-start.2 = (bf16[768,128]{1,0:T(8,128)(2,1)S(1)}, bf16[768,128]{1,0:T(8,128)(2,1)S(1)}, u32[]{:S(2)}, u32[]{:S(2)}) collective-permute-start(bf16[768,128]{1,0:T(8,128)(2,1)S(1)} %get-tuple-element.56), channel_id=1, source_target_pairs={{0,24},{8,16},{16,8},{24,0},{1,25},{9,17},{17,9},{25,1},{2,26},{10... | collective-permute-start | bytes 589832 | tf_op jit(solution)/shard_map/ppermute | solution.py:54
  17.1 6.5 %collective-permute-start.3 = (bf16[272,128]{1,0:T(8,128)(2,1)S(1)}, bf16[272,128]{1,0:T(8,128)(2,1)S(1)}, u32[]{:S(2)}, u32[]{:S(2)}) collective-permute-start(bf16[272,128]{1,0:T(8,128)(2,1)S(1)} %get-tuple-element.58), channel_id=1, source_target_pairs={{0,2},{1,3},{2,0},{3,1},{4,6},{5,7},{6,4},{7,5},{8,10},{9,11},{10,... | collective-permute-start | bytes 208904 | tf_op jit(solution)/shard_map/ppermute | solution.py:54
  18.7 7.2 %collective-permute-start.4 = (bf16[272,128]{1,0:T(8,128)(2,1)S(1)}, bf16[272,128]{1,0:T(8,128)(2,1)S(1)}, u32[]{:S(2)}, u32[]{:S(2)}) collective-permute-start(bf16[272,128]{1,0:T(8,128)(2,1)S(1)} %get-tuple-element.59), channel_id=1, source_target_pairs={{0,4},{1,5},{2,6},{3,7},{4,0},{5,1},{6,2},{7,3},{8,12},{9,13},{10,... | collective-permute-start | bytes 208904 | tf_op jit(solution)/shard_map/ppermute | solution.py:54
  21.3 6.1 %collective-permute-start.5 = (bf16[272,128]{1,0:T(8,128)(2,1)S(1)}, bf16[272,128]{1,0:T(8,128)(2,1)S(1)}, u32[]{:S(2)}, u32[]{:S(2)}) collective-permute-start(bf16[272,128]{1,0:T(8,128)(2,1)S(1)} %get-tuple-element.60), channel_id=1, source_target_pairs={{0,6},{1,7},{2,4},{3,5},{4,2},{5,3},{6,0},{7,1},{8,14},{9,15},{10,... | collective-permute-start | bytes 208904 | tf_op jit(solution)/shard_map/ppermute | solution.py:54
  22.3 5.8 %collective-permute-start.6 = (bf16[384,128]{1,0:T(8,128)(2,1)S(1)}, bf16[384,128]{1,0:T(8,128)(2,1)S(1)}, u32[]{:S(2)}, u32[]{:S(2)}) collective-permute-start(bf16[384,128]{1,0:T(8,128)(2,1)S(1)} %get-tuple-element.69.refs_0_), channel_id=1, source_target_pairs={{0,8},{8,0},{16,24},{24,16},{1,9},{9,1},{17,25},{25,17},{2,10},{10... | collective-permute-start | bytes 294920 | tf_op jit(solution)/shard_map/ppermute | solution.py:54
  23.6 4.6 %collective-permute-start.7 = (bf16[384,128]{1,0:T(8,128)(2,1)S(1)}, bf16[384,128]{1,0:T(8,128)(2,1)S(1)}, u32[]{:S(2)}, u32[]{:S(2)}) collective-permute-start(bf16[384,128]{1,0:T(8,128)(2,1)S(1)} %get-tuple-element.70.refs_1_), channel_id=1, source_target_pairs={{0,16},{8,24},{16,0},{24,8},{1,17},{9,25},{17,1},{25,9},{2,18},{10... | collective-permute-start | bytes 294920 | tf_op jit(solution)/shard_map/ppermute | solution.py:54
  28.1 10.2 %copy-start = (f32[2,512,512]{2,1,0:T(8,128)S(1)}, f32[2,512,512]{2,1,0:T(8,128)}, u32[]{:S(2)}) copy-start(f32[2,512,512]{2,1,0:T(8,128)} %left_ref.1) | copy-start | bytes 6291460
  28.2 4.3 %collective-permute-start.9 = (bf16[272,128]{1,0:T(8,128)(2,1)S(1)}, bf16[272,128]{1,0:T(8,128)(2,1)S(1)}, u32[]{:S(2)}, u32[]{:S(2)}) collective-permute-start(bf16[272,128]{1,0:T(8,128)(2,1)S(1)} %get-tuple-element.72), channel_id=1, source_target_pairs={{0,8},{8,0},{16,24},{24,16},{1,9},{9,1},{17,25},{25,17},{2,10},{10... | collective-permute-start | bytes 208904 | tf_op jit(solution)/shard_map/ppermute | solution.py:54
  29.5 5.0 %collective-permute-start.10 = (bf16[272,128]{1,0:T(8,128)(2,1)S(1)}, bf16[272,128]{1,0:T(8,128)(2,1)S(1)}, u32[]{:S(2)}, u32[]{:S(2)}) collective-permute-start(bf16[272,128]{1,0:T(8,128)(2,1)S(1)} %get-tuple-element.73), channel_id=1, source_target_pairs={{0,16},{8,24},{16,0},{24,8},{1,17},{9,25},{17,1},{25,9},{2,18},{10... | collective-permute-start | bytes 208904 | tf_op jit(solution)/shard_map/ppermute | solution.py:54
  30.5 5.2 %collective-permute-start.11 = (bf16[272,128]{1,0:T(8,128)(2,1)S(1)}, bf16[272,128]{1,0:T(8,128)(2,1)S(1)}, u32[]{:S(2)}, u32[]{:S(2)}) collective-permute-start(bf16[272,128]{1,0:T(8,128)(2,1)S(1)} %get-tuple-element.74), channel_id=1, source_target_pairs={{0,24},{8,16},{16,8},{24,0},{1,25},{9,17},{17,9},{25,1},{2,26},{10... | collective-permute-start | bytes 208904 | tf_op jit(solution)/shard_map/ppermute | solution.py:54
  31.7 5.2 %collective-permute-start.12 = (bf16[1,272,128]{2,1,0:T(8,128)(2,1)S(1)}, bf16[1,272,128]{2,1,0:T(8,128)(2,1)S(1)}, u32[]{:S(2)}, u32[]{:S(2)}) collective-permute-start(bf16[1,272,128]{2,1,0:T(8,128)(2,1)S(1)} %bitcast.6), channel_id=1, source_target_pairs={{0,1},{1,0},{2,3},{3,2},{4,5},{5,4},{6,7},{7,6},{8,9},{9,8},{10,11... | collective-permute-start | bytes 208904 | tf_op jit(solution)/shard_map/ppermute | solution.py:54
  32.5 4.4 %collective-permute-start.13 = (bf16[1,272,128]{2,1,0:T(8,128)(2,1)S(1)}, bf16[1,272,128]{2,1,0:T(8,128)(2,1)S(1)}, u32[]{:S(2)}, u32[]{:S(2)}) collective-permute-start(bf16[1,272,128]{2,1,0:T(8,128)(2,1)S(1)} %bitcast.8), channel_id=1, source_target_pairs={{0,1},{1,0},{2,3},{3,2},{4,5},{5,4},{6,7},{7,6},{8,9},{9,8},{10,11... | collective-permute-start | bytes 208904 | tf_op jit(solution)/shard_map/ppermute | solution.py:54
  33.1 12.4 %collective-permute-start.16 = (bf16[768,128]{1,0:T(8,128)(2,1)S(1)}, bf16[768,128]{1,0:T(8,128)(2,1)S(1)}, u32[]{:S(2)}, u32[]{:S(2)}) collective-permute-start(bf16[768,128]{1,0:T(8,128)(2,1)S(1)} %get-tuple-element.76), channel_id=1, source_target_pairs={{0,8},{8,0},{16,24},{24,16},{1,9},{9,1},{17,25},{25,17},{2,10},{10... | collective-permute-start | bytes 589832 | tf_op jit(solution)/shard_map/ppermute | solution.py:54
  34.5 11.2 %collective-permute-start.17 = (bf16[768,128]{1,0:T(8,128)(2,1)S(1)}, bf16[768,128]{1,0:T(8,128)(2,1)S(1)}, u32[]{:S(2)}, u32[]{:S(2)}) collective-permute-start(bf16[768,128]{1,0:T(8,128)(2,1)S(1)} %get-tuple-element.77), channel_id=1, source_target_pairs={{0,16},{8,24},{16,0},{24,8},{1,17},{9,25},{17,1},{25,9},{2,18},{10... | collective-permute-start | bytes 589832 | tf_op jit(solution)/shard_map/ppermute | solution.py:54
  35.7 10.1 %collective-permute-start.18 = (bf16[768,128]{1,0:T(8,128)(2,1)S(1)}, bf16[768,128]{1,0:T(8,128)(2,1)S(1)}, u32[]{:S(2)}, u32[]{:S(2)}) collective-permute-start(bf16[768,128]{1,0:T(8,128)(2,1)S(1)} %get-tuple-element.78), channel_id=1, source_target_pairs={{0,24},{8,16},{16,8},{24,0},{1,25},{9,17},{17,9},{25,1},{2,26},{10... | collective-permute-start | bytes 589832 | tf_op jit(solution)/shard_map/ppermute | solution.py:54
  36.9 1.3 %collective-permute-start.14 = (bf16[1,272,128]{2,1,0:T(8,128)(2,1)S(1)}, bf16[1,272,128]{2,1,0:T(8,128)(2,1)S(1)}, u32[]{:S(2)}, u32[]{:S(2)}) collective-permute-start(bf16[1,272,128]{2,1,0:T(8,128)(2,1)S(1)} %bitcast.10), channel_id=1, source_target_pairs={{0,1},{1,0},{2,3},{3,2},{4,5},{5,4},{6,7},{7,6},{8,9},{9,8},{10,11... | collective-permute-start | bytes 208904 | tf_op jit(solution)/shard_map/ppermute | solution.py:54
  36.9 1.4 %collective-permute-start.15 = (bf16[1,272,128]{2,1,0:T(8,128)(2,1)S(1)}, bf16[1,272,128]{2,1,0:T(8,128)(2,1)S(1)}, u32[]{:S(2)}, u32[]{:S(2)}) collective-permute-start(bf16[1,272,128]{2,1,0:T(8,128)(2,1)S(1)} %bitcast.12), channel_id=1, source_target_pairs={{0,1},{1,0},{2,3},{3,2},{4,5},{5,4},{6,7},{7,6},{8,9},{9,8},{10,11... | collective-permute-start | bytes 208904 | tf_op jit(solution)/shard_map/ppermute | solution.py:54
  45.8 1.9 %collective-permute-start.19 = (bf16[512,512]{1,0:T(8,128)(2,1)S(1)}, bf16[512,512]{1,0:T(8,128)(2,1)S(1)}, u32[]{:S(2)}, u32[]{:S(2)}) collective-permute-start(bf16[512,512]{1,0:T(8,128)(2,1)S(1)} %shard_map.126.mine_ref), channel_id=1, source_target_pairs={{0,1},{1,0},{2,3},{3,2},{4,5},{5,4},{6,7},{7,6},{8,9},{9,8},{10,11... | collective-permute-start | bytes 1572872 | tf_op jit(solution)/shard_map/ppermute | solution.py:54
  46.0 9.5 %copy-start.1 = (f32[2,512,512]{2,1,0:T(8,128)S(1)}, f32[2,512,512]{2,1,0:T(8,128)}, u32[]{:S(2)}) copy-start(f32[2,512,512]{2,1,0:T(8,128)} %right_ref.1) | copy-start | bytes 6291460
  46.7 2.0 %collective-permute-start.20 = (bf16[4,2,256,128]{3,2,1,0:T(8,128)(2,1)S(1)}, bf16[4,2,256,128]{3,2,1,0:T(8,128)(2,1)S(1)}, u32[]{:S(2)}, u32[]{:S(2)}) collective-permute-start(bf16[4,2,256,128]{3,2,1,0:T(8,128)(2,1)S(1)} %get-tuple-element.85), channel_id=1, source_target_pairs={{0,1},{1,0},{2,3},{3,2},{4,5},{5,4},{6,7},{7,6},{8,9},{9,8},{10,11... | collective-permute-start | bytes 1572872 | tf_op jit(solution)/shard_map/ppermute | solution.py:54
  48.8 9.6 %collective-permute-start.21 = (bf16[64,512]{1,0:T(8,128)(2,1)S(1)}, bf16[64,512]{1,0:T(8,128)(2,1)S(1)}, u32[]{:S(2)}, u32[]{:S(2)}) collective-permute-start(bf16[64,512]{1,0:T(8,128)(2,1)S(1)} %get-tuple-element.87), channel_id=1, source_target_pairs={{0,2},{1,3},{2,0},{3,1},{4,6},{5,7},{6,4},{7,5},{8,10},{9,11},{10,... | collective-permute-start | bytes 196616 | tf_op jit(solution)/shard_map/ppermute | solution.py:54
  49.5 8.9 %collective-permute-start.22 = (bf16[64,512]{1,0:T(8,128)(2,1)S(1)}, bf16[64,512]{1,0:T(8,128)(2,1)S(1)}, u32[]{:S(2)}, u32[]{:S(2)}) collective-permute-start(bf16[64,512]{1,0:T(8,128)(2,1)S(1)} %get-tuple-element.88), channel_id=1, source_target_pairs={{0,4},{1,5},{2,6},{3,7},{4,0},{5,1},{6,2},{7,3},{8,12},{9,13},{10,... | collective-permute-start | bytes 196616 | tf_op jit(solution)/shard_map/ppermute | solution.py:54
  52.9 6.1 %collective-permute-start.23 = (bf16[64,512]{1,0:T(8,128)(2,1)S(1)}, bf16[64,512]{1,0:T(8,128)(2,1)S(1)}, u32[]{:S(2)}, u32[]{:S(2)}) collective-permute-start(bf16[64,512]{1,0:T(8,128)(2,1)S(1)} %get-tuple-element.89), channel_id=1, source_target_pairs={{0,6},{1,7},{2,4},{3,5},{4,2},{5,3},{6,0},{7,1},{8,14},{9,15},{10,... | collective-permute-start | bytes 196616 | tf_op jit(solution)/shard_map/ppermute | solution.py:54
  53.2 9.9 %collective-permute-start.27 = (bf16[768,128]{1,0:T(8,128)(2,1)S(1)}, bf16[768,128]{1,0:T(8,128)(2,1)S(1)}, u32[]{:S(2)}, u32[]{:S(2)}) collective-permute-start(bf16[768,128]{1,0:T(8,128)(2,1)S(1)} %shard_map.133), channel_id=1, source_target_pairs={{0,16},{8,24},{16,0},{24,8},{1,17},{9,25},{17,1},{25,9},{2,18},{10... | collective-permute-start | bytes 589832 | tf_op jit(solution)/shard_map/ppermute | solution.py:54
  54.8 8.4 %collective-permute-start.28 = (bf16[768,128]{1,0:T(8,128)(2,1)S(1)}, bf16[768,128]{1,0:T(8,128)(2,1)S(1)}, u32[]{:S(2)}, u32[]{:S(2)}) collective-permute-start(bf16[768,128]{1,0:T(8,128)(2,1)S(1)} %shard_map.134), channel_id=1, source_target_pairs={{0,8},{8,0},{16,24},{24,16},{1,9},{9,1},{17,25},{25,17},{2,10},{10... | collective-permute-start | bytes 589832 | tf_op jit(solution)/shard_map/ppermute | solution.py:54
  55.6 7.6 %copy-start.3 = (f32[2,8,8192]{2,1,0:T(8,128)S(1)}, f32[2,8,8192]{2,1,0:T(8,128)}, u32[]{:S(2)}) copy-start(f32[2,8,8192]{2,1,0:T(8,128)} %vocab_ref.1) | copy-start | bytes 1572868
  59.6 5.9 %collective-permute-start.24 = (bf16[2,64,512]{2,1,0:T(8,128)(2,1)S(1)}, bf16[2,64,512]{2,1,0:T(8,128)(2,1)S(1)}, u32[]{:S(2)}, u32[]{:S(2)}) collective-permute-start(bf16[2,64,512]{2,1,0:T(8,128)(2,1)S(1)} %shard_map.132.after_ref.refs_0_), channel_id=1, source_target_pairs={{0,8},{8,0},{16,24},{24,16},{1,9},{9,1},{17,25},{25,17},{2,10},{10... | collective-permute-start | bytes 393224 | tf_op jit(solution)/shard_map/ppermute | solution.py:54
  60.5 6.0 %collective-permute-start.25 = (bf16[2,64,512]{2,1,0:T(8,128)(2,1)S(1)}, bf16[2,64,512]{2,1,0:T(8,128)(2,1)S(1)}, u32[]{:S(2)}, u32[]{:S(2)}) collective-permute-start(bf16[2,64,512]{2,1,0:T(8,128)(2,1)S(1)} %shard_map.132.after_ref.refs_0_), channel_id=1, source_target_pairs={{0,16},{8,24},{16,0},{24,8},{1,17},{9,25},{17,1},{25,9},{2,18},{10... | collective-permute-start | bytes 393224 | tf_op jit(solution)/shard_map/ppermute | solution.py:54
  62.0 5.9 %collective-permute-start.26 = (bf16[2,64,512]{2,1,0:T(8,128)(2,1)S(1)}, bf16[2,64,512]{2,1,0:T(8,128)(2,1)S(1)}, u32[]{:S(2)}, u32[]{:S(2)}) collective-permute-start(bf16[2,64,512]{2,1,0:T(8,128)(2,1)S(1)} %shard_map.132.after_ref.refs_0_), channel_id=1, source_target_pairs={{0,24},{8,16},{16,8},{24,0},{1,25},{9,17},{17,9},{25,1},{2,26},{10... | collective-permute-start | bytes 393224 | tf_op jit(solution)/shard_map/ppermute | solution.py:54
  (1 other events, 7.6 us)
